TPU v7x, 128 devices: a whole 4x4x4 slice. The times are simulated.
128 devices in a mesh: prow: 8 (over x, core), pcol: 16 (over z, y).
Axes of the slice: x: 4, y: 4, z: 4, core: 2. Of those that a mesh axis runs over, the one named last changes fastest.
Arguments:
- l_panel: float32 [256, 256], replicated, may hold values from -0.5 to 3, as said below
- l_rows: float32 [8, 256, 12, 256], P('prow', 'pcol'), may hold values from -0.0390625 to 0.0390625
- lbar_panel: float32 [256, 256], replicated, may hold values from -6 to 6
- lbar_rows: float32 [8, 256, 12, 256], P('prow', 'pcol'), may hold values from -6 to 6
- sbar: float32 [8, 256, 12, 16, 6, 256], P('prow', None, None, 'pcol'), may hold values from -90 to 90, as said below
Outputs:
- abar_rows: float32 [8, 256, 12, 256], P('prow', 'pcol')
- abar_panel: float32 [256, 256], replicated
Inputs may be any that keep to these rules, and one draw needn't show every extreme that they name: `l_panel`: lower triangular; diagonal entries between 2 and 3. `sbar`: S read from it is symmetric.
All inputs are finite; a program needn't handle non-finite values.
Results may differ from a plain program's by a relative error of at most 0.000068.
Values sent between devices are 32-bit elements; how exact they have to be, the bound alone decides.
No kernel may reach another device: no remote copies, remote signals or barrier semaphores. Data moves between devices by JAX's collectives and lax.ppermute only.
A program may use at most 192 MiB of HBM per device.

v0:
```python
import jax
import jax.numpy as jnp
from jax import lax
from jax.sharding import PartitionSpec as P


def spread(value, axis, source):
    kept = jnp.where(lax.axis_index(axis) == source, value, 0).astype(value.dtype)
    return lax.psum(kept, axis)


def hdot(left, right):
    return jnp.dot(left, right, precision=lax.Precision.HIGHEST, preferred_element_type=jnp.float32)


def tdot(left, right):
    return lax.dot_general(
        left,
        right,
        (((0,), (0,)), ((), ())),
        precision=lax.Precision.HIGHEST,
        preferred_element_type=jnp.float32,
    )


def shards(l_panel, l_rows, lbar_panel, lbar_rows, sbar):
    grid_rows = lax.axis_size("prow")
    grid_cols = lax.axis_size("pcol")
    tile = l_panel.shape[0]
    width = l_rows.shape[3]
    row_tiles = l_rows.shape[2]
    ratio = grid_cols // grid_rows
    col_tiles = row_tiles // ratio
    full = lax.all_gather(l_rows, "pcol", axis=1, tiled=True)
    block = sbar.reshape(tile * row_tiles, col_tiles * tile)
    mine = l_rows[0].reshape(-1, width)
    own = lbar_rows[0].reshape(-1, width)
    identity = jnp.eye(width, dtype=l_panel.dtype)
    inverse = lax.linalg.triangular_solve(l_panel, identity, left_side=True, lower=True)
    col_index = lax.axis_index("pcol")
    root = col_index % grid_rows
    which = col_index // grid_rows
    grouped = full[0].reshape(tile, col_tiles, ratio, width)
    picked = lax.dynamic_index_in_dim(grouped, which, 2, keepdims=False)
    picked = jnp.transpose(picked, (1, 0, 2)).reshape(col_tiles * tile, width)
    col_panel = spread(picked, "prow", root)
    product = lax.psum_scatter(hdot(block, col_panel), "pcol", scatter_dimension=0, tiled=True)
    adjusted = own - 2.0 * product
    abar_local = hdot(adjusted, inverse)
    gram = lax.psum(tdot(abar_local, mine), ("prow", "pcol"))
    lbar_new = lbar_panel - jnp.tril(gram)
    inner = tdot(l_panel, lbar_new)
    phi = jnp.tril(inner) - 0.5 * jnp.diag(jnp.diag(inner))
    qmat = hdot(tdot(inverse, phi), inverse)
    abar_panel = 0.5 * (qmat + qmat.T)
    abar_rows = abar_local.reshape(l_rows.shape)
    return (abar_rows, abar_panel)


def solution(mesh):
    return jax.shard_map(
        shards,
        mesh=mesh,
        in_specs=(
            P(),
            P("prow", "pcol", None, None),
            P(),
            P("prow", "pcol", None, None),
            P("prow", None, None, "pcol", None, None),
        ),
        out_specs=(P("prow", "pcol", None, None), P()),
        check_vma=False,
    )
```

profile of v0, /device:TPU:1, one launch (start us, length us, event | category | flops | bytes accessed | tf_op | source)
XLA Modules:
  0.0 446.0 jit_solution(2442303199665808642)
XLA Ops:
  7.2 0.7 all-gather.2.cloned.1.call-update
  8.0 53.2 %all-gather.2.cloned.1.call-done = f32[1,256,12,256]{3,1,2,0:T(8,128)} async-done(((f32[1,16,12,256]{3,1,2,0:T(8,128)}), f32[1,256,12,256]{3,1,2,0:T(8,128)}) %all-gather.2.cloned.1.call-update) | async-done | bytes 3145744 | tf_op jit(solution)/shard_map/all_gather | solution.py:34
  61.2 2.7 dynamic-slice_select_fusion
  64.0 108.6 %reduce = f32[256,12,6,256]{3,2,1,0:T(8,128)} reduce(f32[1,256,12,1,6,256]{5,3,4,2,1,0:T(1,128)} %param.9, f32[]{:T(128)} %constant.96), dimensions={0,3}, to_apply=%param.9.reduce_sub_computation | reduce | bytes 37748740 | tf_op args[4]
  172.6 20.5 %copy.22 = f32[384,8,6,256]{3,1,2,0:T(8,128)} copy(f32[384,8,6,256]{3,2,1,0:T(8,128)} %bitcast.43) | data formatting | bytes 37748736
  193.1 19.4 %convolution_bitcast_fusion = f32[3072,256]{1,0:T(8,128)} fusion(f32[1536,256]{1,0:T(8,128)} %all-reduce.3.cloned.1.call-done, f32[3072,1536]{1,0:T(8,128)} %bitcast.42), kind=kOutput, calls=%fused_computation.3 | convolution fusion | flops 14495514624 | bytes 23592960 | tf_op jit(solution)/shard_map/dot_general | solution.py:13
  212.8 0.7 copy-done.1
  213.9 4.2 while.1
  213.9 0.6 fusion.40
  214.5 1.4 dynamic-slice.7
  216.0 0.6 fusion.40
  216.6 1.4 dynamic-slice.7
  218.1 19.7 %custom-call.3 = f32[2,128,128]{1,2,0:T(8,128)S(1)} custom-call(f32[2,128,128]{2,1,0:T(8,128)S(1)} %get-tuple-element.9), custom_call_target="InvertDiagBlocksLowerTriangular" | custom-call | tf_op jit(solution)/shard_map/triangular_solve | solution.py:39
  238.3 0.4 convolution_subtract_fusion
  239.0 47.2 %reduce-scatter.2.cloned.1.call-done = f32[192,256]{1,0:T(8,128)} async-done(((f32[3072,256]{1,0:T(8,128)}), f32[192,256]{1,0:T(8,128)}) %reduce-scatter.2.cloned.1.call-update) | async-done | bytes 196624 | tf_op jit(solution)/shard_map/reduce_scatter | solution.py:47
  286.2 1.3 fusion.9
  287.4 1.4 fusion.30
  289.0 0.8 copy.19
  289.8 143.9 %all-reduce.5.cloned.1.call-done = f32[256,256]{0,1:T(8,128)} async-done(((f32[256,256]{0,1:T(8,128)}), f32[256,256]{0,1:T(8,128)}) %all-reduce.5.cloned.1.call-update) | async-done | bytes 262160 | tf_op jit(solution)/shard_map/psum | solution.py:50
  433.7 1.3 convolution_bitcast_fusion.1
  435.1 2.4 gather_fusion
  437.4 0.6 fusion.1
  438.0 0.4 fusion.12
  438.6 0.8 copy.20
  (38 shorter events, 2.1 us)
Async XLA Ops:
  7.2 54.1 %all-gather.2.cloned.1.call-start = ((), (), s32[]{:S(2)}) async-start(), calls=%async_computation.1 | async-start | bytes 3342336 | tf_op jit(solution)/shard_map/all_gather | solution.py:34
  7.9 185.2 %all-reduce.3.cloned.1.call-start = ((), (), s32[]{:S(2)}) async-start(), calls=%async_computation.2 | async-start | bytes 3145728 | tf_op jit(solution)/shard_map/psum | solution.py:9
  64.0 222.2 %reduce-scatter.2.cloned.1.call-start = ((), (), s32[]{:S(2)}) async-start(), calls=%async_computation.3 | async-start | bytes 3342336 | tf_op jit(solution)/shard_map/reduce_scatter | solution.py:47
  212.5 0.9 copy-start.1
  212.6 1.1 copy-start
  212.6 25.2 %copy-start.3 = (f32[1,16,12,256]{3,1,2,0:T(8,128)S(1)}, f32[1,16,12,256]{3,1,2,0:T(8,128)}, u32[]{:S(2)}) copy-start(f32[1,16,12,256]{3,1,2,0:T(8,128)} %param.8) | copy-start | bytes 589828
  212.6 221.1 %all-reduce.5.cloned.1.call-start = ((), (), s32[]{:S(2)}) async-start(), calls=%async_computation.4 | async-start | bytes 524288 | tf_op jit(solution)/shard_map/psum | solution.py:50
  213.8 75.0 %copy-start.2 = (f32[256,256]{1,0:T(8,128)S(1)}, f32[256,256]{1,0:T(8,128)}, u32[]{:S(2)}) copy-start(f32[256,256]{1,0:T(8,128)} %param.7) | copy-start | bytes 786436
Sparse Core Ops, SparseCore 0:
  10.1 51.0 all-gather.1
  64.1 61.0 all-reduce.2
  212.7 73.4 reduce-scatter.1
  291.3 142.3 all-reduce.4
where the time goes:
time: 446 us
  waiting for transfers between devices  245 us (55%)
  other arithmetic  131 us (29%)
  local copies, waits for them, and re-layouts  30.1 us (7%)
  matrix products  25.3 us (6%)
  between operations  14 us (3%)
    psum x1, waiting for transfers between devices, shards(): gram = lax.psum(tdot(abar_local, mine), ('prow', 'pcol'))  144 us
    unnamed x2, other arithmetic  109 us
    all_gather x1, waiting for transfers between devices, shards(): full = lax.all_gather(l_rows, 'pcol', axis=1, tiled=True)  53.2 us
    reduce_scatter x1, waiting for transfers between devices, shards(): lax.psum_scatter(hdot(block, col_panel), 'pcol', scatter_dimension=0, til...  47.2 us
    unnamed x15, local copies, waits for them, and re-layouts  23.3 us
    dot_general x3, matrix products, hdot(): jnp.dot(left, right, precision=lax.Precision.HIGHEST, preferred_element_t...  21.1 us
    another operation x3, other arithmetic, shards(): lax.linalg.triangular_solve(l_panel, identity, left_side=True, lower=True)  19.7 us
  transfers between devices with their start and end apart: 4, of which 3 were waited for; matrix products, arithmetic and copies ran while one was open for 35% of the time, Pallas kernels for 0%

commit v1 on v0

v1 whole, which is shorter than its diff:
```python
import functools

import jax
import jax.numpy as jnp
from jax import lax
from jax.experimental import pallas as pl
from jax.experimental.pallas import tpu as pltpu
from jax.sharding import PartitionSpec as P

F32 = jnp.float32
BF16 = jnp.bfloat16
AXES = ("prow", "pcol")
NB = 256
UR = 12
TPC = 6
PIECE = 16 * UR
GROUP = 4 * PIECE
SLAB = PIECE * TPC * 2
COLS = TPC * NB
VMEM = pl.BlockSpec(memory_space=pltpu.VMEM)
ANY = pl.BlockSpec(memory_space=pl.ANY)


def pairs(target):
    found = []
    for x in range(4):
        for c in range(2):
            for z in range(4):
                for y in range(4):
                    tx, tc, tz, ty = target(x, c, z, y)
                    found.append(
                        ((2 * x + c) * 16 + 4 * z + y, (2 * (tx % 4) + tc) * 16 + 4 * (tz % 4) + ty % 4)
                    )
    return found


def permute(value, target):
    return lax.ppermute(value, AXES, pairs(target))


def first_axis(step):
    return lambda x, c, z, y: (x, c, z, y + step) if c == 0 else (x, c, z + step, y)


def second_axis(step):
    return lambda x, c, z, y: (x, c, z + step, y) if c == 0 else (x, c, z, y + step)


def other_core(x, c, z, y):
    return x, 1 - c, z, y


def halving(stage):
    def target(x, c, z, y):
        return (x ^ 1 if (stage + c) % 2 == 0 else x ^ 3), c, z, y

    return target


def crossing(stage, mask):
    def target(x, c, z, y):
        axis = (stage + c) % 3
        if axis == 0:
            return x ^ mask, c, z, y
        if axis == 1:
            return x, c, z, y ^ mask
        return x, c, z ^ mask, y

    return target


def to_tiles(k):
    def target(x, c, z, y):
        p, q = 2 * x + c, 4 * z + y
        parity = k ^ (q % 2)
        tp, tq = q // 2, p + 8 * parity
        return tp // 2, tp % 2, tq // 4, tq % 4

    return target


def to_rows(k):
    def target(x, c, z, y):
        p, q = 2 * x + c, 4 * z + y
        half = k ^ (q // 8)
        tp, tq = q % 8, 2 * p + half
        return tp // 2, tp % 2, tq // 4, tq % 4

    return target


def place():
    p, q = lax.axis_index("prow"), lax.axis_index("pcol")
    return p // 2, p % 2, q // 4, q % 4


def split(value):
    high = value.astype(BF16)
    return high, (value - high.astype(F32)).astype(BF16)


def dot3(lh, ll, rh, rl):
    total = jnp.dot(lh, rh, preferred_element_type=F32)
    total += jnp.dot(ll, rh, preferred_element_type=F32)
    total += jnp.dot(lh, rl, preferred_element_type=F32)
    return total


def dot6(left, right):
    return jnp.dot(left, right, precision=lax.Precision.HIGHEST, preferred_element_type=F32)


def tdot6(left, right):
    return lax.dot_general(
        left, right, (((0,), (0,)), ((), ())), precision=lax.Precision.HIGHEST, preferred_element_type=F32
    )


def prep_kernel(step, s_ref, high_ref, low_ref, buffer, sem):
    _, c, z, y = place()
    copies = []
    for i, offset in enumerate((0, 3, 1, 2)):
        zz = jnp.where(c == 0, z + step, z + offset) % 4
        yy = jnp.where(c == 0, y + offset, y + step) % 4
        base = (zz * 4 + yy) * SLAB
        for j in range(2):
            half = SLAB // 2
            copy = pltpu.make_async_copy(
                s_ref.at[pl.ds(base + j * half, half), :],
                buffer.at[pl.ds(i * SLAB + j * half, half), :],
                sem.at[2 * i + j],
            )
            copy.start()
            copies.append(copy)
    rows = PIECE // 2
    for i, copy in enumerate(copies):
        copy.wait()
        for k in range(2 * TPC):
            high, low = split(buffer[pl.ds(i * (SLAB // 2) + k, rows, stride=2 * TPC), :])
            high_ref[i * rows : (i + 1) * rows, k * 128 : (k + 1) * 128] = high
            low_ref[i * rows : (i + 1) * rows, k * 128 : (k + 1) * 128] = low


def prepare(step, s_lines):
    return pl.pallas_call(
        functools.partial(prep_kernel, step),
        in_specs=[ANY],
        out_specs=[VMEM, VMEM],
        out_shape=[jax.ShapeDtypeStruct((GROUP, COLS), BF16)] * 2,
        scratch_shapes=[pltpu.VMEM((4 * SLAB, 128), F32), pltpu.SemaphoreType.DMA((8,))],
        compiler_params=pltpu.CompilerParams(vmem_limit_bytes=40 << 20),
        cost_estimate=pl.CostEstimate(flops=0, bytes_accessed=10_000_000, transcendentals=0),
        name="prepare",
    )(s_lines)


def multiply_kernel(count, *refs):
    groups, out_ref = refs[:-1], refs[-1]
    total = None
    for i in range(count):
        l_ref, high_ref, low_ref = groups[3 * i : 3 * i + 3]
        lh, ll = split(l_ref[...].T)
        part = dot3(lh, ll, high_ref[...], low_ref[...])
        total = part if total is None else total + part
    if len(groups) > 3 * count:
        total += groups[-1][...]
    out_ref[...] = total


def multiply(*operands):
    count = len(operands) // 3
    return pl.pallas_call(
        functools.partial(multiply_kernel, count),
        in_specs=[VMEM] * len(operands),
        out_specs=VMEM,
        out_shape=jax.ShapeDtypeStruct((NB, COLS), F32),
        compiler_params=pltpu.CompilerParams(vmem_limit_bytes=48 << 20),
        cost_estimate=pl.CostEstimate(
            flops=count * 6 * GROUP * COLS * NB, bytes_accessed=count * 6_000_000, transcendentals=0
        ),
        name="multiply",
    )(*operands)


def finish_kernel(la_ref, lb_ref, high_ref, low_ref, acc_ref, cols_ref, keep_ref, send_ref, cross_ref):
    x, c, _, _ = place()
    lh, ll = split(jnp.concatenate([la_ref[...], lb_ref[...]], axis=0).T)
    cross = None
    for half in range(3):
        at = slice(half * 512, (half + 1) * 512)
        part = acc_ref[:, at] + dot3(lh, ll, high_ref[:, at], low_ref[:, at])
        turned = part.T
        for j in range(2):
            v = 2 * half + j
            block = turned[j * NB : (j + 1) * NB].reshape(8, 32, NB)
            rows = cols_ref[:, v].reshape(NB, NB)
            for xx in range(4):
                for core in range(2):
                    piece = block[2 * xx + core]
                    away = xx ^ x
                    if core == 0:
                        order = jnp.where(away == 0, 0, jnp.where(away == 3, 1, jnp.where(away == 1, 2, 3)))
                    else:
                        order = jnp.where(away == 0, 0, jnp.where(away == 1, 1, jnp.where(away == 3, 2, 3)))

                    @pl.when(c == core)
                    def _():
                        keep_ref[order, v] = piece

                    @pl.when(c != core)
                    def _():
                        send_ref[order, v] = piece

            ph, pl_ = split(part[:, j * NB : (j + 1) * NB])
            rh, rl = split(rows)
            term = dot3(ph, pl_, rh, rl)
            cross = term if cross is None else cross + term
    cross_ref[...] = cross


def finish(la, lb, high, low, acc, cols):
    share = jax.ShapeDtypeStruct((4, TPC, 32, NB), F32)
    return pl.pallas_call(
        finish_kernel,
        in_specs=[VMEM] * 6,
        out_specs=[VMEM] * 3,
        out_shape=[share, share, jax.ShapeDtypeStruct((NB, NB), F32)],
        compiler_params=pltpu.CompilerParams(vmem_limit_bytes=48 << 20),
        cost_estimate=pl.CostEstimate(
            flops=7 * GROUP * COLS * NB, bytes_accessed=12_000_000, transcendentals=0
        ),
        name="finish",
    )(la, lb, high, low, acc, cols)


def invert_kernel(l_ref, out_ref):
    n = NB
    row = lax.broadcasted_iota(jnp.int32, (n, n), 0)
    col = lax.broadcasted_iota(jnp.int32, (n, n), 1)
    lower = l_ref[...]
    diagonal = jnp.where(row == col, lower, 0.0)
    by_row = 1.0 / jnp.sum(diagonal, axis=1, keepdims=True)
    by_col = 1.0 / jnp.sum(diagonal, axis=0, keepdims=True)
    strict = jnp.where(row > col, lower * by_row, 0.0)
    power = jnp.where(row // 16 == col // 16, -strict, 0.0)
    inverse = jnp.where(row == col, 1.0, 0.0) + power
    for _ in range(3):
        power = dot6(power, power)
        inverse = inverse + dot6(power, inverse)
    size = 16
    while size < n:
        beside = (row // (2 * size) == col // (2 * size)) & (row // size != col // size)
        inverse = inverse - dot6(inverse, dot6(jnp.where(beside, strict, 0.0), inverse))
        size *= 2
    out_ref[...] = inverse * by_col


def invert(l_panel):
    return pl.pallas_call(
        invert_kernel,
        in_specs=[VMEM],
        out_specs=VMEM,
        out_shape=jax.ShapeDtypeStruct((NB, NB), F32),
        compiler_params=pltpu.CompilerParams(vmem_limit_bytes=24 << 20),
        cost_estimate=pl.CostEstimate(flops=14 * 12 * NB**3, bytes_accessed=20_000_000, transcendentals=0),
        name="invert",
    )(l_panel)


def panel_kernel(share, cross_ref, own_ref, mine_ref, l_ref, inv_ref, lbar_ref, keep_ref, send_ref):
    _, c, _, _ = place()
    row = lax.broadcasted_iota(jnp.int32, (NB, NB), 0)
    col = lax.broadcasted_iota(jnp.int32, (NB, NB), 1)
    inverse = inv_ref[...]
    lower = l_ref[...]
    inner = tdot6(own_ref[...], mine_ref[...]) - 2.0 * cross_ref[...]
    gram = tdot6(inverse, inner)
    fresh = lbar_ref[...] * share - jnp.where(row >= col, gram, 0.0)
    phi = tdot6(lower, fresh)
    phi = jnp.where(row > col, phi, jnp.where(row == col, 0.5 * phi, 0.0))
    full = dot6(tdot6(inverse, phi), inverse)
    result = 0.5 * (full + full.T)
    first, second = result[: NB // 2], result[NB // 2 :]
    keep_ref[...] = jnp.where(c == 0, first, second)
    send_ref[...] = jnp.where(c == 0, second, first)


def panel(cross, own, mine, l_panel, inverse, lbar_panel, share):
    half = jax.ShapeDtypeStruct((NB // 2, NB), F32)
    return pl.pallas_call(
        functools.partial(panel_kernel, share),
        in_specs=[VMEM] * 6,
        out_specs=[VMEM] * 2,
        out_shape=[half, half],
        compiler_params=pltpu.CompilerParams(vmem_limit_bytes=24 << 20),
        cost_estimate=pl.CostEstimate(flops=5 * 12 * NB**3, bytes_accessed=8_000_000, transcendentals=0),
        name="panel",
    )(cross, own, mine, l_panel, inverse, lbar_panel)


def rows_kernel(own_ref, first_ref, second_ref, inv_ref, out_ref):
    _, _, _, y = place()
    swap = y % 2 == 1
    first, second = first_ref[...], second_ref[...]
    even = jnp.where(swap, second, first)
    odd = jnp.where(swap, first, second)
    adjusted = own_ref[...] - 2.0 * jnp.stack([even, odd], axis=1)
    result = dot6(adjusted.reshape(PIECE, NB), inv_ref[...])
    out_ref[...] = result.reshape(TPC, 2, 16, NB)


def finish_rows(own, first, second, inverse):
    return pl.pallas_call(
        rows_kernel,
        in_specs=[VMEM] * 4,
        out_specs=VMEM,
        out_shape=jax.ShapeDtypeStruct((TPC, 2, 16, NB), F32),
        compiler_params=pltpu.CompilerParams(vmem_limit_bytes=24 << 20),
        cost_estimate=pl.CostEstimate(flops=12 * PIECE * NB * NB, bytes_accessed=1_000_000, transcendentals=0),
        name="finish_rows",
    )(own, first, second, inverse)


def shards(l_panel, l_rows, lbar_panel, lbar_rows, sbar):
    p, q = lax.axis_index("prow"), lax.axis_index("pcol")
    s_lines = sbar.reshape(16 * SLAB, 128)
    by_tile = jnp.transpose(l_rows[0], (1, 0, 2))
    own = jnp.transpose(lbar_rows[0], (1, 0, 2))
    piece = l_rows[0].reshape(PIECE, NB)

    tiles = by_tile.reshape(TPC, 2, 16, NB)
    odd_col = q % 2 == 1
    even_u, odd_u = tiles[:, 0], tiles[:, 1]
    t0 = permute(jnp.where(odd_col, odd_u, even_u), to_tiles(0))
    t1 = permute(jnp.where(odd_col, even_u, odd_u), to_tiles(1))
    late = q >= 8
    col_piece = jnp.concatenate([jnp.where(late, t1, t0), jnp.where(late, t0, t1)], axis=1)
    cols = lax.all_gather(col_piece, "prow", axis=0, tiled=False)

    up = permute(piece, first_axis(1))
    down = permute(piece, first_axis(-1))
    far_up = permute(up[: PIECE // 2], first_axis(1))
    far_down = permute(down[PIECE // 2 :], first_axis(-1))
    group = jnp.concatenate([piece, up, down, far_up, far_down], axis=0)
    group_up = permute(group, second_axis(1))
    group_down = permute(group, second_axis(-1))
    group_far_up = permute(group_up[: GROUP // 2], second_axis(1))
    group_far_down = permute(group_down[GROUP // 2 :], second_axis(-1))

    parts = [prepare(step, s_lines) for step in (0, 3, 1, 2)]
    inverse = invert(l_panel)
    total = multiply(group, *parts[0])
    total = multiply(group_up, *parts[1], group_down, *parts[2], total)
    keep, send, cross = finish(group_far_up, group_far_down, *parts[3], total, cols)

    keep = keep + permute(send, other_core)
    keep = keep[:2] + permute(keep[2:], halving(0))
    product = keep[0] + permute(keep[1], halving(1))
    product = product.reshape(TPC, 2, 16, NB)
    r0 = permute(jnp.where(late, product[:, 1], product[:, 0]), to_rows(0))
    r1 = permute(jnp.where(late, product[:, 0], product[:, 1]), to_rows(1))
    abar = finish_rows(own.reshape(TPC, 2, 16, NB), r0, r1, inverse)
    abar_rows = jnp.transpose(abar.reshape(UR, 16, NB), (1, 0, 2))[None]

    share = 1.0 / (lax.axis_size("prow") * lax.axis_size("pcol"))
    mine = by_tile.reshape(PIECE, NB)
    part, other = panel(cross, own.reshape(PIECE, NB), mine, l_panel, inverse, lbar_panel, share)
    part = part + permute(other, other_core)
    for stage in range(3):
        near, opposite, beyond = (permute(part, crossing(stage, mask)) for mask in (1, 3, 2))
        part = (part + near) + (beyond + opposite)
    rest = permute(part, other_core)
    is_first = p % 2 == 0
    abar_panel = jnp.concatenate([jnp.where(is_first, part, rest), jnp.where(is_first, rest, part)], axis=0)
    return abar_rows, abar_panel


def solution(mesh):
    return jax.shard_map(
        shards,
        mesh=mesh,
        in_specs=(
            P(),
            P("prow", "pcol", None, None),
            P(),
            P("prow", "pcol", None, None),
            P("prow", None, None, "pcol", None, None),
        ),
        out_specs=(P("prow", "pcol", None, None), P()),
        check_vma=False,
    )
```

time: 446 us -> 162 us (0.36)
  waiting for transfers between devices: 245 us -> 39.6 us
  other arithmetic: 131 us -> 3.69 us
  starting transfers between devices: 0.34 us -> 49 us
  Pallas kernels: 0 us -> 39.7 us
  matrix products: 25.3 us -> 0 us
  local copies, waits for them, and re-layouts: 30.1 us -> 12.6 us
    psum x2 -> x0, waiting for transfers between devices: 144 us -> none  [the longest x1 144 us: shards(): gram = lax.psum(tdot(abar_local, mine), ('prow', 'pcol'))]
    unnamed x2 -> x0, other arithmetic: 109 us -> none
    all_gather x1, waiting for transfers between devices: 53.2 us -> 0.02 us  [shards(): cols = lax.all_gather(col_piece, 'prow', axis=0, tiled=False)]
    ppermute x0 -> x26, starting transfers between devices: none -> 48.9 us  [permute(): return lax.ppermute(value, AXES, pairs(target))]
    reduce_scatter x1 -> x0, waiting for transfers between devices: 47.2 us -> none  [shards(): lax.psum_scatter(hdot(block, col_panel), 'pcol', scatter_dimension=0, til...]
    pallas_call x0 -> x10, Pallas kernels: none -> 39.7 us  [the longest x2 11.3 us: multiply(): pl.pallas_call(functools.partial(multiply_kernel, count), in_specs=[VMEM]...]
    ppermute x0 -> x26, waiting for transfers between devices: none -> 39.6 us  [permute(): return lax.ppermute(value, AXES, pairs(target))]
    dot_general x6 -> x0, matrix products: 24.4 us -> none  [the longest x3 21.1 us: hdot(): jnp.dot(left, right, precision=lax.Precision.HIGHEST, preferred_element_t...]
  transfers between devices with their start and end apart: 4 -> 27, of which waited for: 3 -> 14; matrix products, arithmetic and copies ran while one was open for 35% -> 2% of each run, Pallas kernels for 0% -> 19%
where the time goes in v1:
time: 162 us; the launch traced here: 159 us
  starting transfers between devices  49 us (30%)
  Pallas kernels  39.7 us (25%)
  waiting for transfers between devices  39.6 us (24%)
  between operations  14.5 us (9%)
  local copies, waits for them, and re-layouts  12.6 us (8%)
  other arithmetic  3.69 us (2%)
    ppermute x26, starting transfers between devices, permute(): return lax.ppermute(value, AXES, pairs(target))  48.9 us
    ppermute x26, waiting for transfers between devices, permute(): return lax.ppermute(value, AXES, pairs(target))  39.6 us
    unnamed x29, local copies, waits for them, and re-layouts  12.4 us
    pallas_call x2, Pallas kernels, multiply(): pl.pallas_call(functools.partial(multiply_kernel, count), in_specs=[VMEM]...  11.3 us
    pallas_call x4, Pallas kernels, prepare(): pl.pallas_call(functools.partial(prep_kernel, step), in_specs=[ANY], out_...  10 us
    pallas_call x1, Pallas kernels, finish(): pl.pallas_call(finish_kernel, in_specs=[VMEM] * 6, out_specs=[VMEM] * 3,...  8.37 us
    pallas_call x1, Pallas kernels, invert(): pl.pallas_call(invert_kernel, in_specs=[VMEM], out_specs=VMEM, out_shape=...  6.45 us
  transfers between devices with their start and end apart: 27, of which 14 were waited for; matrix products, arithmetic and copies ran while one was open for 2% of the time, Pallas kernels for 19%

profile of v1, /device:TPU:1, one launch (start us, length us, event | category | flops | bytes accessed | tf_op | source)
XLA Modules:
  0.0 159.1 jit_solution(12103617329310278081)
XLA Ops:
  8.2 6.1 %collective-permute-start.8 = (f32[6,16,256]{2,1,0:T(8,128)S(1)}, f32[6,16,256]{2,1,0:T(8,128)S(1)}, u32[]{:S(2)}, u32[]{:S(2)}) collective-permute-start(f32[6,16,256]{2,1,0:T(8,128)S(1)} %fusion.1), channel_id=1, source_target_pairs={{0,8},{1,0},{2,24},{3,16},{4,40},{5,32},{6,56},{7,48},{8,72},{9,64... | collective-permute-start | bytes 294920 | tf_op jit(solution)/shard_map/ppermute | solution.py:38
  17.2 7.3 %collective-permute-done.9 = f32[6,16,256]{2,1,0:T(8,128)S(1)} collective-permute-done((f32[6,16,256]{2,1,0:T(8,128)S(1)}, f32[6,16,256]{2,1,0:T(8,128)S(1)}, u32[]{:S(2)}, u32[]{:S(2)}) %collective-permute-start.9) | collective-permute-done | bytes 98336 | tf_op jit(solution)/shard_map/ppermute | solution.py:38
  28.7 2.6 %collective-permute-start.1 = (f32[192,256]{1,0:T(8,128)S(1)}, f32[192,256]{1,0:T(8,128)S(1)}, u32[]{:S(2)}, u32[]{:S(2)}) collective-permute-start(f32[192,256]{1,0:T(8,128)S(1)} %reshape_squeeze.3), channel_id=1, source_target_pairs={{0,3},{1,0},{2,1},{3,2},{4,7},{5,4},{6,5},{7,6},{8,11},{9,8},{10,9... | collective-permute-start | bytes 589832 | tf_op jit(solution)/shard_map/ppermute | solution.py:38
  31.3 3.0 %collective-permute-done = f32[192,256]{1,0:T(8,128)S(1)} collective-permute-done((f32[192,256]{1,0:T(8,128)S(1)}, f32[192,256]{1,0:T(8,128)S(1)}, u32[]{:S(2)}, u32[]{:S(2)}) %collective-permute-start) | collective-permute-done | bytes 196640 | tf_op jit(solution)/shard_map/ppermute | solution.py:38
  34.6 2.6 %collective-permute-start.3 = (f32[96,256]{1,0:T(8,128)S(1)}, f32[96,256]{1,0:T(8,128)S(1)}, u32[]{:S(2)}, u32[]{:S(2)}) collective-permute-start(f32[96,256]{1,0:T(8,128)S(1)} %slice.51), channel_id=1, source_target_pairs={{0,3},{1,0},{2,1},{3,2},{4,7},{5,4},{6,5},{7,6},{8,11},{9,8},{10,9... | collective-permute-start | bytes 294920 | tf_op jit(solution)/shard_map/ppermute | solution.py:38
  39.2 2.7 %collective-permute-start.6 = (f32[768,256]{1,0:T(8,128)S(1)}, f32[768,256]{1,0:T(8,128)S(1)}, u32[]{:S(2)}, u32[]{:S(2)}) collective-permute-start(f32[768,256]{1,0:T(8,128)S(1)} %constant_dynamic-update-slice_fusion.refs_0_), channel_id=1, source_target_pairs={{0,12},{1,13},{2,14},{3,15},{4,0},{5,1},{6,2},{7,3},{8,4},{9,5},{1... | collective-permute-start | bytes 2359304 | tf_op jit(solution)/shard_map/ppermute | solution.py:38
  41.9 2.6 %prepare.7 = (bf16[768,1536]{1,0:T(8,128)(2,1)S(1)}, bf16[768,1536]{1,0:T(8,128)(2,1)S(1)}) custom-call(f32[36864,128]{1,0:T(8,128)} %bitcast.64), custom_call_target="tpu_custom_call" | custom-call | bytes 10000000 | tf_op jit(solution)/shard_map/prepare/pallas_call | solution.py:145
  45.8 2.5 %prepare.5 = (bf16[768,1536]{1,0:T(8,128)(2,1)S(1)}, bf16[768,1536]{1,0:T(8,128)(2,1)S(1)}) custom-call(f32[36864,128]{1,0:T(8,128)} %bitcast.65), custom_call_target="tpu_custom_call" | custom-call | bytes 10000000 | tf_op jit(solution)/shard_map/prepare/pallas_call | solution.py:145
  62.1 2.9 %collective-permute-start.7 = (f32[384,256]{1,0:T(8,128)S(1)}, f32[384,256]{1,0:T(8,128)S(1)}, u32[]{:S(2)}, u32[]{:S(2)}) collective-permute-start(f32[384,256]{1,0:T(8,128)S(1)} %slice.53), channel_id=1, source_target_pairs={{0,12},{1,13},{2,14},{3,15},{4,0},{5,1},{6,2},{7,3},{8,4},{9,5},{1... | collective-permute-start | bytes 1179656 | tf_op jit(solution)/shard_map/ppermute | solution.py:38
  65.0 3.7 %multiply.2.refs_6_ = f32[256,1536]{1,0:T(8,128)S(1)} custom-call(f32[768,256]{1,0:T(8,128)S(1)} %constant_dynamic-update-slice_fusion.refs_0_, bf16[768,1536]{1,0:T(8,128)(2,1)S(1)} %get-tuple-element.21.refs_1_, bf16[768,1536]{1,0:T(8,128)(2,1)} %copy-done.4), custom_call_target="tpu_custom_call" | custom-call | flops 1811939328 | bytes 6000000 | tf_op jit(solution)/shard_map/multiply/pallas_call | solution.py:172
  68.7 7.6 %multiply.3.acc_ref = f32[256,1536]{1,0:T(8,128)S(1)} custom-call(f32[768,256]{1,0:T(8,128)S(1)} %collective-permute-done.4.refs_0_, bf16[768,1536]{1,0:T(8,128)(2,1)} %copy-done, bf16[768,1536]{1,0:T(8,128)(2,1)} %copy-done.1, f32[768,256]{1,0:T(8,128)S(1)} %collective-permute-done.6.refs_3_, bf16[768,1536]{1,0:T(8,128)(2,1)} %copy-done.2, ...), custom_call_target="tpu_custom_call" | custom-call | flops 3623878656 | bytes 12000000 | tf_op jit(solution)/shard_map/multiply/pallas_call | solution.py:172
  77.8 8.4 %finish.1 = (f32[4,6,32,256]{3,2,1,0:T(8,128)S(1)}, f32[4,6,32,256]{3,2,1,0:T(8,128)S(1)}, f32[256,256]{1,0:T(8,128)S(1)}) custom-call(f32[384,256]{1,0:T(8,128)S(1)} %collective-permute-done.5.la_ref, f32[384,256]{1,0:T(8,128)S(1)} %collective-permute-done.7.lb_ref, bf16[768,1536]{1,0:T(8,128)(2,1)} %copy-done.5, bf16[768,1536]{1,0:T(8,128)(2,1)} %copy-done.6, ...), custom_call_target="tpu_custom_call" | custom-call | flops 2113929216 | bytes 12000000 | tf_op jit(solution)/shard_map/finish/pallas_call | solution.py:223
  88.4 6.5 %invert.1.inv_ref = f32[256,256]{1,0:T(8,128)S(1)} custom-call(f32[256,256]{1,0:T(8,128)S(1)} %copy-done.10), custom_call_target="tpu_custom_call" | custom-call | flops 2818572288 | bytes 20000000 | tf_op jit(solution)/shard_map/invert/pallas_call | solution.py:259
  94.9 2.5 %panel.1 = (f32[128,256]{1,0:T(8,128)S(1)}, f32[128,256]{1,0:T(8,128)S(1)}) custom-call(f32[256,256]{1,0:T(8,128)S(1)} %get-tuple-element.25.cross_ref, f32[192,256]{1,0:T(8,128)S(1)} %bitcast.62, f32[192,256]{1,0:T(8,128)S(1)} %bitcast.60, f32[256,256]{1,0:T(8,128)S(1)} %copy-done.10, f32[256,256]{1,0:T(8,128)S(1)} %invert.1.inv_ref, f32[256,256]{1,0:T(8,128)S(1)} %copy-done.11), custom_call_target="tpu_custom_call" | custom-call | flops 1006632960 | bytes 8000000 | tf_op jit(solution)/shard_map/panel/pallas_call | solution.py:290
  100.5 2.7 %collective-permute-start.17 = (f32[128,256]{1,0:T(8,128)S(1)}, f32[128,256]{1,0:T(8,128)S(1)}, u32[]{:S(2)}, u32[]{:S(2)}) collective-permute-start(f32[128,256]{1,0:T(8,128)S(1)} %add.51), channel_id=1, source_target_pairs={{0,64},{1,65},{2,66},{3,67},{4,68},{5,69},{6,70},{7,71},{8,72},{9,... | collective-permute-start | bytes 393224 | tf_op jit(solution)/shard_map/ppermute | solution.py:38
  103.3 3.8 %collective-permute-done.17 = f32[128,256]{1,0:T(8,128)S(1)} collective-permute-done((f32[128,256]{1,0:T(8,128)S(1)}, f32[128,256]{1,0:T(8,128)S(1)}, u32[]{:S(2)}, u32[]{:S(2)}) %collective-permute-start.17) | collective-permute-done | bytes 131104 | tf_op jit(solution)/shard_map/ppermute | solution.py:38
  112.8 4.8 %collective-permute-start.11 = (f32[2,6,32,256]{3,2,1,0:T(8,128)S(1)}, f32[2,6,32,256]{3,2,1,0:T(8,128)S(1)}, u32[]{:S(2)}, u32[]{:S(2)}) collective-permute-start(f32[2,6,32,256]{3,2,1,0:T(8,128)S(1)} %slice.57), channel_id=1, source_target_pairs={{0,32},{1,33},{2,34},{3,35},{4,36},{5,37},{6,38},{7,39},{8,40},{9,... | collective-permute-start | bytes 1179656 | tf_op jit(solution)/shard_map/ppermute | solution.py:38
  119.0 2.9 %collective-permute-start.23 = (f32[128,256]{1,0:T(8,128)S(1)}, f32[128,256]{1,0:T(8,128)S(1)}, u32[]{:S(2)}, u32[]{:S(2)}) collective-permute-start(f32[128,256]{1,0:T(8,128)S(1)} %add_add_fusion.1), channel_id=1, source_target_pairs={{0,8},{1,9},{2,10},{3,11},{4,12},{5,13},{6,14},{7,15},{8,0},{9,1},... | collective-permute-start | bytes 393224 | tf_op jit(solution)/shard_map/ppermute | solution.py:38
  123.3 3.7 %collective-permute-done.23 = f32[128,256]{1,0:T(8,128)S(1)} collective-permute-done((f32[128,256]{1,0:T(8,128)S(1)}, f32[128,256]{1,0:T(8,128)S(1)}, u32[]{:S(2)}, u32[]{:S(2)}) %collective-permute-start.23) | collective-permute-done | bytes 131104 | tf_op jit(solution)/shard_map/ppermute | solution.py:38
  128.6 2.7 %collective-permute-start.25 = (f32[128,256]{1,0:T(8,128)S(1)}, f32[128,256]{1,0:T(8,128)S(1)}, u32[]{:S(2)}, u32[]{:S(2)}) collective-permute-start(f32[128,256]{1,0:T(8,128)S(1)} %add_add_fusion), channel_id=1, source_target_pairs={{0,16},{1,17},{2,18},{3,19},{4,20},{5,21},{6,22},{7,23},{8,24},{9,... | collective-permute-start | bytes 393224 | tf_op jit(solution)/shard_map/ppermute | solution.py:38
  132.4 4.0 %collective-permute-done.12 = f32[6,32,256]{2,1,0:T(8,128)S(1)} collective-permute-done((f32[6,32,256]{2,1,0:T(8,128)S(1)}, f32[6,32,256]{2,1,0:T(8,128)S(1)}, u32[]{:S(2)}, u32[]{:S(2)}) %collective-permute-start.12) | collective-permute-done | bytes 196640 | tf_op jit(solution)/shard_map/ppermute | solution.py:38
  136.4 4.0 %collective-permute-start.13 = (f32[6,16,256]{2,1,0:T(8,128)S(1)}, f32[6,16,256]{2,1,0:T(8,128)S(1)}, u32[]{:S(2)}, u32[]{:S(2)}) collective-permute-start(f32[6,16,256]{2,1,0:T(8,128)S(1)} %get-tuple-element.31), channel_id=1, source_target_pairs={{0,0},{1,16},{2,32},{3,48},{4,64},{5,80},{6,96},{7,112},{8,1},{9,1... | collective-permute-start | bytes 294920 | tf_op jit(solution)/shard_map/ppermute | solution.py:38
  142.1 5.1 %collective-permute-done.13.first_ref = f32[6,16,256]{2,1,0:T(8,128)S(1)} collective-permute-done((f32[6,16,256]{2,1,0:T(8,128)S(1)}, f32[6,16,256]{2,1,0:T(8,128)S(1)}, u32[]{:S(2)}, u32[]{:S(2)}) %collective-permute-start.13) | collective-permute-done | bytes 98336 | tf_op jit(solution)/shard_map/ppermute | solution.py:38
  147.3 3.9 %collective-permute-done.14.second_ref = f32[6,16,256]{2,1,0:T(8,128)S(1)} collective-permute-done((f32[6,16,256]{2,1,0:T(8,128)S(1)}, f32[6,16,256]{2,1,0:T(8,128)S(1)}, u32[]{:S(2)}, u32[]{:S(2)}) %collective-permute-start.14) | collective-permute-done | bytes 98336 | tf_op jit(solution)/shard_map/ppermute | solution.py:38
  (92 shorter events, 46.0 us)
Async XLA Ops:
  7.2 69.2 %all-gather.3.cloned.1.call-start = ((), (), s32[]{:S(2)}) async-start(), calls=%async_computation | async-start | bytes 1769472 | tf_op jit(solution)/shard_map/all_gather | solution.py:338
  8.2 9.0 %collective-permute-start.8 = (f32[6,16,256]{2,1,0:T(8,128)S(1)}, f32[6,16,256]{2,1,0:T(8,128)S(1)}, u32[]{:S(2)}, u32[]{:S(2)}) collective-permute-start(f32[6,16,256]{2,1,0:T(8,128)S(1)} %fusion.1), channel_id=1, source_target_pairs={{0,8},{1,0},{2,24},{3,16},{4,40},{5,32},{6,56},{7,48},{8,72},{9,64... | collective-permute-start | bytes 294920 | tf_op jit(solution)/shard_map/ppermute | solution.py:38
  15.2 9.2 %collective-permute-start.9 = (f32[6,16,256]{2,1,0:T(8,128)S(1)}, f32[6,16,256]{2,1,0:T(8,128)S(1)}, u32[]{:S(2)}, u32[]{:S(2)}) collective-permute-start(f32[6,16,256]{2,1,0:T(8,128)S(1)} %select_bitcast_fusion.2), channel_id=1, source_target_pairs={{0,0},{1,8},{2,16},{3,24},{4,32},{5,40},{6,48},{7,56},{8,64},{9,72... | collective-permute-start | bytes 294920 | tf_op jit(solution)/shard_map/ppermute | solution.py:38
  26.3 8.0 %collective-permute-start = (f32[192,256]{1,0:T(8,128)S(1)}, f32[192,256]{1,0:T(8,128)S(1)}, u32[]{:S(2)}, u32[]{:S(2)}) collective-permute-start(f32[192,256]{1,0:T(8,128)S(1)} %reshape_squeeze.3), channel_id=1, source_target_pairs={{0,1},{1,2},{2,3},{3,0},{4,5},{5,6},{6,7},{7,4},{8,9},{9,10},{10,1... | collective-permute-start | bytes 589832 | tf_op jit(solution)/shard_map/ppermute | solution.py:38
  28.7 5.8 %collective-permute-start.1 = (f32[192,256]{1,0:T(8,128)S(1)}, f32[192,256]{1,0:T(8,128)S(1)}, u32[]{:S(2)}, u32[]{:S(2)}) collective-permute-start(f32[192,256]{1,0:T(8,128)S(1)} %reshape_squeeze.3), channel_id=1, source_target_pairs={{0,3},{1,0},{2,1},{3,2},{4,7},{5,4},{6,5},{7,6},{8,11},{9,8},{10,9... | collective-permute-start | bytes 589832 | tf_op jit(solution)/shard_map/ppermute | solution.py:38
  34.3 4.8 %collective-permute-start.2 = (f32[96,256]{1,0:T(8,128)S(1)}, f32[96,256]{1,0:T(8,128)S(1)}, u32[]{:S(2)}, u32[]{:S(2)}) collective-permute-start(f32[96,256]{1,0:T(8,128)S(1)} %slice.50), channel_id=1, source_target_pairs={{0,1},{1,2},{2,3},{3,0},{4,5},{5,6},{6,7},{7,4},{8,9},{9,10},{10,1... | collective-permute-start | bytes 294920 | tf_op jit(solution)/shard_map/ppermute | solution.py:38
  34.6 4.6 %collective-permute-start.3 = (f32[96,256]{1,0:T(8,128)S(1)}, f32[96,256]{1,0:T(8,128)S(1)}, u32[]{:S(2)}, u32[]{:S(2)}) collective-permute-start(f32[96,256]{1,0:T(8,128)S(1)} %slice.51), channel_id=1, source_target_pairs={{0,3},{1,0},{2,1},{3,2},{4,7},{5,4},{6,5},{7,6},{8,11},{9,8},{10,9... | collective-permute-start | bytes 294920 | tf_op jit(solution)/shard_map/ppermute | solution.py:38
  39.1 22.8 %collective-permute-start.4 = (f32[768,256]{1,0:T(8,128)S(1)}, f32[768,256]{1,0:T(8,128)S(1)}, u32[]{:S(2)}, u32[]{:S(2)}) collective-permute-start(f32[768,256]{1,0:T(8,128)S(1)} %constant_dynamic-update-slice_fusion.refs_0_), channel_id=1, source_target_pairs={{0,4},{1,5},{2,6},{3,7},{4,8},{5,9},{6,10},{7,11},{8,12},{9,13},{1... | collective-permute-start | bytes 2359304 | tf_op jit(solution)/shard_map/ppermute | solution.py:38
  39.2 22.8 %collective-permute-start.6 = (f32[768,256]{1,0:T(8,128)S(1)}, f32[768,256]{1,0:T(8,128)S(1)}, u32[]{:S(2)}, u32[]{:S(2)}) collective-permute-start(f32[768,256]{1,0:T(8,128)S(1)} %constant_dynamic-update-slice_fusion.refs_0_), channel_id=1, source_target_pairs={{0,12},{1,13},{2,14},{3,15},{4,0},{5,1},{6,2},{7,3},{8,4},{9,5},{1... | collective-permute-start | bytes 2359304 | tf_op jit(solution)/shard_map/ppermute | solution.py:38
  61.9 14.4 %collective-permute-start.5 = (f32[384,256]{1,0:T(8,128)S(1)}, f32[384,256]{1,0:T(8,128)S(1)}, u32[]{:S(2)}, u32[]{:S(2)}) collective-permute-start(f32[384,256]{1,0:T(8,128)S(1)} %slice.52), channel_id=1, source_target_pairs={{0,4},{1,5},{2,6},{3,7},{4,8},{5,9},{6,10},{7,11},{8,12},{9,13},{1... | collective-permute-start | bytes 1179656 | tf_op jit(solution)/shard_map/ppermute | solution.py:38
  62.1 14.2 %collective-permute-start.7 = (f32[384,256]{1,0:T(8,128)S(1)}, f32[384,256]{1,0:T(8,128)S(1)}, u32[]{:S(2)}, u32[]{:S(2)}) collective-permute-start(f32[384,256]{1,0:T(8,128)S(1)} %slice.53), channel_id=1, source_target_pairs={{0,12},{1,13},{2,14},{3,15},{4,0},{5,1},{6,2},{7,3},{8,4},{9,5},{1... | collective-permute-start | bytes 1179656 | tf_op jit(solution)/shard_map/ppermute | solution.py:38
  86.2 26.5 %collective-permute-start.10 = (f32[4,6,32,256]{3,2,1,0:T(8,128)S(1)}, f32[4,6,32,256]{3,2,1,0:T(8,128)S(1)}, u32[]{:S(2)}, u32[]{:S(2)}) collective-permute-start(f32[4,6,32,256]{3,2,1,0:T(8,128)S(1)} %get-tuple-element.24), channel_id=1, source_target_pairs={{0,16},{1,17},{2,18},{3,19},{4,20},{5,21},{6,22},{7,23},{8,24},{9,... | collective-permute-start | bytes 2359304 | tf_op jit(solution)/shard_map/ppermute | solution.py:38
  100.5 6.5 %collective-permute-start.17 = (f32[128,256]{1,0:T(8,128)S(1)}, f32[128,256]{1,0:T(8,128)S(1)}, u32[]{:S(2)}, u32[]{:S(2)}) collective-permute-start(f32[128,256]{1,0:T(8,128)S(1)} %add.51), channel_id=1, source_target_pairs={{0,64},{1,65},{2,66},{3,67},{4,68},{5,69},{6,70},{7,71},{8,72},{9,... | collective-permute-start | bytes 393224 | tf_op jit(solution)/shard_map/ppermute | solution.py:38
  103.3 5.5 %collective-permute-start.18 = (f32[128,256]{1,0:T(8,128)S(1)}, f32[128,256]{1,0:T(8,128)S(1)}, u32[]{:S(2)}, u32[]{:S(2)}) collective-permute-start(f32[128,256]{1,0:T(8,128)S(1)} %add.51), channel_id=1, source_target_pairs={{0,96},{1,97},{2,98},{3,99},{4,100},{5,101},{6,102},{7,103},{8,104... | collective-permute-start | bytes 393224 | tf_op jit(solution)/shard_map/ppermute | solution.py:38
  108.8 8.9 %collective-permute-start.19 = (f32[128,256]{1,0:T(8,128)S(1)}, f32[128,256]{1,0:T(8,128)S(1)}, u32[]{:S(2)}, u32[]{:S(2)}) collective-permute-start(f32[128,256]{1,0:T(8,128)S(1)} %add_add_fusion.2), channel_id=1, source_target_pairs={{0,1},{1,0},{2,3},{3,2},{4,5},{5,4},{6,7},{7,6},{8,9},{9,8},{10,11... | collective-permute-start | bytes 393224 | tf_op jit(solution)/shard_map/ppermute | solution.py:38
  108.8 8.8 %collective-permute-start.20 = (f32[128,256]{1,0:T(8,128)S(1)}, f32[128,256]{1,0:T(8,128)S(1)}, u32[]{:S(2)}, u32[]{:S(2)}) collective-permute-start(f32[128,256]{1,0:T(8,128)S(1)} %add_add_fusion.2), channel_id=1, source_target_pairs={{0,2},{1,3},{2,0},{3,1},{4,6},{5,7},{6,4},{7,5},{8,10},{9,11},{10,... | collective-permute-start | bytes 393224 | tf_op jit(solution)/shard_map/ppermute | solution.py:38
  111.1 6.6 %collective-permute-start.21 = (f32[128,256]{1,0:T(8,128)S(1)}, f32[128,256]{1,0:T(8,128)S(1)}, u32[]{:S(2)}, u32[]{:S(2)}) collective-permute-start(f32[128,256]{1,0:T(8,128)S(1)} %add_add_fusion.2), channel_id=1, source_target_pairs={{0,3},{1,2},{2,1},{3,0},{4,7},{5,6},{6,5},{7,4},{8,11},{9,10},{10,... | collective-permute-start | bytes 393224 | tf_op jit(solution)/shard_map/ppermute | solution.py:38
  112.8 18.5 %collective-permute-start.11 = (f32[2,6,32,256]{3,2,1,0:T(8,128)S(1)}, f32[2,6,32,256]{3,2,1,0:T(8,128)S(1)}, u32[]{:S(2)}, u32[]{:S(2)}) collective-permute-start(f32[2,6,32,256]{3,2,1,0:T(8,128)S(1)} %slice.57), channel_id=1, source_target_pairs={{0,32},{1,33},{2,34},{3,35},{4,36},{5,37},{6,38},{7,39},{8,40},{9,... | collective-permute-start | bytes 1179656 | tf_op jit(solution)/shard_map/ppermute | solution.py:38
  117.7 5.6 %collective-permute-start.22 = (f32[128,256]{1,0:T(8,128)S(1)}, f32[128,256]{1,0:T(8,128)S(1)}, u32[]{:S(2)}, u32[]{:S(2)}) collective-permute-start(f32[128,256]{1,0:T(8,128)S(1)} %add_add_fusion.1), channel_id=1, source_target_pairs={{0,4},{1,5},{2,6},{3,7},{4,0},{5,1},{6,2},{7,3},{8,12},{9,13},{10,... | collective-permute-start | bytes 393224 | tf_op jit(solution)/shard_map/ppermute | solution.py:38
  119.0 8.0 %collective-permute-start.23 = (f32[128,256]{1,0:T(8,128)S(1)}, f32[128,256]{1,0:T(8,128)S(1)}, u32[]{:S(2)}, u32[]{:S(2)}) collective-permute-start(f32[128,256]{1,0:T(8,128)S(1)} %add_add_fusion.1), channel_id=1, source_target_pairs={{0,8},{1,9},{2,10},{3,11},{4,12},{5,13},{6,14},{7,15},{8,0},{9,1},... | collective-permute-start | bytes 393224 | tf_op jit(solution)/shard_map/ppermute | solution.py:38
  121.9 6.7 %collective-permute-start.24 = (f32[128,256]{1,0:T(8,128)S(1)}, f32[128,256]{1,0:T(8,128)S(1)}, u32[]{:S(2)}, u32[]{:S(2)}) collective-permute-start(f32[128,256]{1,0:T(8,128)S(1)} %add_add_fusion.1), channel_id=1, source_target_pairs={{0,12},{1,13},{2,14},{3,15},{4,8},{5,9},{6,10},{7,11},{8,4},{9,5},... | collective-permute-start | bytes 393224 | tf_op jit(solution)/shard_map/ppermute | solution.py:38
  131.5 4.9 %collective-permute-start.12 = (f32[6,32,256]{2,1,0:T(8,128)S(1)}, f32[6,32,256]{2,1,0:T(8,128)S(1)}, u32[]{:S(2)}, u32[]{:S(2)}) collective-permute-start(f32[6,32,256]{2,1,0:T(8,128)S(1)} %slice_bitcast_fusion), channel_id=1, source_target_pairs={{0,96},{1,97},{2,98},{3,99},{4,100},{5,101},{6,102},{7,103},{8,104... | collective-permute-start | bytes 589832 | tf_op jit(solution)/shard_map/ppermute | solution.py:38
  136.4 10.9 %collective-permute-start.13 = (f32[6,16,256]{2,1,0:T(8,128)S(1)}, f32[6,16,256]{2,1,0:T(8,128)S(1)}, u32[]{:S(2)}, u32[]{:S(2)}) collective-permute-start(f32[6,16,256]{2,1,0:T(8,128)S(1)} %get-tuple-element.31), channel_id=1, source_target_pairs={{0,0},{1,16},{2,32},{3,48},{4,64},{5,80},{6,96},{7,112},{8,1},{9,1... | collective-permute-start | bytes 294920 | tf_op jit(solution)/shard_map/ppermute | solution.py:38
  140.4 10.8 %collective-permute-start.14 = (f32[6,16,256]{2,1,0:T(8,128)S(1)}, f32[6,16,256]{2,1,0:T(8,128)S(1)}, u32[]{:S(2)}, u32[]{:S(2)}) collective-permute-start(f32[6,16,256]{2,1,0:T(8,128)S(1)} %get-tuple-element.30), channel_id=1, source_target_pairs={{0,1},{1,17},{2,33},{3,49},{4,65},{5,81},{6,97},{7,113},{8,0},{9,1... | collective-permute-start | bytes 294920 | tf_op jit(solution)/shard_map/ppermute | solution.py:38
  (15 other events, 57.9 us)
Sparse Core Ops, SparseCore 0:
  25.3 25.8 all-gather.2

commit v2 on v0

v2 whole, which is shorter than its diff:
```python
import functools

import jax
import jax.numpy as jnp
from jax import lax
from jax.experimental import pallas as pl
from jax.experimental.pallas import tpu as pltpu
from jax.sharding import PartitionSpec as P

F32 = jnp.float32
BF16 = jnp.bfloat16
AXES = ("prow", "pcol")
NB = 256
UR = 12
TPC = 6
PIECE = 16 * UR
GROUP = 4 * PIECE
SLAB = PIECE * TPC * 2
COLS = TPC * NB
VMEM = pl.BlockSpec(memory_space=pltpu.VMEM)
ANY = pl.BlockSpec(memory_space=pl.ANY)
HBM = pl.BlockSpec(memory_space=pltpu.HBM)


def pairs(target):
    found = []
    for x in range(4):
        for c in range(2):
            for z in range(4):
                for y in range(4):
                    tx, tc, tz, ty = target(x, c, z, y)
                    found.append(
                        ((2 * x + c) * 16 + 4 * z + y, (2 * (tx % 4) + tc) * 16 + 4 * (tz % 4) + ty % 4)
                    )
    return found


def permute(value, target):
    return lax.ppermute(value, AXES, pairs(target))


def first_axis(step):
    return lambda x, c, z, y: (x, c, z, y + step) if c == 0 else (x, c, z + step, y)


def second_axis(step):
    return lambda x, c, z, y: (x, c, z + step, y) if c == 0 else (x, c, z, y + step)


def other_core(x, c, z, y):
    return x, 1 - c, z, y


def halving(stage):
    def target(x, c, z, y):
        return (x ^ 1 if (stage + c) % 2 == 0 else x ^ 3), c, z, y

    return target


def crossing(stage, mask):
    def target(x, c, z, y):
        axis = (stage + c) % 3
        if axis == 0:
            return x ^ mask, c, z, y
        if axis == 1:
            return x, c, z, y ^ mask
        return x, c, z ^ mask, y

    return target


def opposite_half(x, c, z, y):
    return x, c, z ^ 2, y


def to_tiles(x, c, z, y):
    p, q = 2 * x + c, 4 * z + y
    tp, tq = (q % 8) ^ p, 8 * (q // 8) + p
    return tp // 2, tp % 2, tq // 4, tq % 4


def to_rows(x, c, z, y):
    p, q = 2 * x + c, 4 * z + y
    tp, tq = q % 8, 8 * (q // 8) + (p ^ (q % 8))
    return tp // 2, tp % 2, tq // 4, tq % 4


def place():
    p, q = lax.axis_index("prow"), lax.axis_index("pcol")
    return p // 2, p % 2, q // 4, q % 4


def split(value):
    high = value.astype(BF16)
    return high, (value - high.astype(F32)).astype(BF16)


def dot3(lh, ll, rh, rl):
    total = jnp.dot(lh, rh, preferred_element_type=F32)
    total += jnp.dot(ll, rh, preferred_element_type=F32)
    total += jnp.dot(lh, rl, preferred_element_type=F32)
    return total


def dot6(left, right):
    return jnp.dot(left, right, precision=lax.Precision.HIGHEST, preferred_element_type=F32)


def tdot6(left, right):
    return lax.dot_general(
        left, right, (((0,), (0,)), ((), ())), precision=lax.Precision.HIGHEST, preferred_element_type=F32
    )


def call(kernel, inputs, outputs, limit, flops=0, size=0, scratch=(), specs=None):
    if specs:
        inputs = [
            pltpu.with_memory_space_constraint(value, pltpu.HBM) if spec is HBM else value
            for value, spec in zip(inputs, specs)
        ]
    return pl.pallas_call(
        kernel,
        in_specs=specs or [VMEM] * len(inputs),
        out_specs=[VMEM] * len(outputs),
        out_shape=list(outputs),
        scratch_shapes=list(scratch),
        compiler_params=pltpu.CompilerParams(vmem_limit_bytes=limit << 20),
        cost_estimate=pl.CostEstimate(flops=flops, bytes_accessed=size, transcendentals=0),
        name=(kernel.func if isinstance(kernel, functools.partial) else kernel).__name__,
    )(*inputs)


def kept(*shape):
    return pltpu.VMEM(shape, F32)


def free(*shape):
    return jax.ShapeDtypeStruct(shape, F32)


def order_rows(l_ref, piece_ref):
    piece_ref[...] = jnp.swapaxes(l_ref[...], 0, 1).reshape(PIECE, NB)


def split_tiles(rows_ref, _, __, keep_ref, send_ref):
    high = place()[2] // 2
    for v in range(TPC):
        keep_ref[v] = rows_ref[2 * v + high]
        send_ref[v] = rows_ref[2 * v + 1 - high]


def join_group(own_ref, up_ref, down_ref, far_up_ref, far_down_ref, _, out_ref):
    out_ref[:PIECE] = own_ref[...]
    out_ref[PIECE : 2 * PIECE] = up_ref[...]
    out_ref[2 * PIECE : 3 * PIECE] = down_ref[...]
    out_ref[3 * PIECE : 3 * PIECE + PIECE // 2] = far_up_ref[...]
    out_ref[3 * PIECE + PIECE // 2 :] = far_down_ref[...]


def take_halves(up_ref, down_ref, _, __, first_ref, second_ref):
    first_ref[...] = up_ref[: GROUP // 2]
    second_ref[...] = down_ref[GROUP // 2 :]


def fetch(step, s_ref, held_ref, sem):
    _, c, z, y = place()
    copies = []
    for i, offset in enumerate((0, 3, 1, 2)):
        zz = jnp.where(c == 0, z + step, z + offset) % 4
        yy = jnp.where(c == 0, y + offset, y + step) % 4
        copy = pltpu.make_async_copy(
            s_ref.at[pl.ds((zz * 4 + yy) * SLAB, SLAB), :],
            held_ref.at[pl.ds(i * SLAB, SLAB), :],
            sem.at[i],
        )
        copy.start()
        copies.append(copy)
    return copies


def grids():
    row = lax.broadcasted_iota(jnp.int32, (NB, NB), 0)
    col = lax.broadcasted_iota(jnp.int32, (NB, NB), 1)
    return row, col


def invert_blocks(
    s_ref, l_ref, lbar_ref, own_ref, mine_ref, _, __,
    first_s, second_s, strict_ref, inverse_ref, l_out, lbar_out, own_out, mine_out, sem, small,
):
    panel = pltpu.make_async_copy(l_ref, l_out, small.at[0])
    panel.start()
    copies = fetch(0, s_ref, first_s, sem.at[0])
    for i, (src, dst) in enumerate(((lbar_ref, lbar_out), (own_ref, own_out), (mine_ref, mine_out))):
        copy = pltpu.make_async_copy(src, dst, small.at[i + 1])
        copy.start()
        copies.append(copy)
    copies += fetch(3, s_ref, second_s, sem.at[1])
    panel.wait()
    row, col = grids()
    lower = l_out[...]
    by_row = 1.0 / jnp.sum(jnp.where(row == col, lower, 0.0), axis=1, keepdims=True)
    strict = jnp.where(row > col, lower * by_row, 0.0)
    power = jnp.where(row // 16 == col // 16, -strict, 0.0)
    inverse = jnp.where(row == col, 1.0, 0.0) + power
    for _ in range(3):
        power = dot6(power, power)
        inverse = inverse + dot6(power, inverse)
    strict_ref[...] = strict
    inverse_ref[...] = inverse
    for copy in copies:
        copy.wait()


def invert_rest(s_ref, strict_ref, blocks_ref, l_ref, _, third_s, fourth_s, inverse_ref, sem):
    copies = fetch(1, s_ref, third_s, sem.at[0]) + fetch(2, s_ref, fourth_s, sem.at[1])

    @pl.when(place()[0] >= 0)
    def _():
        row, col = grids()
        strict = strict_ref[...]
        inverse = blocks_ref[...]
        size = 16
        while size < NB:
            beside = (row // (2 * size) == col // (2 * size)) & (row // size != col // size)
            inverse = inverse - dot6(inverse, dot6(jnp.where(beside, strict, 0.0), inverse))
            size *= 2
        by_col = 1.0 / jnp.sum(jnp.where(row == col, l_ref[...], 0.0), axis=0, keepdims=True)
        inverse_ref[...] = inverse * by_col

    for copy in copies:
        copy.wait()


def product(lh, ll, s_ref, j):
    at = range(4 * j, 4 * j + 4)
    lines = jnp.concatenate([s_ref[pl.ds(k, GROUP, stride=2 * TPC), :] for k in at], axis=1)
    return dot3(lh, ll, *split(lines))


def multiply_first(l_ref, s_ref, out_ref):
    lh, ll = split(l_ref[...].T)
    for j in range(3):
        out_ref[:, j * 512 : (j + 1) * 512] = product(lh, ll, s_ref, j)


def multiply_next(la_ref, sa_ref, lb_ref, sb_ref, acc_ref, out_ref):
    ah, al = split(la_ref[...].T)
    bh, bl = split(lb_ref[...].T)
    for j in range(3):
        at = slice(j * 512, (j + 1) * 512)
        out_ref[:, at] = acc_ref[:, at] + product(ah, al, sa_ref, j) + product(bh, bl, sb_ref, j)


def multiply_last(la_ref, lb_ref, s_ref, acc_ref, _, keep_ref, send_ref):
    x, c, z, y = place()
    lh, ll = split(jnp.concatenate([la_ref[...], lb_ref[...]], axis=0).T)
    turn = 2 * (z % 2) + y // 2
    for j in range(3):
        at = slice(j * 512, (j + 1) * 512)
        part = acc_ref[:, at] + product(lh, ll, s_ref, j)
        turned = part.T.reshape(2, 2, 8, 16, NB)
        for odd in range(2):

            @pl.when((c ^ (y % 2)) == odd)
            def _():
                for i in range(4):
                    away = i ^ turn ^ x
                    near = jnp.where(away == 0, 0, jnp.where(away == 1, 2, jnp.where(away == 3, 1, 3)))
                    far = jnp.where(away == 0, 0, jnp.where(away == 1, 1, jnp.where(away == 3, 2, 3)))
                    mine = jnp.where(c == 0, near, far)
                    other = jnp.where(c == 0, far, near)
                    for v in range(2):
                        keep_ref[mine, 2 * j + v] = turned[v, :, 2 * i + odd]
                        send_ref[other, 2 * j + v] = turned[v, :, 2 * i + 1 - odd]


def add_cores(rows, rows_in, keep_ref, send_ref):
    keep_ref[...] = rows[:2] + rows_in[:2]
    send_ref[...] = rows[2:] + rows_in[2:]


def add_pairs(rows, rows_in, keep_ref, send_ref):
    keep_ref[...] = rows[0] + rows_in[0]
    send_ref[...] = rows[1] + rows_in[1]


def add_rows(rows, rows_in, keep_ref, send_ref):
    high = place()[2] // 2
    keep_ref[...] = rows[:, high] + rows_in[:, high]
    send_ref[...] = rows[:, 1 - high] + rows_in[:, 1 - high]


def join_rows(keep_ref, other_ref, out_ref):
    high = place()[2] // 2
    for v in range(TPC):
        out_ref[2 * v + high] = keep_ref[v]
        out_ref[2 * v + 1 - high] = other_ref[v]


def finish_rows(own_ref, product_ref, inv_ref, out_ref):
    adjusted = own_ref[...] - 2.0 * product_ref[...]
    out_ref[...] = dot6(adjusted.reshape(PIECE, NB), inv_ref[...]).reshape(UR, 16, NB)


def start_panel(share, own_ref, mine_ref, inv_ref, lbar_ref, out_ref):
    row, col = grids()
    gram = tdot6(inv_ref[...], tdot6(own_ref[...].reshape(PIECE, NB), mine_ref[...].reshape(PIECE, NB)))
    out_ref[...] = lbar_ref[...] * share - jnp.where(row >= col, gram, 0.0)


def finish_panel(first_ref, second_ref, l_first_ref, l_second_ref, l_ref, inv_ref, base_ref, keep_ref, send_ref):
    c = place()[1]
    row, col = grids()
    half = PIECE // 2
    cross = tdot6(first_ref[...].reshape(half, NB), l_first_ref[...].reshape(half, NB))
    cross += tdot6(second_ref[...].reshape(half, NB), l_second_ref[...].reshape(half, NB))
    inverse = inv_ref[...]
    fresh = base_ref[...] + jnp.where(row >= col, 2.0 * tdot6(inverse, cross), 0.0)
    phi = tdot6(l_ref[...], fresh)
    phi = jnp.where(row > col, phi, jnp.where(row == col, 0.5 * phi, 0.0))
    full = dot6(tdot6(inverse, phi), inverse)
    result = 0.5 * (full + full.T)
    n = NB // 2
    row, col = row[:n, :n], col[:n, :n]
    last = result[n:, n:]
    mixed = jnp.where(row >= col, result[:n, :n], last)
    diagonal = jnp.sum(jnp.where(row == col, last, 0.0), axis=0, keepdims=True)
    lower = result[n:, :n]
    keep_ref[:n] = jnp.where(c == 0, lower, mixed)
    send_ref[:n] = jnp.where(c == 0, mixed, lower)
    keep_ref[n:] = jnp.broadcast_to(diagonal, (8, n))
    send_ref[n:] = jnp.broadcast_to(diagonal, (8, n))


def add_two(part, other, out_ref):
    out_ref[...] = part[...] + other[...]


def add_four(part, near, opposite, beyond, _, out_ref):
    out_ref[...] = (part[...] + near[...]) + (beyond[...] + opposite[...])


def unpack(part, rest, out_ref):
    c = place()[1]
    n = NB // 2
    row = lax.broadcasted_iota(jnp.int32, (n, n), 0)
    col = lax.broadcasted_iota(jnp.int32, (n, n), 1)
    lower = jnp.where(c == 0, part[:n], rest[:n])
    mixed = jnp.where(c == 0, rest[:n], part[:n])
    diagonal = jnp.where(c == 0, rest[n : n + 1], part[n : n + 1])
    turned = mixed.T
    out_ref[:n, :n] = jnp.where(row >= col, mixed, turned)
    out_ref[n:, n:] = jnp.where(row == col, diagonal, jnp.where(row < col, mixed, turned))
    out_ref[n:, :n] = lower
    out_ref[:n, n:] = lower.T


def shards(l_panel, l_rows, lbar_panel, lbar_rows, sbar):
    share = 1.0 / (lax.axis_size("prow") * lax.axis_size("pcol"))
    s_lines = sbar.reshape(16 * SLAB, 128)
    mine = jnp.transpose(l_rows[0], (1, 0, 2))
    own = jnp.transpose(lbar_rows[0], (1, 0, 2))
    dma = pltpu.SemaphoreType.DMA
    lines = kept(4 * SLAB, 128)
    square = kept(NB, NB)

    (piece,) = call(order_rows, [mine], [free(PIECE, NB)], 4, size=400_000)
    up = permute(piece, first_axis(1))
    down = permute(piece, first_axis(-1))
    s0, s3, strict, blocks, l_kept, lbar_kept, own_kept, mine_kept = call(
        invert_blocks,
        [s_lines, l_panel, lbar_panel, own, mine, up, down],
        [lines, lines, square, square, square, square, kept(UR, 16, NB), kept(UR, 16, NB)],
        4,
        flops=6 * 12 * NB**3,
        size=10_000_000,
        scratch=[dma((2, 4)), dma((4,))],
        specs=[HBM] * 5 + [ANY] * 2,
    )
    far_up = permute(up[: PIECE // 2], first_axis(1))
    far_down = permute(down[PIECE // 2 :], first_axis(-1))
    tile = kept(TPC, 16, NB)
    rows = permute(mine, to_tiles)
    (group,) = call(
        join_group,
        [piece, up, down, far_up, far_down, blocks],
        [free(GROUP, NB)],
        4,
        size=1_600_000,
        specs=[VMEM] * 5 + [ANY],
    )
    group_up = permute(group, second_axis(1))
    group_down = permute(group, second_axis(-1))
    s1, s2, inverse = call(
        invert_rest,
        [s_lines, strict, blocks, l_kept, group],
        [lines, lines, square],
        4,
        flops=8 * 12 * NB**3,
        size=10_000_000,
        scratch=[dma((2, 4))],
        specs=[HBM] + [VMEM] * 3 + [ANY],
    )
    work = dict(flops=6 * GROUP * COLS * NB, size=6_000_000)
    wide = kept(NB, COLS)
    (total,) = call(multiply_first, [group, s0], [wide], 8, **work)
    l_keep, l_send = call(
        split_tiles, [rows, inverse, total], [tile, tile], 4, size=800_000, specs=[VMEM, ANY, ANY]
    )
    l_other = permute(l_send, opposite_half)
    pass_up, pass_down = call(
        take_halves,
        [group_up, group_down, total, l_keep],
        [free(GROUP // 2, NB)] * 2,
        4,
        size=1_000_000,
        specs=[VMEM, VMEM, ANY, ANY],
    )
    far_a = permute(pass_up, second_axis(1))
    far_b = permute(pass_down, second_axis(-1))
    (total,) = call(multiply_next, [group_up, s3, group_down, s1, total], [wide], 8, **work)
    share4 = kept(4, TPC, 2, 16, NB)
    keep, send = call(
        multiply_last, [far_a, far_b, s2, total, l_other], [share4, share4], 8, specs=[VMEM] * 4 + [ANY], **work
    )

    share2 = kept(2, TPC, 2, 16, NB)
    share1 = kept(TPC, 2, 16, NB)
    (base,) = call(
        functools.partial(start_panel, share), [own_kept, mine_kept, inverse, lbar_kept], [square], 6,
        flops=2 * 12 * NB**3, size=4_000_000,
    )
    keep, send = call(add_cores, [keep, permute(send, other_core)], [share2, share2], 6, size=2_000_000)
    keep, send = call(add_pairs, [keep, permute(send, halving(0))], [share1, share1], 6, size=1_000_000)
    keep, send = call(add_rows, [keep, permute(send, halving(1))], [tile, tile], 6, size=1_000_000)
    half = kept(NB // 2 + 8, NB // 2)
    part, other = call(
        finish_panel,
        [keep, send, l_keep, l_other, l_kept, inverse, base],
        [half, half],
        8,
        flops=6 * 12 * NB**3,
        size=4_000_000,
    )

    (rows,) = call(join_rows, [keep, permute(send, opposite_half)], [free(UR, 16, NB)], 4, size=800_000)
    (part,) = call(add_two, [part, permute(other, other_core)], [half], 4, size=500_000)

    def add_around(stage, after):
        others = [permute(part, crossing(stage, mask)) for mask in (1, 3, 2)]
        return call(add_four, [part, *others, after], [half], 4, size=1_000_000, specs=[VMEM] * 4 + [ANY])

    (part,) = add_around(0, rows)
    rows = permute(rows, to_rows)
    (part,) = add_around(1, inverse)
    (part,) = add_around(2, rows)
    (abar,) = call(
        finish_rows,
        [own_kept, rows, inverse],
        [free(UR, 16, NB)],
        6,
        flops=12 * PIECE * NB * NB,
        size=1_000_000,
    )
    rest = permute(part, other_core)
    (abar_panel,) = call(unpack, [part, rest], [free(NB, NB)], 4, size=500_000)
    return jnp.transpose(abar, (1, 0, 2))[None], abar_panel


def solution(mesh):
    return jax.shard_map(
        shards,
        mesh=mesh,
        in_specs=(
            P(),
            P("prow", "pcol", None, None),
            P(),
            P("prow", "pcol", None, None),
            P("prow", None, None, "pcol", None, None),
        ),
        out_specs=(P("prow", "pcol", None, None), P()),
        check_vma=False,
    )
```

time: 446 us -> 105 us (0.24)
  the two profiles are of different devices: /device:TPU:1 before, /device:TPU:7 now
where the time goes in v2:
time: 105 us
  starting transfers between devices  46.9 us (45%)
  waiting for transfers between devices  32.4 us (31%)
  Pallas kernels  24 us (23%)
    ppermute x26, starting transfers between devices, permute(): return lax.ppermute(value, AXES, pairs(target))  46.9 us
    ppermute x26, waiting for transfers between devices, permute(): return lax.ppermute(value, AXES, pairs(target))  32.4 us
    pallas_call x21, Pallas kernels, call(): pl.pallas_call(kernel, in_specs=specs or [VMEM] * len(inputs), out_specs=...  24 us
  transfers between devices with their start and end apart: 26, of which 14 were waited for; matrix products, arithmetic and copies ran while one was open for 0% of the time, Pallas kernels for 19%

profile of v2, /device:TPU:7, one launch (start us, length us, event | category | flops | bytes accessed | tf_op | source)
XLA Modules:
  0.0 105.2 jit_solution(16030323741202720200)
XLA Ops:
  1.6 3.8 %collective-permute-start.1 = (f32[192,256]{1,0:T(8,128)S(1)}, f32[192,256]{1,0:T(8,128)S(1)}, u32[]{:S(2)}, u32[]{:S(2)}) collective-permute-start(f32[192,256]{1,0:T(8,128)S(1)} %order_rows.1.own_ref), channel_id=1, source_target_pairs={{0,3},{1,0},{2,1},{3,2},{4,7},{5,4},{6,5},{7,6},{8,11},{9,8},{10,9... | collective-permute-start | bytes 589832 | tf_op jit(solution)/shard_map/ppermute | solution.py:39
  5.4 2.6 %collective-permute-done.1.__.down_ref = f32[192,256]{1,0:T(8,128)S(1)} collective-permute-done((f32[192,256]{1,0:T(8,128)S(1)}, f32[192,256]{1,0:T(8,128)S(1)}, u32[]{:S(2)}, u32[]{:S(2)}) %collective-permute-start.1) | collective-permute-done | bytes 196640 | tf_op jit(solution)/shard_map/ppermute | solution.py:39
  8.1 3.2 %collective-permute-start.3 = (f32[96,256]{1,0:T(8,128)S(1)}, f32[96,256]{1,0:T(8,128)S(1)}, u32[]{:S(2)}, u32[]{:S(2)}) collective-permute-start(f32[96,256]{1,0:T(8,128)S(1)} %slice.9), channel_id=1, source_target_pairs={{0,3},{1,0},{2,1},{3,2},{4,7},{5,4},{6,5},{7,6},{8,11},{9,8},{10,9... | collective-permute-start | bytes 294920 | tf_op jit(solution)/shard_map/ppermute | solution.py:39
  11.6 4.2 %invert_blocks.1 = (f32[9216,128]{1,0:T(8,128)S(1)}, f32[9216,128]{1,0:T(8,128)S(1)}, f32[256,256]{1,0:T(8,128)S(1)}, f32[256,256]{1,0:T(8,128)S(1)}, f32[256,25...) custom-call(f32[36864,128]{1,0:T(8,128)} %bitcast.13, ...), custom_call_target="tpu_custom_call" | custom-call | flops 1207959552 | bytes 10000000 | tf_op jit(solution)/shard_map/invert_blocks/pallas_call | solution.py:122
  16.3 2.9 %collective-permute-start.5 = (f32[768,256]{1,0:T(8,128)S(1)}, f32[768,256]{1,0:T(8,128)S(1)}, u32[]{:S(2)}, u32[]{:S(2)}) collective-permute-start(f32[768,256]{1,0:T(8,128)S(1)} %join_group.1.l_ref._), channel_id=1, source_target_pairs={{0,12},{1,13},{2,14},{3,15},{4,0},{5,1},{6,2},{7,3},{8,4},{9,5},{1... | collective-permute-start | bytes 2359304 | tf_op jit(solution)/shard_map/ppermute | solution.py:39
  19.2 3.4 %collective-permute-start.6 = (f32[12,16,256]{2,1,0:T(8,128)S(1)}, f32[12,16,256]{2,1,0:T(8,128)S(1)}, u32[]{:S(2)}, u32[]{:S(2)}) collective-permute-start(f32[12,16,256]{2,1,0:T(8,128)S(1)} %bitcast.12), channel_id=1, source_target_pairs={{0,0},{1,16},{2,32},{3,48},{4,64},{5,80},{6,96},{7,112},{8,8},{9,2... | collective-permute-start | bytes 589832 | tf_op jit(solution)/shard_map/ppermute | solution.py:39
  22.5 4.5 %invert_rest.1 = (f32[9216,128]{1,0:T(8,128)S(1)}, f32[9216,128]{1,0:T(8,128)S(1)}, f32[256,256]{1,0:T(8,128)S(1)}) custom-call(f32[36864,128]{1,0:T(8,128)} %bitcast.14, f32[256,256]{1,0:T(8,128)S(1)} %get-tuple-element.30.strict_ref, f32[256,256]{1,0:T(8,128)S(1)} %get-tuple-element.28._.blocks_ref, f32[256,256]{1,0:T(8,128)S(1)} %get-tuple-element.31.l_ref, ...), custom_call_target="tpu_custom_call" | custom-call | flops 1610612736 | bytes 10000000 | tf_op jit(solution)/shard_map/invert_rest/pallas_call | solution.py:122
  27.1 2.1 %multiply_first.1.__._.acc_ref = f32[256,1536]{1,0:T(8,128)S(1)} custom-call(f32[768,256]{1,0:T(8,128)S(1)} %join_group.1.l_ref._, f32[9216,128]{1,0:T(8,128)S(1)} %get-tuple-element.29.s_ref), custom_call_target="tpu_custom_call" | custom-call | flops 1811939328 | bytes 6000000 | tf_op jit(solution)/shard_map/multiply_first/pallas_call | solution.py:122
  29.1 3.2 %collective-permute-done.6.rows_ref = f32[12,16,256]{2,1,0:T(8,128)S(1)} collective-permute-done((f32[12,16,256]{2,1,0:T(8,128)S(1)}, f32[12,16,256]{2,1,0:T(8,128)S(1)}, u32[]{:S(2)}, u32[]{:S(2)}) %collective-permute-start.6) | collective-permute-done | bytes 196640 | tf_op jit(solution)/shard_map/ppermute | solution.py:39
  32.3 3.1 %collective-permute-done.4.up_ref.la_ref = f32[768,256]{1,0:T(8,128)S(1)} collective-permute-done((f32[768,256]{1,0:T(8,128)S(1)}, f32[768,256]{1,0:T(8,128)S(1)}, u32[]{:S(2)}, u32[]{:S(2)}) %collective-permute-start.4) | collective-permute-done | bytes 786464 | tf_op jit(solution)/shard_map/ppermute | solution.py:39
  35.6 2.7 %collective-permute-start.8 = (f32[384,256]{1,0:T(8,128)S(1)}, f32[384,256]{1,0:T(8,128)S(1)}, u32[]{:S(2)}, u32[]{:S(2)}) collective-permute-start(f32[384,256]{1,0:T(8,128)S(1)} %get-tuple-element.35), channel_id=1, source_target_pairs={{0,12},{1,13},{2,14},{3,15},{4,0},{5,1},{6,2},{7,3},{8,4},{9,5},{1... | collective-permute-start | bytes 1179656 | tf_op jit(solution)/shard_map/ppermute | solution.py:39
  38.9 3.9 %multiply_next.1.acc_ref = f32[256,1536]{1,0:T(8,128)S(1)} custom-call(f32[768,256]{1,0:T(8,128)S(1)} %collective-permute-done.4.up_ref.la_ref, f32[9216,128]{1,0:T(8,128)S(1)} %get-tuple-element.37.sa_ref, f32[768,256]{1,0:T(8,128)S(1)} %collective-permute-done.5.down_ref.lb_ref, f32[9216,128]{1,0:T(8,128)S(1)} %get-tuple-element.38.sb_ref, ...), custom_call_target="tpu_custom_call" | custom-call | flops 1811939328 | bytes 6000000 | tf_op jit(solution)/shard_map/multiply_next/pallas_call | solution.py:122
  44.2 2.9 %multiply_last.1 = (f32[4,6,2,16,256]{4,3,2,1,0:T(8,128)S(1)}, f32[4,6,2,16,256]{4,3,2,1,0:T(8,128)S(1)}) custom-call(f32[384,256]{1,0:T(8,128)S(1)} %collective-permute-done.7.la_ref, f32[384,256]{1,0:T(8,128)S(1)} %collective-permute-done.8.lb_ref, f32[9216,128]{1,0:T(8,128)S(1)} %get-tuple-element.36.s_ref, f32[256,1536]{1,0:T(8,128)S(1)} %multiply_next.1.acc_ref, ...), custom_call_target="tpu_custom_call" | custom-call | flops 1811939328 | bytes 6000000 | tf_op jit(solution)/shard_map/multiply_last/pallas_call | solution.py:122
  47.1 4.3 %collective-permute-start.10 = (f32[4,6,2,16,256]{4,3,2,1,0:T(8,128)S(1)}, f32[4,6,2,16,256]{4,3,2,1,0:T(8,128)S(1)}, u32[]{:S(2)}, u32[]{:S(2)}) collective-permute-start(f32[4,6,2,16,256]{4,3,2,1,0:T(8,128)S(1)} %get-tuple-element.41), channel_id=1, source_target_pairs={{0,16},{1,17},{2,18},{3,19},{4,20},{5,21},{6,22},{7,23},{8,24},{9,... | collective-permute-start | bytes 2359304 | tf_op jit(solution)/shard_map/ppermute | solution.py:39
  51.4 1.9 %collective-permute-done.10.rows_in = f32[4,6,2,16,256]{4,3,2,1,0:T(8,128)S(1)} collective-permute-done((f32[4,6,2,16,256]{4,3,2,1,0:T(8,128)S(1)}, f32[4,6,2,16,256]{4,3,2,1,0:T(8,128)S(1)}, u32[]{:S(2)}, u32[]{:S(2)}) %collective-permute-start.10) | collective-permute-done | bytes 786464 | tf_op jit(solution)/shard_map/ppermute | solution.py:39
  53.5 7.8 %collective-permute-done.11.rows_in = f32[2,6,2,16,256]{4,3,2,1,0:T(8,128)S(1)} collective-permute-done((f32[2,6,2,16,256]{4,3,2,1,0:T(8,128)S(1)}, f32[2,6,2,16,256]{4,3,2,1,0:T(8,128)S(1)}, u32[]{:S(2)}, u32[]{:S(2)}) %collective-permute-start.11) | collective-permute-done | bytes 393248 | tf_op jit(solution)/shard_map/ppermute | solution.py:39
  62.6 3.7 %collective-permute-done.12.rows_in = f32[6,2,16,256]{3,2,1,0:T(8,128)S(1)} collective-permute-done((f32[6,2,16,256]{3,2,1,0:T(8,128)S(1)}, f32[6,2,16,256]{3,2,1,0:T(8,128)S(1)}, u32[]{:S(2)}, u32[]{:S(2)}) %collective-permute-start.12) | collective-permute-done | bytes 196640 | tf_op jit(solution)/shard_map/ppermute | solution.py:39
  67.8 3.1 %finish_panel.1 = (f32[136,128]{1,0:T(8,128)S(1)}, f32[136,128]{1,0:T(8,128)S(1)}) custom-call(f32[6,16,256]{2,1,0:T(8,128)S(1)} %get-tuple-element.46.keep_ref.first_ref, f32[6,16,256]{2,1,0:T(8,128)S(1)} %get-tuple-element.47.second_ref, f32[6,16,256]{2,1,0:T(8,128)S(1)} %get-tuple-element.33.__.l_first_ref, ...), custom_call_target="tpu_custom_call" | custom-call | flops 1207959552 | bytes 4000000 | tf_op jit(solution)/shard_map/finish_panel/pallas_call | solution.py:122
  70.9 2.7 %collective-permute-start.15 = (f32[136,128]{1,0:T(8,128)S(1)}, f32[136,128]{1,0:T(8,128)S(1)}, u32[]{:S(2)}, u32[]{:S(2)}) collective-permute-start(f32[136,128]{1,0:T(8,128)S(1)} %get-tuple-element.51), channel_id=1, source_target_pairs={{0,16},{1,17},{2,18},{3,19},{4,20},{5,21},{6,22},{7,23},{8,24},{9,... | collective-permute-start | bytes 208904 | tf_op jit(solution)/shard_map/ppermute | solution.py:39
  77.3 4.8 %collective-permute-start.14 = (f32[12,16,256]{2,1,0:T(8,128)S(1)}, f32[12,16,256]{2,1,0:T(8,128)S(1)}, u32[]{:S(2)}, u32[]{:S(2)}) collective-permute-start(f32[12,16,256]{2,1,0:T(8,128)S(1)} %join_rows.1._), channel_id=1, source_target_pairs={{0,0},{1,17},{2,34},{3,51},{4,68},{5,85},{6,102},{7,119},{8,8},{9,... | collective-permute-start | bytes 589832 | tf_op jit(solution)/shard_map/ppermute | solution.py:39
  84.9 2.3 %collective-permute-done.21.beyond = f32[136,128]{1,0:T(8,128)S(1)} collective-permute-done((f32[136,128]{1,0:T(8,128)S(1)}, f32[136,128]{1,0:T(8,128)S(1)}, u32[]{:S(2)}, u32[]{:S(2)}) %collective-permute-start.21) | collective-permute-done | bytes 69664 | tf_op jit(solution)/shard_map/ppermute | solution.py:39
  88.5 2.0 %collective-permute-start.24 = (f32[136,128]{1,0:T(8,128)S(1)}, f32[136,128]{1,0:T(8,128)S(1)}, u32[]{:S(2)}, u32[]{:S(2)}) collective-permute-start(f32[136,128]{1,0:T(8,128)S(1)} %add_four.4.part), channel_id=1, source_target_pairs={{0,8},{1,9},{2,10},{3,11},{4,12},{5,13},{6,14},{7,15},{8,0},{9,1},... | collective-permute-start | bytes 208904 | tf_op jit(solution)/shard_map/ppermute | solution.py:39
  91.2 2.3 %collective-permute-done.24.beyond = f32[136,128]{1,0:T(8,128)S(1)} collective-permute-done((f32[136,128]{1,0:T(8,128)S(1)}, f32[136,128]{1,0:T(8,128)S(1)}, u32[]{:S(2)}, u32[]{:S(2)}) %collective-permute-start.24) | collective-permute-done | bytes 69664 | tf_op jit(solution)/shard_map/ppermute | solution.py:39
  94.8 8.5 %collective-permute-start.25 = (f32[136,128]{1,0:T(8,128)S(1)}, f32[136,128]{1,0:T(8,128)S(1)}, u32[]{:S(2)}, u32[]{:S(2)}) collective-permute-start(f32[136,128]{1,0:T(8,128)S(1)} %add_four.5.part), channel_id=1, source_target_pairs={{0,16},{1,17},{2,18},{3,19},{4,20},{5,21},{6,22},{7,23},{8,24},{9,... | collective-permute-start | bytes 208904 | tf_op jit(solution)/shard_map/ppermute | solution.py:39
  (55 shorter events, 18.5 us)
Async XLA Ops:
  1.6 6.4 %collective-permute-start.1 = (f32[192,256]{1,0:T(8,128)S(1)}, f32[192,256]{1,0:T(8,128)S(1)}, u32[]{:S(2)}, u32[]{:S(2)}) collective-permute-start(f32[192,256]{1,0:T(8,128)S(1)} %order_rows.1.own_ref), channel_id=1, source_target_pairs={{0,3},{1,0},{2,1},{3,2},{4,7},{5,4},{6,5},{7,6},{8,11},{9,8},{10,9... | collective-permute-start | bytes 589832 | tf_op jit(solution)/shard_map/ppermute | solution.py:39
  5.4 6.0 %collective-permute-start = (f32[192,256]{1,0:T(8,128)S(1)}, f32[192,256]{1,0:T(8,128)S(1)}, u32[]{:S(2)}, u32[]{:S(2)}) collective-permute-start(f32[192,256]{1,0:T(8,128)S(1)} %order_rows.1.own_ref), channel_id=1, source_target_pairs={{0,1},{1,2},{2,3},{3,0},{4,5},{5,6},{6,7},{7,4},{8,9},{9,10},{10,1... | collective-permute-start | bytes 589832 | tf_op jit(solution)/shard_map/ppermute | solution.py:39
  8.1 7.7 %collective-permute-start.3 = (f32[96,256]{1,0:T(8,128)S(1)}, f32[96,256]{1,0:T(8,128)S(1)}, u32[]{:S(2)}, u32[]{:S(2)}) collective-permute-start(f32[96,256]{1,0:T(8,128)S(1)} %slice.9), channel_id=1, source_target_pairs={{0,3},{1,0},{2,1},{3,2},{4,7},{5,4},{6,5},{7,6},{8,11},{9,8},{10,9... | collective-permute-start | bytes 294920 | tf_op jit(solution)/shard_map/ppermute | solution.py:39
  11.5 4.7 %collective-permute-start.2 = (f32[96,256]{1,0:T(8,128)S(1)}, f32[96,256]{1,0:T(8,128)S(1)}, u32[]{:S(2)}, u32[]{:S(2)}) collective-permute-start(f32[96,256]{1,0:T(8,128)S(1)} %slice.8), channel_id=1, source_target_pairs={{0,1},{1,2},{2,3},{3,0},{4,5},{5,6},{6,7},{7,4},{8,9},{9,10},{10,1... | collective-permute-start | bytes 294920 | tf_op jit(solution)/shard_map/ppermute | solution.py:39
  16.3 16.1 %collective-permute-start.5 = (f32[768,256]{1,0:T(8,128)S(1)}, f32[768,256]{1,0:T(8,128)S(1)}, u32[]{:S(2)}, u32[]{:S(2)}) collective-permute-start(f32[768,256]{1,0:T(8,128)S(1)} %join_group.1.l_ref._), channel_id=1, source_target_pairs={{0,12},{1,13},{2,14},{3,15},{4,0},{5,1},{6,2},{7,3},{8,4},{9,5},{1... | collective-permute-start | bytes 2359304 | tf_op jit(solution)/shard_map/ppermute | solution.py:39
  19.2 16.3 %collective-permute-start.4 = (f32[768,256]{1,0:T(8,128)S(1)}, f32[768,256]{1,0:T(8,128)S(1)}, u32[]{:S(2)}, u32[]{:S(2)}) collective-permute-start(f32[768,256]{1,0:T(8,128)S(1)} %join_group.1.l_ref._), channel_id=1, source_target_pairs={{0,4},{1,5},{2,6},{3,7},{4,8},{5,9},{6,10},{7,11},{8,12},{9,13},{1... | collective-permute-start | bytes 2359304 | tf_op jit(solution)/shard_map/ppermute | solution.py:39
  19.2 13.1 %collective-permute-start.6 = (f32[12,16,256]{2,1,0:T(8,128)S(1)}, f32[12,16,256]{2,1,0:T(8,128)S(1)}, u32[]{:S(2)}, u32[]{:S(2)}) collective-permute-start(f32[12,16,256]{2,1,0:T(8,128)S(1)} %bitcast.12), channel_id=1, source_target_pairs={{0,0},{1,16},{2,32},{3,48},{4,64},{5,80},{6,96},{7,112},{8,8},{9,2... | collective-permute-start | bytes 589832 | tf_op jit(solution)/shard_map/ppermute | solution.py:39
  35.5 8.7 %collective-permute-start.7 = (f32[384,256]{1,0:T(8,128)S(1)}, f32[384,256]{1,0:T(8,128)S(1)}, u32[]{:S(2)}, u32[]{:S(2)}) collective-permute-start(f32[384,256]{1,0:T(8,128)S(1)} %get-tuple-element.34), channel_id=1, source_target_pairs={{0,4},{1,5},{2,6},{3,7},{4,8},{5,9},{6,10},{7,11},{8,12},{9,13},{1... | collective-permute-start | bytes 1179656 | tf_op jit(solution)/shard_map/ppermute | solution.py:39
  35.6 8.7 %collective-permute-start.8 = (f32[384,256]{1,0:T(8,128)S(1)}, f32[384,256]{1,0:T(8,128)S(1)}, u32[]{:S(2)}, u32[]{:S(2)}) collective-permute-start(f32[384,256]{1,0:T(8,128)S(1)} %get-tuple-element.35), channel_id=1, source_target_pairs={{0,12},{1,13},{2,14},{3,15},{4,0},{5,1},{6,2},{7,3},{8,4},{9,5},{1... | collective-permute-start | bytes 1179656 | tf_op jit(solution)/shard_map/ppermute | solution.py:39
  38.2 6.0 %collective-permute-start.9 = (f32[6,16,256]{2,1,0:T(8,128)S(1)}, f32[6,16,256]{2,1,0:T(8,128)S(1)}, u32[]{:S(2)}, u32[]{:S(2)}) collective-permute-start(f32[6,16,256]{2,1,0:T(8,128)S(1)} %get-tuple-element.39), channel_id=1, source_target_pairs={{0,8},{1,9},{2,10},{3,11},{4,12},{5,13},{6,14},{7,15},{8,0},{9,1},... | collective-permute-start | bytes 294920 | tf_op jit(solution)/shard_map/ppermute | solution.py:39
  47.1 6.2 %collective-permute-start.10 = (f32[4,6,2,16,256]{4,3,2,1,0:T(8,128)S(1)}, f32[4,6,2,16,256]{4,3,2,1,0:T(8,128)S(1)}, u32[]{:S(2)}, u32[]{:S(2)}) collective-permute-start(f32[4,6,2,16,256]{4,3,2,1,0:T(8,128)S(1)} %get-tuple-element.41), channel_id=1, source_target_pairs={{0,16},{1,17},{2,18},{3,19},{4,20},{5,21},{6,22},{7,23},{8,24},{9,... | collective-permute-start | bytes 2359304 | tf_op jit(solution)/shard_map/ppermute | solution.py:39
  53.4 7.9 %collective-permute-start.11 = (f32[2,6,2,16,256]{4,3,2,1,0:T(8,128)S(1)}, f32[2,6,2,16,256]{4,3,2,1,0:T(8,128)S(1)}, u32[]{:S(2)}, u32[]{:S(2)}) collective-permute-start(f32[2,6,2,16,256]{4,3,2,1,0:T(8,128)S(1)} %get-tuple-element.43), channel_id=1, source_target_pairs={{0,32},{1,33},{2,34},{3,35},{4,36},{5,37},{6,38},{7,39},{8,40},{9,... | collective-permute-start | bytes 1179656 | tf_op jit(solution)/shard_map/ppermute | solution.py:39
  61.4 4.9 %collective-permute-start.12 = (f32[6,2,16,256]{3,2,1,0:T(8,128)S(1)}, f32[6,2,16,256]{3,2,1,0:T(8,128)S(1)}, u32[]{:S(2)}, u32[]{:S(2)}) collective-permute-start(f32[6,2,16,256]{3,2,1,0:T(8,128)S(1)} %get-tuple-element.45), channel_id=1, source_target_pairs={{0,96},{1,97},{2,98},{3,99},{4,100},{5,101},{6,102},{7,103},{8,104... | collective-permute-start | bytes 589832 | tf_op jit(solution)/shard_map/ppermute | solution.py:39
  66.3 11.0 %collective-permute-start.13 = (f32[6,16,256]{2,1,0:T(8,128)S(1)}, f32[6,16,256]{2,1,0:T(8,128)S(1)}, u32[]{:S(2)}, u32[]{:S(2)}) collective-permute-start(f32[6,16,256]{2,1,0:T(8,128)S(1)} %get-tuple-element.47.second_ref), channel_id=1, source_target_pairs={{0,8},{1,9},{2,10},{3,11},{4,12},{5,13},{6,14},{7,15},{8,0},{9,1},... | collective-permute-start | bytes 294920 | tf_op jit(solution)/shard_map/ppermute | solution.py:39
  74.6 7.6 %collective-permute-start.18 = (f32[136,128]{1,0:T(8,128)S(1)}, f32[136,128]{1,0:T(8,128)S(1)}, u32[]{:S(2)}, u32[]{:S(2)}) collective-permute-start(f32[136,128]{1,0:T(8,128)S(1)} %add_two.1.part), channel_id=1, source_target_pairs={{0,64},{1,65},{2,66},{3,67},{4,68},{5,69},{6,70},{7,71},{8,72},{9,... | collective-permute-start | bytes 208904 | tf_op jit(solution)/shard_map/ppermute | solution.py:39
  74.7 7.5 %collective-permute-start.17 = (f32[136,128]{1,0:T(8,128)S(1)}, f32[136,128]{1,0:T(8,128)S(1)}, u32[]{:S(2)}, u32[]{:S(2)}) collective-permute-start(f32[136,128]{1,0:T(8,128)S(1)} %add_two.1.part), channel_id=1, source_target_pairs={{0,96},{1,97},{2,98},{3,99},{4,100},{5,101},{6,102},{7,103},{8,104... | collective-permute-start | bytes 208904 | tf_op jit(solution)/shard_map/ppermute | solution.py:39
  75.5 6.6 %collective-permute-start.16 = (f32[136,128]{1,0:T(8,128)S(1)}, f32[136,128]{1,0:T(8,128)S(1)}, u32[]{:S(2)}, u32[]{:S(2)}) collective-permute-start(f32[136,128]{1,0:T(8,128)S(1)} %add_two.1.part), channel_id=1, source_target_pairs={{0,32},{1,33},{2,34},{3,35},{4,36},{5,37},{6,38},{7,39},{8,40},{9,... | collective-permute-start | bytes 208904 | tf_op jit(solution)/shard_map/ppermute | solution.py:39
  77.3 17.5 %collective-permute-start.14 = (f32[12,16,256]{2,1,0:T(8,128)S(1)}, f32[12,16,256]{2,1,0:T(8,128)S(1)}, u32[]{:S(2)}, u32[]{:S(2)}) collective-permute-start(f32[12,16,256]{2,1,0:T(8,128)S(1)} %join_rows.1._), channel_id=1, source_target_pairs={{0,0},{1,17},{2,34},{3,51},{4,68},{5,85},{6,102},{7,119},{8,8},{9,... | collective-permute-start | bytes 589832 | tf_op jit(solution)/shard_map/ppermute | solution.py:39
  82.2 5.0 %collective-permute-start.21 = (f32[136,128]{1,0:T(8,128)S(1)}, f32[136,128]{1,0:T(8,128)S(1)}, u32[]{:S(2)}, u32[]{:S(2)}) collective-permute-start(f32[136,128]{1,0:T(8,128)S(1)} %add_four.3.part), channel_id=1, source_target_pairs={{0,2},{1,3},{2,0},{3,1},{4,6},{5,7},{6,4},{7,5},{8,10},{9,11},{10,... | collective-permute-start | bytes 208904 | tf_op jit(solution)/shard_map/ppermute | solution.py:39
  83.8 4.7 %collective-permute-start.20 = (f32[136,128]{1,0:T(8,128)S(1)}, f32[136,128]{1,0:T(8,128)S(1)}, u32[]{:S(2)}, u32[]{:S(2)}) collective-permute-start(f32[136,128]{1,0:T(8,128)S(1)} %add_four.3.part), channel_id=1, source_target_pairs={{0,3},{1,2},{2,1},{3,0},{4,7},{5,6},{6,5},{7,4},{8,11},{9,10},{10,... | collective-permute-start | bytes 208904 | tf_op jit(solution)/shard_map/ppermute | solution.py:39
  88.5 5.0 %collective-permute-start.24 = (f32[136,128]{1,0:T(8,128)S(1)}, f32[136,128]{1,0:T(8,128)S(1)}, u32[]{:S(2)}, u32[]{:S(2)}) collective-permute-start(f32[136,128]{1,0:T(8,128)S(1)} %add_four.4.part), channel_id=1, source_target_pairs={{0,8},{1,9},{2,10},{3,11},{4,12},{5,13},{6,14},{7,15},{8,0},{9,1},... | collective-permute-start | bytes 208904 | tf_op jit(solution)/shard_map/ppermute | solution.py:39
  90.4 4.4 %collective-permute-start.23 = (f32[136,128]{1,0:T(8,128)S(1)}, f32[136,128]{1,0:T(8,128)S(1)}, u32[]{:S(2)}, u32[]{:S(2)}) collective-permute-start(f32[136,128]{1,0:T(8,128)S(1)} %add_four.4.part), channel_id=1, source_target_pairs={{0,12},{1,13},{2,14},{3,15},{4,8},{5,9},{6,10},{7,11},{8,4},{9,5},... | collective-permute-start | bytes 208904 | tf_op jit(solution)/shard_map/ppermute | solution.py:39
  90.4 4.4 %collective-permute-start.22 = (f32[136,128]{1,0:T(8,128)S(1)}, f32[136,128]{1,0:T(8,128)S(1)}, u32[]{:S(2)}, u32[]{:S(2)}) collective-permute-start(f32[136,128]{1,0:T(8,128)S(1)} %add_four.4.part), channel_id=1, source_target_pairs={{0,4},{1,5},{2,6},{3,7},{4,0},{5,1},{6,2},{7,3},{8,12},{9,13},{10,... | collective-permute-start | bytes 208904 | tf_op jit(solution)/shard_map/ppermute | solution.py:39
  94.8 9.5 %collective-permute-start.25 = (f32[136,128]{1,0:T(8,128)S(1)}, f32[136,128]{1,0:T(8,128)S(1)}, u32[]{:S(2)}, u32[]{:S(2)}) collective-permute-start(f32[136,128]{1,0:T(8,128)S(1)} %add_four.5.part), channel_id=1, source_target_pairs={{0,16},{1,17},{2,18},{3,19},{4,20},{5,21},{6,22},{7,23},{8,24},{9,... | collective-permute-start | bytes 208904 | tf_op jit(solution)/shard_map/ppermute | solution.py:39
  (4 other events, 16.1 us)

commit v3 on v2

--- a/solution.py
+++ b/solution.py
@@ -139,28 +139,21 @@
     return jax.ShapeDtypeStruct(shape, F32)
 
 
-def order_rows(l_ref, piece_ref):
-    piece_ref[...] = jnp.swapaxes(l_ref[...], 0, 1).reshape(PIECE, NB)
-
-
-def split_tiles(rows_ref, _, __, keep_ref, send_ref):
+def split_tiles(rows_ref, _, keep_ref, send_ref):
     high = place()[2] // 2
     for v in range(TPC):
         keep_ref[v] = rows_ref[2 * v + high]
         send_ref[v] = rows_ref[2 * v + 1 - high]
 
 
-def join_group(own_ref, up_ref, down_ref, far_up_ref, far_down_ref, _, out_ref):
-    out_ref[:PIECE] = own_ref[...]
-    out_ref[PIECE : 2 * PIECE] = up_ref[...]
-    out_ref[2 * PIECE : 3 * PIECE] = down_ref[...]
-    out_ref[3 * PIECE : 3 * PIECE + PIECE // 2] = far_up_ref[...]
-    out_ref[3 * PIECE + PIECE // 2 :] = far_down_ref[...]
-
-
-def take_halves(up_ref, down_ref, _, __, first_ref, second_ref):
-    first_ref[...] = up_ref[: GROUP // 2]
-    second_ref[...] = down_ref[GROUP // 2 :]
+def join_group(own_ref, up_ref, down_ref, far_ref, _, first_ref, second_ref):
+    def ordered(ref):
+        return jnp.swapaxes(ref[...], 0, 1).reshape(PIECE, NB)
+
+    first_ref[:PIECE] = ordered(own_ref)
+    first_ref[PIECE:] = ordered(up_ref)
+    second_ref[:PIECE] = ordered(down_ref)
+    second_ref[PIECE:] = ordered(far_ref)
 
 
 def fetch(step, s_ref, held_ref, sem):
@@ -186,7 +179,7 @@
 
 
 def invert_blocks(
-    s_ref, l_ref, lbar_ref, own_ref, mine_ref, _, __,
+    s_ref, l_ref, lbar_ref, own_ref, mine_ref,
     first_s, second_s, strict_ref, inverse_ref, l_out, lbar_out, own_out, mine_out, sem, small,
 ):
     panel = pltpu.make_async_copy(l_ref, l_out, small.at[0])
@@ -213,24 +206,16 @@
         copy.wait()
 
 
-def invert_rest(s_ref, strict_ref, blocks_ref, l_ref, _, third_s, fourth_s, inverse_ref, sem):
-    copies = fetch(1, s_ref, third_s, sem.at[0]) + fetch(2, s_ref, fourth_s, sem.at[1])
-
-    @pl.when(place()[0] >= 0)
-    def _():
-        row, col = grids()
-        strict = strict_ref[...]
-        inverse = blocks_ref[...]
-        size = 16
-        while size < NB:
-            beside = (row // (2 * size) == col // (2 * size)) & (row // size != col // size)
-            inverse = inverse - dot6(inverse, dot6(jnp.where(beside, strict, 0.0), inverse))
-            size *= 2
-        by_col = 1.0 / jnp.sum(jnp.where(row == col, l_ref[...], 0.0), axis=0, keepdims=True)
-        inverse_ref[...] = inverse * by_col
-
-    for copy in copies:
-        copy.wait()
+def invert_rest(strict_ref, blocks_ref, l_ref, _, inverse_ref):
+    row, col = grids()
+    strict = strict_ref[...]
+    inverse = blocks_ref[...]
+    size = 16
+    while size < NB:
+        beside = (row // (2 * size) == col // (2 * size)) & (row // size != col // size)
+        inverse = inverse - dot6(inverse, dot6(jnp.where(beside, strict, 0.0), inverse))
+        size *= 2
+    inverse_ref[...] = inverse * (1.0 / jnp.sum(jnp.where(row == col, l_ref[...], 0.0), axis=0, keepdims=True))
 
 
 def product(lh, ll, s_ref, j):
@@ -239,23 +224,45 @@
     return dot3(lh, ll, *split(lines))
 
 
-def multiply_first(l_ref, s_ref, out_ref):
-    lh, ll = split(l_ref[...].T)
-    for j in range(3):
-        out_ref[:, j * 512 : (j + 1) * 512] = product(lh, ll, s_ref, j)
-
-
-def multiply_next(la_ref, sa_ref, lb_ref, sb_ref, acc_ref, out_ref):
-    ah, al = split(la_ref[...].T)
-    bh, bl = split(lb_ref[...].T)
+def beside_copies(copies, compute):
+    pl.when(place()[0] >= 0)(compute)
+    for copy in copies:
+        copy.wait()
+
+
+def parts(first_ref, second_ref):
+    return split(jnp.concatenate([first_ref[...], second_ref[...]], axis=0).T)
+
+
+def multiply_first(la_ref, lb_ref, s_ref, s_all_ref, out_ref, next_ref, sem):
+    def compute():
+        lh, ll = parts(la_ref, lb_ref)
+        for j in range(3):
+            out_ref[:, j * 512 : (j + 1) * 512] = product(lh, ll, s_ref, j)
+
+    beside_copies(fetch(1, s_all_ref, next_ref, sem), compute)
+
+
+def multiply_up(la_ref, lb_ref, s_ref, acc_ref, s_all_ref, out_ref, next_ref, sem):
+    def compute():
+        lh, ll = parts(la_ref, lb_ref)
+        for j in range(3):
+            at = slice(j * 512, (j + 1) * 512)
+            out_ref[:, at] = acc_ref[:, at] + product(lh, ll, s_ref, j)
+
+    beside_copies(fetch(2, s_all_ref, next_ref, sem), compute)
+
+
+def multiply_down(la_ref, lb_ref, s_ref, acc_ref, _, out_ref):
+    lh, ll = parts(la_ref, lb_ref)
     for j in range(3):
         at = slice(j * 512, (j + 1) * 512)
-        out_ref[:, at] = acc_ref[:, at] + product(ah, al, sa_ref, j) + product(bh, bl, sb_ref, j)
-
-
-def multiply_last(la_ref, lb_ref, s_ref, acc_ref, _, keep_ref, send_ref):
+        out_ref[:, at] = acc_ref[:, at] + product(lh, ll, s_ref, j)
+
+
+def multiply_last(la_ref, lb_ref, s_ref, acc_ref, keep_ref, send_ref):
     x, c, z, y = place()
-    lh, ll = split(jnp.concatenate([la_ref[...], lb_ref[...]], axis=0).T)
+    lh, ll = parts(la_ref, lb_ref)
     turn = 2 * (z % 2) + y // 2
     for j in range(3):
         at = slice(j * 512, (j + 1) * 512)
@@ -281,7 +288,7 @@
     send_ref[...] = rows[2:] + rows_in[2:]
 
 
-def add_pairs(rows, rows_in, keep_ref, send_ref):
+def add_pairs(rows, rows_in, _, __, keep_ref, send_ref):
     keep_ref[...] = rows[0] + rows_in[0]
     send_ref[...] = rows[1] + rows_in[1]
 
@@ -310,7 +317,9 @@
     out_ref[...] = lbar_ref[...] * share - jnp.where(row >= col, gram, 0.0)
 
 
-def finish_panel(first_ref, second_ref, l_first_ref, l_second_ref, l_ref, inv_ref, base_ref, keep_ref, send_ref):
+def finish_panel(
+    first_ref, second_ref, l_first_ref, l_second_ref, l_ref, inv_ref, base_ref, keep_ref, send_ref, second_out
+):
     c = place()[1]
     row, col = grids()
     half = PIECE // 2
@@ -332,6 +341,7 @@
     send_ref[:n] = jnp.where(c == 0, mixed, lower)
     keep_ref[n:] = jnp.broadcast_to(diagonal, (8, n))
     send_ref[n:] = jnp.broadcast_to(diagonal, (8, n))
+    second_out[...] = second_ref[...]
 
 
 def add_two(part, other, out_ref):
@@ -366,80 +376,98 @@
     lines = kept(4 * SLAB, 128)
     square = kept(NB, NB)
 
-    (piece,) = call(order_rows, [mine], [free(PIECE, NB)], 4, size=400_000)
-    up = permute(piece, first_axis(1))
-    down = permute(piece, first_axis(-1))
+    up = permute(mine, first_axis(1))
+    down = permute(mine, first_axis(-1))
+    far = permute(mine, first_axis(2))
     s0, s3, strict, blocks, l_kept, lbar_kept, own_kept, mine_kept = call(
         invert_blocks,
-        [s_lines, l_panel, lbar_panel, own, mine, up, down],
+        [s_lines, l_panel, lbar_panel, own, mine],
         [lines, lines, square, square, square, square, kept(UR, 16, NB), kept(UR, 16, NB)],
         4,
         flops=6 * 12 * NB**3,
         size=10_000_000,
         scratch=[dma((2, 4)), dma((4,))],
-        specs=[HBM] * 5 + [ANY] * 2,
-    )
-    far_up = permute(up[: PIECE // 2], first_axis(1))
-    far_down = permute(down[PIECE // 2 :], first_axis(-1))
+        specs=[HBM] * 5,
+    )
     tile = kept(TPC, 16, NB)
     rows = permute(mine, to_tiles)
-    (group,) = call(
+    first, second = call(
         join_group,
-        [piece, up, down, far_up, far_down, blocks],
-        [free(GROUP, NB)],
+        [mine_kept, up, down, far, blocks],
+        [free(GROUP // 2, NB)] * 2,
         4,
         size=1_600_000,
-        specs=[VMEM] * 5 + [ANY],
-    )
-    group_up = permute(group, second_axis(1))
-    group_down = permute(group, second_axis(-1))
-    s1, s2, inverse = call(
-        invert_rest,
-        [s_lines, strict, blocks, l_kept, group],
-        [lines, lines, square],
-        4,
-        flops=8 * 12 * NB**3,
-        size=10_000_000,
-        scratch=[dma((2, 4))],
-        specs=[HBM] + [VMEM] * 3 + [ANY],
-    )
+        specs=[VMEM] * 4 + [ANY],
+    )
+    up_first = permute(first, second_axis(1))
+    down_second = permute(second, second_axis(-1))
+    up_second = permute(second, second_axis(1))
+    down_first = permute(first, second_axis(-1))
+    far_first = permute(up_first, second_axis(1))
+    far_second = permute(down_second, second_axis(-1))
     work = dict(flops=6 * GROUP * COLS * NB, size=6_000_000)
     wide = kept(NB, COLS)
-    (total,) = call(multiply_first, [group, s0], [wide], 8, **work)
-    l_keep, l_send = call(
-        split_tiles, [rows, inverse, total], [tile, tile], 4, size=800_000, specs=[VMEM, ANY, ANY]
-    )
+    total, s1 = call(
+        multiply_first,
+        [first, second, s0, s_lines],
+        [wide, lines],
+        8,
+        scratch=[dma((4,))],
+        specs=[VMEM] * 3 + [HBM],
+        **work,
+    )
+    l_keep, l_send = call(split_tiles, [rows, total], [tile, tile], 4, size=800_000, specs=[VMEM, ANY])
     l_other = permute(l_send, opposite_half)
-    pass_up, pass_down = call(
-        take_halves,
-        [group_up, group_down, total, l_keep],
-        [free(GROUP // 2, NB)] * 2,
-        4,
-        size=1_000_000,
-        specs=[VMEM, VMEM, ANY, ANY],
-    )
-    far_a = permute(pass_up, second_axis(1))
-    far_b = permute(pass_down, second_axis(-1))
-    (total,) = call(multiply_next, [group_up, s3, group_down, s1, total], [wide], 8, **work)
+    total, s2 = call(
+        multiply_up,
+        [up_first, up_second, s3, total, s_lines],
+        [wide, lines],
+        8,
+        scratch=[dma((4,))],
+        specs=[VMEM] * 4 + [HBM],
+        **work,
+    )
+    (total,) = call(
+        multiply_down,
+        [down_first, down_second, s1, total, rows],
+        [wide],
+        8,
+        specs=[VMEM] * 4 + [ANY],
+        **work,
+    )
     share4 = kept(4, TPC, 2, 16, NB)
-    keep, send = call(
-        multiply_last, [far_a, far_b, s2, total, l_other], [share4, share4], 8, specs=[VMEM] * 4 + [ANY], **work
-    )
+    keep, send = call(multiply_last, [far_first, far_second, s2, total], [share4, share4], 8, **work)
 
     share2 = kept(2, TPC, 2, 16, NB)
     share1 = kept(TPC, 2, 16, NB)
+    keep, send = call(add_cores, [keep, permute(send, other_core)], [share2, share2], 6, size=2_000_000)
+    (inverse,) = call(
+        invert_rest,
+        [strict, blocks, l_kept, keep],
+        [square],
+        6,
+        flops=8 * 12 * NB**3,
+        size=6_000_000,
+        specs=[VMEM] * 3 + [ANY],
+    )
+    keep, send = call(
+        add_pairs,
+        [keep, permute(send, halving(0)), inverse, l_other],
+        [share1, share1],
+        6,
+        size=1_000_000,
+        specs=[VMEM] * 2 + [ANY] * 2,
+    )
     (base,) = call(
         functools.partial(start_panel, share), [own_kept, mine_kept, inverse, lbar_kept], [square], 6,
         flops=2 * 12 * NB**3, size=4_000_000,
     )
-    keep, send = call(add_cores, [keep, permute(send, other_core)], [share2, share2], 6, size=2_000_000)
-    keep, send = call(add_pairs, [keep, permute(send, halving(0))], [share1, share1], 6, size=1_000_000)
     keep, send = call(add_rows, [keep, permute(send, halving(1))], [tile, tile], 6, size=1_000_000)
     half = kept(NB // 2 + 8, NB // 2)
-    part, other = call(
+    part, other, send = call(
         finish_panel,
         [keep, send, l_keep, l_other, l_kept, inverse, base],
-        [half, half],
+        [half, half, tile],
         8,
         flops=6 * 12 * NB**3,
         size=4_000_000,

time: 105 us -> 93.8 us (0.89)
  waiting for transfers between devices: 32.4 us -> 18.8 us
  starting transfers between devices: 46.9 us -> 49.2 us
    ppermute x26 -> x27, waiting for transfers between devices: 32.4 us -> 18.8 us  [permute(): return lax.ppermute(value, AXES, pairs(target))]
    ppermute x26 -> x27, starting transfers between devices: 46.9 us -> 49.2 us  [permute(): return lax.ppermute(value, AXES, pairs(target))]
    pallas_call x21 -> x20, Pallas kernels: 24 us -> 24.8 us  [call(): pl.pallas_call(kernel, in_specs=specs or [VMEM] * len(inputs), out_specs=...]
  transfers between devices with their start and end apart: 26 -> 27, of which waited for: 14 -> 13; matrix products, arithmetic and copies ran while one was open for 0% -> 0% of each run, Pallas kernels for 19% -> 19%
where the time goes in v3:
time: 93.8 us; the launch traced here: 93.7 us
  starting transfers between devices  49.2 us (52%)
  Pallas kernels  24.8 us (26%)
  waiting for transfers between devices  18.8 us (20%)
    ppermute x27, starting transfers between devices, permute(): return lax.ppermute(value, AXES, pairs(target))  49.2 us
    pallas_call x20, Pallas kernels, call(): pl.pallas_call(kernel, in_specs=specs or [VMEM] * len(inputs), out_specs=...  24.8 us
    ppermute x27, waiting for transfers between devices, permute(): return lax.ppermute(value, AXES, pairs(target))  18.8 us
  transfers between devices with their start and end apart: 27, of which 13 were waited for; matrix products, arithmetic and copies ran while one was open for 0% of the time, Pallas kernels for 19%

profile of v3, /device:TPU:7, one launch (start us, length us, event | category | flops | bytes accessed | tf_op | source)
XLA Modules:
  0.0 93.7 jit_solution(3567281924582991720)
XLA Ops:
  0.6 1.7 %collective-permute-start = (f32[12,16,256]{2,1,0:T(8,128)}, f32[12,16,256]{2,1,0:T(8,128)S(1)}, u32[]{:S(2)}, u32[]{:S(2)}) collective-permute-start(f32[12,16,256]{2,1,0:T(8,128)} %bitcast.14), channel_id=1, source_target_pairs={{0,1},{1,2},{2,3},{3,0},{4,5},{5,6},{6,7},{7,4},{8,9},{9,10},{10,1... | collective-permute-start | bytes 589832 | tf_op jit(solution)/shard_map/ppermute | solution.py:39
  2.3 2.2 %collective-permute-start.1 = (f32[12,16,256]{2,1,0:T(8,128)}, f32[12,16,256]{2,1,0:T(8,128)S(1)}, u32[]{:S(2)}, u32[]{:S(2)}) collective-permute-start(f32[12,16,256]{2,1,0:T(8,128)} %bitcast.15), channel_id=1, source_target_pairs={{0,3},{1,0},{2,1},{3,2},{4,7},{5,4},{6,5},{7,6},{8,11},{9,8},{10,9... | collective-permute-start | bytes 589832 | tf_op jit(solution)/shard_map/ppermute | solution.py:39
  5.8 4.1 %invert_blocks.1 = (f32[9216,128]{1,0:T(8,128)S(1)}, f32[9216,128]{1,0:T(8,128)S(1)}, f32[256,256]{1,0:T(8,128)S(1)}, f32[256,256]{1,0:T(8,128)S(1)}, f32[256,25...) custom-call(f32[36864,128]{1,0:T(8,128)} %bitcast.10, ...), custom_call_target="tpu_custom_call" | custom-call | flops 1207959552 | bytes 10000000 | tf_op jit(solution)/shard_map/invert_blocks/pallas_call | solution.py:122
  12.5 1.7 %collective-permute-start.5 = (f32[384,256]{1,0:T(8,128)S(1)}, f32[384,256]{1,0:T(8,128)S(1)}, u32[]{:S(2)}, u32[]{:S(2)}) collective-permute-start(f32[384,256]{1,0:T(8,128)S(1)} %get-tuple-element.33.lb_ref), channel_id=1, source_target_pairs={{0,12},{1,13},{2,14},{3,15},{4,0},{5,1},{6,2},{7,3},{8,4},{9,5},{1... | collective-permute-start | bytes 1179656 | tf_op jit(solution)/shard_map/ppermute | solution.py:39
  14.2 2.7 %collective-permute-start.8 = (f32[384,256]{1,0:T(8,128)S(1)}, f32[384,256]{1,0:T(8,128)S(1)}, u32[]{:S(2)}, u32[]{:S(2)}) collective-permute-start(f32[384,256]{1,0:T(8,128)S(1)} %get-tuple-element.32.la_ref), channel_id=1, source_target_pairs={{0,12},{1,13},{2,14},{3,15},{4,0},{5,1},{6,2},{7,3},{8,4},{9,5},{1... | collective-permute-start | bytes 1179656 | tf_op jit(solution)/shard_map/ppermute | solution.py:39
  16.9 2.6 %collective-permute-start.9 = (f32[12,16,256]{2,1,0:T(8,128)S(1)}, f32[12,16,256]{2,1,0:T(8,128)S(1)}, u32[]{:S(2)}, u32[]{:S(2)}) collective-permute-start(f32[12,16,256]{2,1,0:T(8,128)S(1)} %bitcast.18), channel_id=1, source_target_pairs={{0,0},{1,16},{2,32},{3,48},{4,64},{5,80},{6,96},{7,112},{8,8},{9,2... | collective-permute-start | bytes 589832 | tf_op jit(solution)/shard_map/ppermute | solution.py:39
  19.7 2.1 %collective-permute-start.4 = (f32[384,256]{1,0:T(8,128)S(1)}, f32[384,256]{1,0:T(8,128)S(1)}, u32[]{:S(2)}, u32[]{:S(2)}) collective-permute-start(f32[384,256]{1,0:T(8,128)S(1)} %collective-permute-done.3.la_ref), channel_id=1, source_target_pairs={{0,4},{1,5},{2,6},{3,7},{4,8},{5,9},{6,10},{7,11},{8,12},{9,13},{1... | collective-permute-start | bytes 1179656 | tf_op jit(solution)/shard_map/ppermute | solution.py:39
  22.3 2.4 %multiply_first.1 = (f32[256,1536]{1,0:T(8,128)S(1)}, f32[9216,128]{1,0:T(8,128)S(1)}) custom-call(f32[384,256]{1,0:T(8,128)S(1)} %get-tuple-element.32.la_ref, f32[384,256]{1,0:T(8,128)S(1)} %get-tuple-element.33.lb_ref, f32[9216,128]{1,0:T(8,128)S(1)} %get-tuple-element.35.s_ref, f32[36864,128]{1,0:T(8,128)} %bitcast.11), custom_call_target="tpu_custom_call" | custom-call | flops 1811939328 | bytes 6000000 | tf_op jit(solution)/shard_map/multiply_first/pallas_call | solution.py:122
  24.7 2.4 %multiply_up.1 = (f32[256,1536]{1,0:T(8,128)S(1)}, f32[9216,128]{1,0:T(8,128)S(1)}) custom-call(f32[384,256]{1,0:T(8,128)S(1)} %collective-permute-done.3.la_ref, f32[384,256]{1,0:T(8,128)S(1)} %collective-permute-done.7.lb_ref, f32[9216,128]{1,0:T(8,128)S(1)} %get-tuple-element.34.s_ref, f32[256,1536]{1,0:T(8,128)S(1)} %get-tuple-element.36.acc_ref._, ...), custom_call_target="tpu_custom_call" | custom-call | flops 1811939328 | bytes 6000000 | tf_op jit(solution)/shard_map/multiply_up/pallas_call | solution.py:122
  28.3 2.1 %multiply_down.1.acc_ref = f32[256,1536]{1,0:T(8,128)S(1)} custom-call(f32[384,256]{1,0:T(8,128)S(1)} %collective-permute-done.8.la_ref, f32[384,256]{1,0:T(8,128)S(1)} %collective-permute-done.5.lb_ref, f32[9216,128]{1,0:T(8,128)S(1)} %get-tuple-element.38.s_ref, f32[256,1536]{1,0:T(8,128)S(1)} %get-tuple-element.39.acc_ref, ...), custom_call_target="tpu_custom_call" | custom-call | flops 1811939328 | bytes 6000000 | tf_op jit(solution)/shard_map/multiply_down/pallas_call | solution.py:122
  32.0 3.1 %multiply_last.1 = (f32[4,6,2,16,256]{4,3,2,1,0:T(8,128)S(1)}, f32[4,6,2,16,256]{4,3,2,1,0:T(8,128)S(1)}) custom-call(f32[384,256]{1,0:T(8,128)S(1)} %collective-permute-done.4.la_ref, f32[384,256]{1,0:T(8,128)S(1)} %collective-permute-done.6.lb_ref, f32[9216,128]{1,0:T(8,128)S(1)} %get-tuple-element.37.s_ref, f32[256,1536]{1,0:T(8,128)S(1)} %multiply_down.1.acc_ref), custom_call_target="tpu_custom_call" | custom-call | flops 1811939328 | bytes 6000000 | tf_op jit(solution)/shard_map/multiply_last/pallas_call | solution.py:122
  35.1 3.2 %collective-permute-start.10 = (f32[4,6,2,16,256]{4,3,2,1,0:T(8,128)S(1)}, f32[4,6,2,16,256]{4,3,2,1,0:T(8,128)S(1)}, u32[]{:S(2)}, u32[]{:S(2)}) collective-permute-start(f32[4,6,2,16,256]{4,3,2,1,0:T(8,128)S(1)} %get-tuple-element.41), channel_id=1, source_target_pairs={{0,16},{1,17},{2,18},{3,19},{4,20},{5,21},{6,22},{7,23},{8,24},{9,... | collective-permute-start | bytes 2359304 | tf_op jit(solution)/shard_map/ppermute | solution.py:39
  38.3 1.9 %collective-permute-done.10.rows_in = f32[4,6,2,16,256]{4,3,2,1,0:T(8,128)S(1)} collective-permute-done((f32[4,6,2,16,256]{4,3,2,1,0:T(8,128)S(1)}, f32[4,6,2,16,256]{4,3,2,1,0:T(8,128)S(1)}, u32[]{:S(2)}, u32[]{:S(2)}) %collective-permute-start.10) | collective-permute-done | bytes 786464 | tf_op jit(solution)/shard_map/ppermute | solution.py:39
  40.5 2.8 %collective-permute-start.12 = (f32[6,16,256]{2,1,0:T(8,128)S(1)}, f32[6,16,256]{2,1,0:T(8,128)S(1)}, u32[]{:S(2)}, u32[]{:S(2)}) collective-permute-start(f32[6,16,256]{2,1,0:T(8,128)S(1)} %get-tuple-element.46), channel_id=1, source_target_pairs={{0,8},{1,9},{2,10},{3,11},{4,12},{5,13},{6,14},{7,15},{8,0},{9,1},... | collective-permute-start | bytes 294920 | tf_op jit(solution)/shard_map/ppermute | solution.py:39
  43.2 4.3 %invert_rest.1._.inv_ref = f32[256,256]{1,0:T(8,128)S(1)} custom-call(f32[256,256]{1,0:T(8,128)S(1)} %get-tuple-element.44.strict_ref, f32[256,256]{1,0:T(8,128)S(1)} %get-tuple-element.31._.blocks_ref, f32[256,256]{1,0:T(8,128)S(1)} %get-tuple-element.45.l_ref, f32[2,6,2,16,256]{4,3,2,1,0:T(8,128)S(1)} %get-tuple-element.42._.rows), custom_call_target="tpu_custom_call" | custom-call | flops 1610612736 | bytes 6000000 | tf_op jit(solution)/shard_map/invert_rest/pallas_call | solution.py:122
  49.5 3.4 %collective-permute-done.13.rows_in = f32[6,2,16,256]{3,2,1,0:T(8,128)S(1)} collective-permute-done((f32[6,2,16,256]{3,2,1,0:T(8,128)S(1)}, f32[6,2,16,256]{3,2,1,0:T(8,128)S(1)}, u32[]{:S(2)}, u32[]{:S(2)}) %collective-permute-start.13) | collective-permute-done | bytes 196640 | tf_op jit(solution)/shard_map/ppermute | solution.py:39
  52.9 3.1 %finish_panel.1 = (f32[136,128]{1,0:T(8,128)S(1)}, f32[136,128]{1,0:T(8,128)S(1)}, f32[6,16,256]{2,1,0:T(8,128)S(1)}) custom-call(f32[6,16,256]{2,1,0:T(8,128)S(1)} %get-tuple-element.49.first_ref.keep_ref, f32[6,16,256]{2,1,0:T(8,128)S(1)} %get-tuple-element.50.second_ref, f32[6,16,256]{2,1,0:T(8,128)S(1)} %get-tuple-element.51.l_first_ref, ...), custom_call_target="tpu_custom_call" | custom-call | flops 1207959552 | bytes 4000000 | tf_op jit(solution)/shard_map/finish_panel/pallas_call | solution.py:122
  56.0 3.1 %collective-permute-start.14 = (f32[6,16,256]{2,1,0:T(8,128)S(1)}, f32[6,16,256]{2,1,0:T(8,128)S(1)}, u32[]{:S(2)}, u32[]{:S(2)}) collective-permute-start(f32[6,16,256]{2,1,0:T(8,128)S(1)} %get-tuple-element.53), channel_id=1, source_target_pairs={{0,8},{1,9},{2,10},{3,11},{4,12},{5,13},{6,14},{7,15},{8,0},{9,1},... | collective-permute-start | bytes 294920 | tf_op jit(solution)/shard_map/ppermute | solution.py:39
  59.1 2.7 %collective-permute-start.16 = (f32[136,128]{1,0:T(8,128)S(1)}, f32[136,128]{1,0:T(8,128)S(1)}, u32[]{:S(2)}, u32[]{:S(2)}) collective-permute-start(f32[136,128]{1,0:T(8,128)S(1)} %get-tuple-element.55), channel_id=1, source_target_pairs={{0,16},{1,17},{2,18},{3,19},{4,20},{5,21},{6,22},{7,23},{8,24},{9,... | collective-permute-start | bytes 208904 | tf_op jit(solution)/shard_map/ppermute | solution.py:39
  66.0 3.7 %collective-permute-start.15 = (f32[12,16,256]{2,1,0:T(8,128)S(1)}, f32[12,16,256]{2,1,0:T(8,128)S(1)}, u32[]{:S(2)}, u32[]{:S(2)}) collective-permute-start(f32[12,16,256]{2,1,0:T(8,128)S(1)} %join_rows.1._), channel_id=1, source_target_pairs={{0,0},{1,17},{2,34},{3,51},{4,68},{5,85},{6,102},{7,119},{8,8},{9,... | collective-permute-start | bytes 589832 | tf_op jit(solution)/shard_map/ppermute | solution.py:39
  74.2 1.9 %collective-permute-done.21.opposite = f32[136,128]{1,0:T(8,128)S(1)} collective-permute-done((f32[136,128]{1,0:T(8,128)S(1)}, f32[136,128]{1,0:T(8,128)S(1)}, u32[]{:S(2)}, u32[]{:S(2)}) %collective-permute-start.21) | collective-permute-done | bytes 69664 | tf_op jit(solution)/shard_map/ppermute | solution.py:39
  76.9 4.0 %collective-permute-start.24 = (f32[136,128]{1,0:T(8,128)S(1)}, f32[136,128]{1,0:T(8,128)S(1)}, u32[]{:S(2)}, u32[]{:S(2)}) collective-permute-start(f32[136,128]{1,0:T(8,128)S(1)} %add_four.4.part), channel_id=1, source_target_pairs={{0,12},{1,13},{2,14},{3,15},{4,8},{5,9},{6,10},{7,11},{8,4},{9,5},... | collective-permute-start | bytes 208904 | tf_op jit(solution)/shard_map/ppermute | solution.py:39
  82.8 2.7 %collective-permute-done.25.beyond = f32[136,128]{1,0:T(8,128)S(1)} collective-permute-done((f32[136,128]{1,0:T(8,128)S(1)}, f32[136,128]{1,0:T(8,128)S(1)}, u32[]{:S(2)}, u32[]{:S(2)}) %collective-permute-start.25) | collective-permute-done | bytes 69664 | tf_op jit(solution)/shard_map/ppermute | solution.py:39
  85.5 6.4 %collective-permute-start.26 = (f32[136,128]{1,0:T(8,128)S(1)}, f32[136,128]{1,0:T(8,128)S(1)}, u32[]{:S(2)}, u32[]{:S(2)}) collective-permute-start(f32[136,128]{1,0:T(8,128)S(1)} %add_four.5.part), channel_id=1, source_target_pairs={{0,16},{1,17},{2,18},{3,19},{4,20},{5,21},{6,22},{7,23},{8,24},{9,... | collective-permute-start | bytes 208904 | tf_op jit(solution)/shard_map/ppermute | solution.py:39
  (52 shorter events, 22.7 us)
Async XLA Ops:
  0.6 9.3 %collective-permute-start = (f32[12,16,256]{2,1,0:T(8,128)}, f32[12,16,256]{2,1,0:T(8,128)S(1)}, u32[]{:S(2)}, u32[]{:S(2)}) collective-permute-start(f32[12,16,256]{2,1,0:T(8,128)} %bitcast.14), channel_id=1, source_target_pairs={{0,1},{1,2},{2,3},{3,0},{4,5},{5,6},{6,7},{7,4},{8,9},{9,10},{10,1... | collective-permute-start | bytes 589832 | tf_op jit(solution)/shard_map/ppermute | solution.py:39
  2.3 7.6 %collective-permute-start.1 = (f32[12,16,256]{2,1,0:T(8,128)}, f32[12,16,256]{2,1,0:T(8,128)S(1)}, u32[]{:S(2)}, u32[]{:S(2)}) collective-permute-start(f32[12,16,256]{2,1,0:T(8,128)} %bitcast.15), channel_id=1, source_target_pairs={{0,3},{1,0},{2,1},{3,2},{4,7},{5,4},{6,5},{7,6},{8,11},{9,8},{10,9... | collective-permute-start | bytes 589832 | tf_op jit(solution)/shard_map/ppermute | solution.py:39
  4.5 6.8 %collective-permute-start.2 = (f32[12,16,256]{2,1,0:T(8,128)}, f32[12,16,256]{2,1,0:T(8,128)S(1)}, u32[]{:S(2)}, u32[]{:S(2)}) collective-permute-start(f32[12,16,256]{2,1,0:T(8,128)} %bitcast.16), channel_id=1, source_target_pairs={{0,2},{1,3},{2,0},{3,1},{4,6},{5,7},{6,4},{7,5},{8,10},{9,11},{10,... | collective-permute-start | bytes 589832 | tf_op jit(solution)/shard_map/ppermute | solution.py:39
  11.5 8.2 %collective-permute-start.3 = (f32[384,256]{1,0:T(8,128)S(1)}, f32[384,256]{1,0:T(8,128)S(1)}, u32[]{:S(2)}, u32[]{:S(2)}) collective-permute-start(f32[384,256]{1,0:T(8,128)S(1)} %get-tuple-element.32.la_ref), channel_id=1, source_target_pairs={{0,4},{1,5},{2,6},{3,7},{4,8},{5,9},{6,10},{7,11},{8,12},{9,13},{1... | collective-permute-start | bytes 1179656 | tf_op jit(solution)/shard_map/ppermute | solution.py:39
  12.5 9.3 %collective-permute-start.5 = (f32[384,256]{1,0:T(8,128)S(1)}, f32[384,256]{1,0:T(8,128)S(1)}, u32[]{:S(2)}, u32[]{:S(2)}) collective-permute-start(f32[384,256]{1,0:T(8,128)S(1)} %get-tuple-element.33.lb_ref), channel_id=1, source_target_pairs={{0,12},{1,13},{2,14},{3,15},{4,0},{5,1},{6,2},{7,3},{8,4},{9,5},{1... | collective-permute-start | bytes 1179656 | tf_op jit(solution)/shard_map/ppermute | solution.py:39
  14.2 10.5 %collective-permute-start.7 = (f32[384,256]{1,0:T(8,128)S(1)}, f32[384,256]{1,0:T(8,128)S(1)}, u32[]{:S(2)}, u32[]{:S(2)}) collective-permute-start(f32[384,256]{1,0:T(8,128)S(1)} %get-tuple-element.33.lb_ref), channel_id=1, source_target_pairs={{0,4},{1,5},{2,6},{3,7},{4,8},{5,9},{6,10},{7,11},{8,12},{9,13},{1... | collective-permute-start | bytes 1179656 | tf_op jit(solution)/shard_map/ppermute | solution.py:39
  14.2 14.1 %collective-permute-start.8 = (f32[384,256]{1,0:T(8,128)S(1)}, f32[384,256]{1,0:T(8,128)S(1)}, u32[]{:S(2)}, u32[]{:S(2)}) collective-permute-start(f32[384,256]{1,0:T(8,128)S(1)} %get-tuple-element.32.la_ref), channel_id=1, source_target_pairs={{0,12},{1,13},{2,14},{3,15},{4,0},{5,1},{6,2},{7,3},{8,4},{9,5},{1... | collective-permute-start | bytes 1179656 | tf_op jit(solution)/shard_map/ppermute | solution.py:39
  16.9 11.4 %collective-permute-start.9 = (f32[12,16,256]{2,1,0:T(8,128)S(1)}, f32[12,16,256]{2,1,0:T(8,128)S(1)}, u32[]{:S(2)}, u32[]{:S(2)}) collective-permute-start(f32[12,16,256]{2,1,0:T(8,128)S(1)} %bitcast.18), channel_id=1, source_target_pairs={{0,0},{1,16},{2,32},{3,48},{4,64},{5,80},{6,96},{7,112},{8,8},{9,2... | collective-permute-start | bytes 589832 | tf_op jit(solution)/shard_map/ppermute | solution.py:39
  19.7 12.3 %collective-permute-start.4 = (f32[384,256]{1,0:T(8,128)S(1)}, f32[384,256]{1,0:T(8,128)S(1)}, u32[]{:S(2)}, u32[]{:S(2)}) collective-permute-start(f32[384,256]{1,0:T(8,128)S(1)} %collective-permute-done.3.la_ref), channel_id=1, source_target_pairs={{0,4},{1,5},{2,6},{3,7},{4,8},{5,9},{6,10},{7,11},{8,12},{9,13},{1... | collective-permute-start | bytes 1179656 | tf_op jit(solution)/shard_map/ppermute | solution.py:39
  21.8 10.2 %collective-permute-start.6 = (f32[384,256]{1,0:T(8,128)S(1)}, f32[384,256]{1,0:T(8,128)S(1)}, u32[]{:S(2)}, u32[]{:S(2)}) collective-permute-start(f32[384,256]{1,0:T(8,128)S(1)} %collective-permute-done.5.lb_ref), channel_id=1, source_target_pairs={{0,12},{1,13},{2,14},{3,15},{4,0},{5,1},{6,2},{7,3},{8,4},{9,5},{1... | collective-permute-start | bytes 1179656 | tf_op jit(solution)/shard_map/ppermute | solution.py:39
  35.1 5.1 %collective-permute-start.10 = (f32[4,6,2,16,256]{4,3,2,1,0:T(8,128)S(1)}, f32[4,6,2,16,256]{4,3,2,1,0:T(8,128)S(1)}, u32[]{:S(2)}, u32[]{:S(2)}) collective-permute-start(f32[4,6,2,16,256]{4,3,2,1,0:T(8,128)S(1)} %get-tuple-element.41), channel_id=1, source_target_pairs={{0,16},{1,17},{2,18},{3,19},{4,20},{5,21},{6,22},{7,23},{8,24},{9,... | collective-permute-start | bytes 2359304 | tf_op jit(solution)/shard_map/ppermute | solution.py:39
  40.3 7.9 %collective-permute-start.11 = (f32[2,6,2,16,256]{4,3,2,1,0:T(8,128)S(1)}, f32[2,6,2,16,256]{4,3,2,1,0:T(8,128)S(1)}, u32[]{:S(2)}, u32[]{:S(2)}) collective-permute-start(f32[2,6,2,16,256]{4,3,2,1,0:T(8,128)S(1)} %get-tuple-element.43), channel_id=1, source_target_pairs={{0,32},{1,33},{2,34},{3,35},{4,36},{5,37},{6,38},{7,39},{8,40},{9,... | collective-permute-start | bytes 1179656 | tf_op jit(solution)/shard_map/ppermute | solution.py:39
  40.5 7.1 %collective-permute-start.12 = (f32[6,16,256]{2,1,0:T(8,128)S(1)}, f32[6,16,256]{2,1,0:T(8,128)S(1)}, u32[]{:S(2)}, u32[]{:S(2)}) collective-permute-start(f32[6,16,256]{2,1,0:T(8,128)S(1)} %get-tuple-element.46), channel_id=1, source_target_pairs={{0,8},{1,9},{2,10},{3,11},{4,12},{5,13},{6,14},{7,15},{8,0},{9,1},... | collective-permute-start | bytes 294920 | tf_op jit(solution)/shard_map/ppermute | solution.py:39
  48.3 4.6 %collective-permute-start.13 = (f32[6,2,16,256]{3,2,1,0:T(8,128)S(1)}, f32[6,2,16,256]{3,2,1,0:T(8,128)S(1)}, u32[]{:S(2)}, u32[]{:S(2)}) collective-permute-start(f32[6,2,16,256]{3,2,1,0:T(8,128)S(1)} %get-tuple-element.48), channel_id=1, source_target_pairs={{0,96},{1,97},{2,98},{3,99},{4,100},{5,101},{6,102},{7,103},{8,104... | collective-permute-start | bytes 589832 | tf_op jit(solution)/shard_map/ppermute | solution.py:39
  56.0 10.0 %collective-permute-start.14 = (f32[6,16,256]{2,1,0:T(8,128)S(1)}, f32[6,16,256]{2,1,0:T(8,128)S(1)}, u32[]{:S(2)}, u32[]{:S(2)}) collective-permute-start(f32[6,16,256]{2,1,0:T(8,128)S(1)} %get-tuple-element.53), channel_id=1, source_target_pairs={{0,8},{1,9},{2,10},{3,11},{4,12},{5,13},{6,14},{7,15},{8,0},{9,1},... | collective-permute-start | bytes 294920 | tf_op jit(solution)/shard_map/ppermute | solution.py:39
  62.7 7.1 %collective-permute-start.17 = (f32[136,128]{1,0:T(8,128)S(1)}, f32[136,128]{1,0:T(8,128)S(1)}, u32[]{:S(2)}, u32[]{:S(2)}) collective-permute-start(f32[136,128]{1,0:T(8,128)S(1)} %add_two.1.part), channel_id=1, source_target_pairs={{0,32},{1,33},{2,34},{3,35},{4,36},{5,37},{6,38},{7,39},{8,40},{9,... | collective-permute-start | bytes 208904 | tf_op jit(solution)/shard_map/ppermute | solution.py:39
  63.7 6.1 %collective-permute-start.18 = (f32[136,128]{1,0:T(8,128)S(1)}, f32[136,128]{1,0:T(8,128)S(1)}, u32[]{:S(2)}, u32[]{:S(2)}) collective-permute-start(f32[136,128]{1,0:T(8,128)S(1)} %add_two.1.part), channel_id=1, source_target_pairs={{0,96},{1,97},{2,98},{3,99},{4,100},{5,101},{6,102},{7,103},{8,104... | collective-permute-start | bytes 208904 | tf_op jit(solution)/shard_map/ppermute | solution.py:39
  64.7 5.0 %collective-permute-start.19 = (f32[136,128]{1,0:T(8,128)S(1)}, f32[136,128]{1,0:T(8,128)S(1)}, u32[]{:S(2)}, u32[]{:S(2)}) collective-permute-start(f32[136,128]{1,0:T(8,128)S(1)} %add_two.1.part), channel_id=1, source_target_pairs={{0,64},{1,65},{2,66},{3,67},{4,68},{5,69},{6,70},{7,71},{8,72},{9,... | collective-permute-start | bytes 208904 | tf_op jit(solution)/shard_map/ppermute | solution.py:39
  66.0 19.4 %collective-permute-start.15 = (f32[12,16,256]{2,1,0:T(8,128)S(1)}, f32[12,16,256]{2,1,0:T(8,128)S(1)}, u32[]{:S(2)}, u32[]{:S(2)}) collective-permute-start(f32[12,16,256]{2,1,0:T(8,128)S(1)} %join_rows.1._), channel_id=1, source_target_pairs={{0,0},{1,17},{2,34},{3,51},{4,68},{5,85},{6,102},{7,119},{8,8},{9,... | collective-permute-start | bytes 589832 | tf_op jit(solution)/shard_map/ppermute | solution.py:39
  71.4 4.7 %collective-permute-start.21 = (f32[136,128]{1,0:T(8,128)S(1)}, f32[136,128]{1,0:T(8,128)S(1)}, u32[]{:S(2)}, u32[]{:S(2)}) collective-permute-start(f32[136,128]{1,0:T(8,128)S(1)} %add_four.3.part), channel_id=1, source_target_pairs={{0,3},{1,2},{2,1},{3,0},{4,7},{5,6},{6,5},{7,4},{8,11},{9,10},{10,... | collective-permute-start | bytes 208904 | tf_op jit(solution)/shard_map/ppermute | solution.py:39
  71.8 5.0 %collective-permute-start.22 = (f32[136,128]{1,0:T(8,128)S(1)}, f32[136,128]{1,0:T(8,128)S(1)}, u32[]{:S(2)}, u32[]{:S(2)}) collective-permute-start(f32[136,128]{1,0:T(8,128)S(1)} %add_four.3.part), channel_id=1, source_target_pairs={{0,2},{1,3},{2,0},{3,1},{4,6},{5,7},{6,4},{7,5},{8,10},{9,11},{10,... | collective-permute-start | bytes 208904 | tf_op jit(solution)/shard_map/ppermute | solution.py:39
  76.9 6.0 %collective-permute-start.24 = (f32[136,128]{1,0:T(8,128)S(1)}, f32[136,128]{1,0:T(8,128)S(1)}, u32[]{:S(2)}, u32[]{:S(2)}) collective-permute-start(f32[136,128]{1,0:T(8,128)S(1)} %add_four.4.part), channel_id=1, source_target_pairs={{0,12},{1,13},{2,14},{3,15},{4,8},{5,9},{6,10},{7,11},{8,4},{9,5},... | collective-permute-start | bytes 208904 | tf_op jit(solution)/shard_map/ppermute | solution.py:39
  80.8 4.7 %collective-permute-start.25 = (f32[136,128]{1,0:T(8,128)S(1)}, f32[136,128]{1,0:T(8,128)S(1)}, u32[]{:S(2)}, u32[]{:S(2)}) collective-permute-start(f32[136,128]{1,0:T(8,128)S(1)} %add_four.4.part), channel_id=1, source_target_pairs={{0,8},{1,9},{2,10},{3,11},{4,12},{5,13},{6,14},{7,15},{8,0},{9,1},... | collective-permute-start | bytes 208904 | tf_op jit(solution)/shard_map/ppermute | solution.py:39
  85.5 7.4 %collective-permute-start.26 = (f32[136,128]{1,0:T(8,128)S(1)}, f32[136,128]{1,0:T(8,128)S(1)}, u32[]{:S(2)}, u32[]{:S(2)}) collective-permute-start(f32[136,128]{1,0:T(8,128)S(1)} %add_four.5.part), channel_id=1, source_target_pairs={{0,16},{1,17},{2,18},{3,19},{4,20},{5,21},{6,22},{7,23},{8,24},{9,... | collective-permute-start | bytes 208904 | tf_op jit(solution)/shard_map/ppermute | solution.py:39
  (4 other events, 23.6 us)

commit v4 on v3

--- a/solution.py
+++ b/solution.py
@@ -60,10 +60,9 @@
 
 def crossing(stage, mask):
     def target(x, c, z, y):
-        axis = (stage + c) % 3
-        if axis == 0:
+        if stage == 2:
             return x ^ mask, c, z, y
-        if axis == 1:
+        if stage == c:
             return x, c, z, y ^ mask
         return x, c, z ^ mask, y
 
@@ -207,15 +206,24 @@
 
 
 def invert_rest(strict_ref, blocks_ref, l_ref, _, inverse_ref):
-    row, col = grids()
-    strict = strict_ref[...]
-    inverse = blocks_ref[...]
+    n = NB // 2
+    row = lax.broadcasted_iota(jnp.int32, (n, n), 0)
+    col = lax.broadcasted_iota(jnp.int32, (n, n), 1)
+    strict = [strict_ref[:n, :n], strict_ref[n:, n:]]
+    inverse = [blocks_ref[:n, :n], blocks_ref[n:, n:]]
     size = 16
-    while size < NB:
+    while size < n:
         beside = (row // (2 * size) == col // (2 * size)) & (row // size != col // size)
-        inverse = inverse - dot6(inverse, dot6(jnp.where(beside, strict, 0.0), inverse))
+        inner = [dot6(jnp.where(beside, strict[i], 0.0), inverse[i]) for i in range(2)]
+        inverse = [inverse[i] - dot6(inverse[i], inner[i]) for i in range(2)]
         size *= 2
-    inverse_ref[...] = inverse * (1.0 / jnp.sum(jnp.where(row == col, l_ref[...], 0.0), axis=0, keepdims=True))
+    below = -dot6(inverse[1], dot6(strict_ref[n:, :n], inverse[0]))
+    diagonal = [jnp.where(row == col, l_ref[at : at + n, at : at + n], 0.0) for at in (0, n)]
+    by_col = [1.0 / jnp.sum(value, axis=0, keepdims=True) for value in diagonal]
+    inverse_ref[:n, :n] = inverse[0] * by_col[0]
+    inverse_ref[:n, n:] = jnp.zeros((n, n), F32)
+    inverse_ref[n:, :n] = below * by_col[0]
+    inverse_ref[n:, n:] = inverse[1] * by_col[1]
 
 
 def product(lh, ll, s_ref, j):
@@ -311,14 +319,17 @@
     out_ref[...] = dot6(adjusted.reshape(PIECE, NB), inv_ref[...]).reshape(UR, 16, NB)
 
 
-def start_panel(share, own_ref, mine_ref, inv_ref, lbar_ref, out_ref):
+def start_panel(share, own_ref, mine_ref, inv_ref, lbar_ref, l_ref, out_ref, inv_t_ref, l_t_ref):
     row, col = grids()
-    gram = tdot6(inv_ref[...], tdot6(own_ref[...].reshape(PIECE, NB), mine_ref[...].reshape(PIECE, NB)))
+    inv_t = inv_ref[...].T
+    inv_t_ref[...] = inv_t
+    l_t_ref[...] = l_ref[...].T
+    gram = dot6(inv_t, tdot6(own_ref[...].reshape(PIECE, NB), mine_ref[...].reshape(PIECE, NB)))
     out_ref[...] = lbar_ref[...] * share - jnp.where(row >= col, gram, 0.0)
 
 
 def finish_panel(
-    first_ref, second_ref, l_first_ref, l_second_ref, l_ref, inv_ref, base_ref, keep_ref, send_ref, second_out
+    first_ref, second_ref, l_first_ref, l_second_ref, l_t_ref, inv_t_ref, inv_ref, base_ref, keep_ref, send_ref, second_out
 ):
     c = place()[1]
     row, col = grids()
@@ -326,10 +337,11 @@
     cross = tdot6(first_ref[...].reshape(half, NB), l_first_ref[...].reshape(half, NB))
     cross += tdot6(second_ref[...].reshape(half, NB), l_second_ref[...].reshape(half, NB))
     inverse = inv_ref[...]
-    fresh = base_ref[...] + jnp.where(row >= col, 2.0 * tdot6(inverse, cross), 0.0)
-    phi = tdot6(l_ref[...], fresh)
+    inv_t = inv_t_ref[...]
+    fresh = base_ref[...] + jnp.where(row >= col, 2.0 * dot6(inv_t, cross), 0.0)
+    phi = dot6(l_t_ref[...], fresh)
     phi = jnp.where(row > col, phi, jnp.where(row == col, 0.5 * phi, 0.0))
-    full = dot6(tdot6(inverse, phi), inverse)
+    full = dot6(dot6(inv_t, phi), inverse)
     result = 0.5 * (full + full.T)
     n = NB // 2
     row, col = row[:n, :n], col[:n, :n]
@@ -348,7 +360,7 @@
     out_ref[...] = part[...] + other[...]
 
 
-def add_four(part, near, opposite, beyond, _, out_ref):
+def add_four(part, beyond, near, opposite, _, out_ref):
     out_ref[...] = (part[...] + near[...]) + (beyond[...] + opposite[...])
 
 
@@ -376,9 +388,9 @@
     lines = kept(4 * SLAB, 128)
     square = kept(NB, NB)
 
+    far = permute(mine, first_axis(2))
     up = permute(mine, first_axis(1))
     down = permute(mine, first_axis(-1))
-    far = permute(mine, first_axis(2))
     s0, s3, strict, blocks, l_kept, lbar_kept, own_kept, mine_kept = call(
         invert_blocks,
         [s_lines, l_panel, lbar_panel, own, mine],
@@ -458,15 +470,15 @@
         size=1_000_000,
         specs=[VMEM] * 2 + [ANY] * 2,
     )
-    (base,) = call(
-        functools.partial(start_panel, share), [own_kept, mine_kept, inverse, lbar_kept], [square], 6,
+    base, inv_t, l_t = call(
+        functools.partial(start_panel, share), [own_kept, mine_kept, inverse, lbar_kept, l_kept], [square] * 3, 6,
         flops=2 * 12 * NB**3, size=4_000_000,
     )
     keep, send = call(add_rows, [keep, permute(send, halving(1))], [tile, tile], 6, size=1_000_000)
     half = kept(NB // 2 + 8, NB // 2)
     part, other, send = call(
         finish_panel,
-        [keep, send, l_keep, l_other, l_kept, inverse, base],
+        [keep, send, l_keep, l_other, l_t, inv_t, inverse, base],
         [half, half, tile],
         8,
         flops=6 * 12 * NB**3,
@@ -477,13 +489,13 @@
     (part,) = call(add_two, [part, permute(other, other_core)], [half], 4, size=500_000)
 
     def add_around(stage, after):
-        others = [permute(part, crossing(stage, mask)) for mask in (1, 3, 2)]
+        others = [permute(part, crossing(stage, mask)) for mask in (2, 1, 3)]
         return call(add_four, [part, *others, after], [half], 4, size=1_000_000, specs=[VMEM] * 4 + [ANY])
 
     (part,) = add_around(0, rows)
     rows = permute(rows, to_rows)
     (part,) = add_around(1, inverse)
-    (part,) = add_around(2, rows)
+    (part,) = add_around(2, inverse)
     (abar,) = call(
         finish_rows,
         [own_kept, rows, inverse],

time: 93.8 us -> 90.7 us (0.967)
  the two profiles are of different devices: /device:TPU:7 before, /device:TPU:1 now
where the time goes in v4:
time: 90.7 us; the launch traced here: 90.6 us
  starting transfers between devices  48.4 us (53%)
  Pallas kernels  22.5 us (25%)
  waiting for transfers between devices  18.8 us (21%)
    ppermute x27, starting transfers between devices, permute(): return lax.ppermute(value, AXES, pairs(target))  48.4 us
    pallas_call x20, Pallas kernels, call(): pl.pallas_call(kernel, in_specs=specs or [VMEM] * len(inputs), out_specs=...  22.5 us
    ppermute x27, waiting for transfers between devices, permute(): return lax.ppermute(value, AXES, pairs(target))  18.8 us
  transfers between devices with their start and end apart: 27, of which 10 were waited for; matrix products, arithmetic and copies ran while one was open for 0% of the time, Pallas kernels for 17%

profile of v4, /device:TPU:1, one launch (start us, length us, event | category | flops | bytes accessed | tf_op | source)
XLA Modules:
  0.0 90.6 jit_solution(5378217063755115896)
XLA Ops:
  0.6 2.5 %collective-permute-start = (f32[12,16,256]{2,1,0:T(8,128)}, f32[12,16,256]{2,1,0:T(8,128)S(1)}, u32[]{:S(2)}, u32[]{:S(2)}) collective-permute-start(f32[12,16,256]{2,1,0:T(8,128)} %bitcast.14), channel_id=1, source_target_pairs={{0,1},{1,2},{2,3},{3,0},{4,5},{5,6},{6,7},{7,4},{8,9},{9,10},{10,1... | collective-permute-start | bytes 589832 | tf_op jit(solution)/shard_map/ppermute | solution.py:39
  3.2 2.2 %collective-permute-start.1 = (f32[12,16,256]{2,1,0:T(8,128)}, f32[12,16,256]{2,1,0:T(8,128)S(1)}, u32[]{:S(2)}, u32[]{:S(2)}) collective-permute-start(f32[12,16,256]{2,1,0:T(8,128)} %bitcast.15), channel_id=1, source_target_pairs={{0,3},{1,0},{2,1},{3,2},{4,7},{5,4},{6,5},{7,6},{8,11},{9,8},{10,9... | collective-permute-start | bytes 589832 | tf_op jit(solution)/shard_map/ppermute | solution.py:39
  6.6 4.1 %invert_blocks.1 = (f32[9216,128]{1,0:T(8,128)S(1)}, f32[9216,128]{1,0:T(8,128)S(1)}, f32[256,256]{1,0:T(8,128)S(1)}, f32[256,256]{1,0:T(8,128)S(1)}, f32[256,25...) custom-call(f32[36864,128]{1,0:T(8,128)} %bitcast.10, ...), custom_call_target="tpu_custom_call" | custom-call | flops 1207959552 | bytes 10000000 | tf_op jit(solution)/shard_map/invert_blocks/pallas_call | solution.py:121
  15.0 2.7 %collective-permute-start.8 = (f32[384,256]{1,0:T(8,128)S(1)}, f32[384,256]{1,0:T(8,128)S(1)}, u32[]{:S(2)}, u32[]{:S(2)}) collective-permute-start(f32[384,256]{1,0:T(8,128)S(1)} %get-tuple-element.35.la_ref), channel_id=1, source_target_pairs={{0,12},{1,13},{2,14},{3,15},{4,0},{5,1},{6,2},{7,3},{8,4},{9,5},{1... | collective-permute-start | bytes 1179656 | tf_op jit(solution)/shard_map/ppermute | solution.py:39
  17.7 1.9 %collective-permute-start.9 = (f32[12,16,256]{2,1,0:T(8,128)S(1)}, f32[12,16,256]{2,1,0:T(8,128)S(1)}, u32[]{:S(2)}, u32[]{:S(2)}) collective-permute-start(f32[12,16,256]{2,1,0:T(8,128)S(1)} %bitcast.18), channel_id=1, source_target_pairs={{0,0},{1,16},{2,32},{3,48},{4,64},{5,80},{6,96},{7,112},{8,8},{9,2... | collective-permute-start | bytes 589832 | tf_op jit(solution)/shard_map/ppermute | solution.py:39
  20.5 2.9 %collective-permute-start.4 = (f32[384,256]{1,0:T(8,128)S(1)}, f32[384,256]{1,0:T(8,128)S(1)}, u32[]{:S(2)}, u32[]{:S(2)}) collective-permute-start(f32[384,256]{1,0:T(8,128)S(1)} %collective-permute-done.3.la_ref), channel_id=1, source_target_pairs={{0,4},{1,5},{2,6},{3,7},{4,8},{5,9},{6,10},{7,11},{8,12},{9,13},{1... | collective-permute-start | bytes 1179656 | tf_op jit(solution)/shard_map/ppermute | solution.py:39
  23.4 3.3 %collective-permute-start.6 = (f32[384,256]{1,0:T(8,128)S(1)}, f32[384,256]{1,0:T(8,128)S(1)}, u32[]{:S(2)}, u32[]{:S(2)}) collective-permute-start(f32[384,256]{1,0:T(8,128)S(1)} %collective-permute-done.5.lb_ref), channel_id=1, source_target_pairs={{0,12},{1,13},{2,14},{3,15},{4,0},{5,1},{6,2},{7,3},{8,4},{9,5},{1... | collective-permute-start | bytes 1179656 | tf_op jit(solution)/shard_map/ppermute | solution.py:39
  26.6 2.4 %multiply_first.1 = (f32[256,1536]{1,0:T(8,128)S(1)}, f32[9216,128]{1,0:T(8,128)S(1)}) custom-call(f32[384,256]{1,0:T(8,128)S(1)} %get-tuple-element.35.la_ref, f32[384,256]{1,0:T(8,128)S(1)} %get-tuple-element.36.lb_ref, f32[9216,128]{1,0:T(8,128)S(1)} %get-tuple-element.38.s_ref, f32[36864,128]{1,0:T(8,128)} %bitcast.11), custom_call_target="tpu_custom_call" | custom-call | flops 1811939328 | bytes 6000000 | tf_op jit(solution)/shard_map/multiply_first/pallas_call | solution.py:121
  29.0 2.4 %multiply_up.1 = (f32[256,1536]{1,0:T(8,128)S(1)}, f32[9216,128]{1,0:T(8,128)S(1)}) custom-call(f32[384,256]{1,0:T(8,128)S(1)} %collective-permute-done.3.la_ref, f32[384,256]{1,0:T(8,128)S(1)} %collective-permute-done.7.lb_ref, f32[9216,128]{1,0:T(8,128)S(1)} %get-tuple-element.37.s_ref, f32[256,1536]{1,0:T(8,128)S(1)} %get-tuple-element.39.acc_ref._, ...), custom_call_target="tpu_custom_call" | custom-call | flops 1811939328 | bytes 6000000 | tf_op jit(solution)/shard_map/multiply_up/pallas_call | solution.py:121
  31.5 2.1 %multiply_down.1.acc_ref = f32[256,1536]{1,0:T(8,128)S(1)} custom-call(f32[384,256]{1,0:T(8,128)S(1)} %collective-permute-done.8.la_ref, f32[384,256]{1,0:T(8,128)S(1)} %collective-permute-done.5.lb_ref, f32[9216,128]{1,0:T(8,128)S(1)} %get-tuple-element.41.s_ref, f32[256,1536]{1,0:T(8,128)S(1)} %get-tuple-element.42.acc_ref, ...), custom_call_target="tpu_custom_call" | custom-call | flops 1811939328 | bytes 6000000 | tf_op jit(solution)/shard_map/multiply_down/pallas_call | solution.py:121
  33.6 3.1 %multiply_last.1 = (f32[4,6,2,16,256]{4,3,2,1,0:T(8,128)S(1)}, f32[4,6,2,16,256]{4,3,2,1,0:T(8,128)S(1)}) custom-call(f32[384,256]{1,0:T(8,128)S(1)} %collective-permute-done.4.la_ref, f32[384,256]{1,0:T(8,128)S(1)} %collective-permute-done.6.lb_ref, f32[9216,128]{1,0:T(8,128)S(1)} %get-tuple-element.40.s_ref, f32[256,1536]{1,0:T(8,128)S(1)} %multiply_down.1.acc_ref), custom_call_target="tpu_custom_call" | custom-call | flops 1811939328 | bytes 6000000 | tf_op jit(solution)/shard_map/multiply_last/pallas_call | solution.py:121
  37.8 1.9 %collective-permute-done.10.rows_in = f32[4,6,2,16,256]{4,3,2,1,0:T(8,128)S(1)} collective-permute-done((f32[4,6,2,16,256]{4,3,2,1,0:T(8,128)S(1)}, f32[4,6,2,16,256]{4,3,2,1,0:T(8,128)S(1)}, u32[]{:S(2)}, u32[]{:S(2)}) %collective-permute-start.10) | collective-permute-done | bytes 786464 | tf_op jit(solution)/shard_map/ppermute | solution.py:39
  39.8 3.9 %collective-permute-start.11 = (f32[2,6,2,16,256]{4,3,2,1,0:T(8,128)S(1)}, f32[2,6,2,16,256]{4,3,2,1,0:T(8,128)S(1)}, u32[]{:S(2)}, u32[]{:S(2)}) collective-permute-start(f32[2,6,2,16,256]{4,3,2,1,0:T(8,128)S(1)} %get-tuple-element.46), channel_id=1, source_target_pairs={{0,32},{1,33},{2,34},{3,35},{4,36},{5,37},{6,38},{7,39},{8,40},{9,... | collective-permute-start | bytes 1179656 | tf_op jit(solution)/shard_map/ppermute | solution.py:39
  43.7 2.8 %collective-permute-start.12 = (f32[6,16,256]{2,1,0:T(8,128)S(1)}, f32[6,16,256]{2,1,0:T(8,128)S(1)}, u32[]{:S(2)}, u32[]{:S(2)}) collective-permute-start(f32[6,16,256]{2,1,0:T(8,128)S(1)} %get-tuple-element.49), channel_id=1, source_target_pairs={{0,8},{1,9},{2,10},{3,11},{4,12},{5,13},{6,14},{7,15},{8,0},{9,1},... | collective-permute-start | bytes 294920 | tf_op jit(solution)/shard_map/ppermute | solution.py:39
  46.5 2.0 %invert_rest.1._.inv_ref = f32[256,256]{1,0:T(8,128)S(1)} custom-call(f32[256,256]{1,0:T(8,128)S(1)} %get-tuple-element.47.strict_ref, f32[256,256]{1,0:T(8,128)S(1)} %get-tuple-element.34._.blocks_ref, f32[256,256]{1,0:T(8,128)S(1)} %get-tuple-element.48.l_ref, f32[2,6,2,16,256]{4,3,2,1,0:T(8,128)S(1)} %get-tuple-element.45._.rows), custom_call_target="tpu_custom_call" | custom-call | flops 1610612736 | bytes 6000000 | tf_op jit(solution)/shard_map/invert_rest/pallas_call | solution.py:121
  50.1 3.7 %collective-permute-done.13.rows_in = f32[6,2,16,256]{3,2,1,0:T(8,128)S(1)} collective-permute-done((f32[6,2,16,256]{3,2,1,0:T(8,128)S(1)}, f32[6,2,16,256]{3,2,1,0:T(8,128)S(1)}, u32[]{:S(2)}, u32[]{:S(2)}) %collective-permute-start.13) | collective-permute-done | bytes 196640 | tf_op jit(solution)/shard_map/ppermute | solution.py:39
  53.9 3.1 %finish_panel.1 = (f32[136,128]{1,0:T(8,128)S(1)}, f32[136,128]{1,0:T(8,128)S(1)}, f32[6,16,256]{2,1,0:T(8,128)S(1)}) custom-call(f32[6,16,256]{2,1,0:T(8,128)S(1)} %get-tuple-element.52.first_ref.keep_ref, f32[6,16,256]{2,1,0:T(8,128)S(1)} %get-tuple-element.53.second_ref, f32[6,16,256]{2,1,0:T(8,128)S(1)} %get-tuple-element.54.l_first_ref, ...), custom_call_target="tpu_custom_call" | custom-call | flops 1207959552 | bytes 4000000 | tf_op jit(solution)/shard_map/finish_panel/pallas_call | solution.py:121
  57.0 2.2 %collective-permute-start.16 = (f32[136,128]{1,0:T(8,128)S(1)}, f32[136,128]{1,0:T(8,128)S(1)}, u32[]{:S(2)}, u32[]{:S(2)}) collective-permute-start(f32[136,128]{1,0:T(8,128)S(1)} %get-tuple-element.61), channel_id=1, source_target_pairs={{0,16},{1,17},{2,18},{3,19},{4,20},{5,21},{6,22},{7,23},{8,24},{9,... | collective-permute-start | bytes 208904 | tf_op jit(solution)/shard_map/ppermute | solution.py:39
  59.1 2.7 %collective-permute-start.14 = (f32[6,16,256]{2,1,0:T(8,128)S(1)}, f32[6,16,256]{2,1,0:T(8,128)S(1)}, u32[]{:S(2)}, u32[]{:S(2)}) collective-permute-start(f32[6,16,256]{2,1,0:T(8,128)S(1)} %get-tuple-element.59), channel_id=1, source_target_pairs={{0,8},{1,9},{2,10},{3,11},{4,12},{5,13},{6,14},{7,15},{8,0},{9,1},... | collective-permute-start | bytes 294920 | tf_op jit(solution)/shard_map/ppermute | solution.py:39
  65.2 4.0 %collective-permute-start.15 = (f32[12,16,256]{2,1,0:T(8,128)S(1)}, f32[12,16,256]{2,1,0:T(8,128)S(1)}, u32[]{:S(2)}, u32[]{:S(2)}) collective-permute-start(f32[12,16,256]{2,1,0:T(8,128)S(1)} %join_rows.1._), channel_id=1, source_target_pairs={{0,0},{1,17},{2,34},{3,51},{4,68},{5,85},{6,102},{7,119},{8,8},{9,... | collective-permute-start | bytes 589832 | tf_op jit(solution)/shard_map/ppermute | solution.py:39
  70.8 1.8 %collective-permute-start.22 = (f32[136,128]{1,0:T(8,128)S(1)}, f32[136,128]{1,0:T(8,128)S(1)}, u32[]{:S(2)}, u32[]{:S(2)}) collective-permute-start(f32[136,128]{1,0:T(8,128)S(1)} %add_four.3.part), channel_id=1, source_target_pairs={{0,12},{1,13},{2,14},{3,15},{4,8},{5,9},{6,10},{7,11},{8,4},{9,5},... | collective-permute-start | bytes 208904 | tf_op jit(solution)/shard_map/ppermute | solution.py:39
  72.6 7.5 %collective-permute-done.20.beyond = f32[136,128]{1,0:T(8,128)S(1)} collective-permute-done((f32[136,128]{1,0:T(8,128)S(1)}, f32[136,128]{1,0:T(8,128)S(1)}, u32[]{:S(2)}, u32[]{:S(2)}) %collective-permute-start.20) | collective-permute-done | bytes 69664 | tf_op jit(solution)/shard_map/ppermute | solution.py:39
  81.5 2.7 %collective-permute-start.25 = (f32[136,128]{1,0:T(8,128)S(1)}, f32[136,128]{1,0:T(8,128)S(1)}, u32[]{:S(2)}, u32[]{:S(2)}) collective-permute-start(f32[136,128]{1,0:T(8,128)S(1)} %add_four.4.part), channel_id=1, source_target_pairs={{0,96},{1,97},{2,98},{3,99},{4,100},{5,101},{6,102},{7,103},{8,104... | collective-permute-start | bytes 208904 | tf_op jit(solution)/shard_map/ppermute | solution.py:39
  86.5 2.2 %collective-permute-start.26 = (f32[136,128]{1,0:T(8,128)S(1)}, f32[136,128]{1,0:T(8,128)S(1)}, u32[]{:S(2)}, u32[]{:S(2)}) collective-permute-start(f32[136,128]{1,0:T(8,128)S(1)} %add_four.5.part), channel_id=1, source_target_pairs={{0,16},{1,17},{2,18},{3,19},{4,20},{5,21},{6,22},{7,23},{8,24},{9,... | collective-permute-start | bytes 208904 | tf_op jit(solution)/shard_map/ppermute | solution.py:39
  (52 shorter events, 19.7 us)
Async XLA Ops:
  0.6 10.1 %collective-permute-start = (f32[12,16,256]{2,1,0:T(8,128)}, f32[12,16,256]{2,1,0:T(8,128)S(1)}, u32[]{:S(2)}, u32[]{:S(2)}) collective-permute-start(f32[12,16,256]{2,1,0:T(8,128)} %bitcast.14), channel_id=1, source_target_pairs={{0,1},{1,2},{2,3},{3,0},{4,5},{5,6},{6,7},{7,4},{8,9},{9,10},{10,1... | collective-permute-start | bytes 589832 | tf_op jit(solution)/shard_map/ppermute | solution.py:39
  3.2 7.6 %collective-permute-start.1 = (f32[12,16,256]{2,1,0:T(8,128)}, f32[12,16,256]{2,1,0:T(8,128)S(1)}, u32[]{:S(2)}, u32[]{:S(2)}) collective-permute-start(f32[12,16,256]{2,1,0:T(8,128)} %bitcast.15), channel_id=1, source_target_pairs={{0,3},{1,0},{2,1},{3,2},{4,7},{5,4},{6,5},{7,6},{8,11},{9,8},{10,9... | collective-permute-start | bytes 589832 | tf_op jit(solution)/shard_map/ppermute | solution.py:39
  5.4 6.8 %collective-permute-start.2 = (f32[12,16,256]{2,1,0:T(8,128)}, f32[12,16,256]{2,1,0:T(8,128)S(1)}, u32[]{:S(2)}, u32[]{:S(2)}) collective-permute-start(f32[12,16,256]{2,1,0:T(8,128)} %bitcast.16), channel_id=1, source_target_pairs={{0,2},{1,3},{2,0},{3,1},{4,6},{5,7},{6,4},{7,5},{8,10},{9,11},{10,... | collective-permute-start | bytes 589832 | tf_op jit(solution)/shard_map/ppermute | solution.py:39
  12.3 8.2 %collective-permute-start.3 = (f32[384,256]{1,0:T(8,128)S(1)}, f32[384,256]{1,0:T(8,128)S(1)}, u32[]{:S(2)}, u32[]{:S(2)}) collective-permute-start(f32[384,256]{1,0:T(8,128)S(1)} %get-tuple-element.35.la_ref), channel_id=1, source_target_pairs={{0,4},{1,5},{2,6},{3,7},{4,8},{5,9},{6,10},{7,11},{8,12},{9,13},{1... | collective-permute-start | bytes 1179656 | tf_op jit(solution)/shard_map/ppermute | solution.py:39
  13.4 10.0 %collective-permute-start.5 = (f32[384,256]{1,0:T(8,128)S(1)}, f32[384,256]{1,0:T(8,128)S(1)}, u32[]{:S(2)}, u32[]{:S(2)}) collective-permute-start(f32[384,256]{1,0:T(8,128)S(1)} %get-tuple-element.36.lb_ref), channel_id=1, source_target_pairs={{0,12},{1,13},{2,14},{3,15},{4,0},{5,1},{6,2},{7,3},{8,4},{9,5},{1... | collective-permute-start | bytes 1179656 | tf_op jit(solution)/shard_map/ppermute | solution.py:39
  15.0 14.0 %collective-permute-start.7 = (f32[384,256]{1,0:T(8,128)S(1)}, f32[384,256]{1,0:T(8,128)S(1)}, u32[]{:S(2)}, u32[]{:S(2)}) collective-permute-start(f32[384,256]{1,0:T(8,128)S(1)} %get-tuple-element.36.lb_ref), channel_id=1, source_target_pairs={{0,4},{1,5},{2,6},{3,7},{4,8},{5,9},{6,10},{7,11},{8,12},{9,13},{1... | collective-permute-start | bytes 1179656 | tf_op jit(solution)/shard_map/ppermute | solution.py:39
  15.0 16.4 %collective-permute-start.8 = (f32[384,256]{1,0:T(8,128)S(1)}, f32[384,256]{1,0:T(8,128)S(1)}, u32[]{:S(2)}, u32[]{:S(2)}) collective-permute-start(f32[384,256]{1,0:T(8,128)S(1)} %get-tuple-element.35.la_ref), channel_id=1, source_target_pairs={{0,12},{1,13},{2,14},{3,15},{4,0},{5,1},{6,2},{7,3},{8,4},{9,5},{1... | collective-permute-start | bytes 1179656 | tf_op jit(solution)/shard_map/ppermute | solution.py:39
  17.7 13.7 %collective-permute-start.9 = (f32[12,16,256]{2,1,0:T(8,128)S(1)}, f32[12,16,256]{2,1,0:T(8,128)S(1)}, u32[]{:S(2)}, u32[]{:S(2)}) collective-permute-start(f32[12,16,256]{2,1,0:T(8,128)S(1)} %bitcast.18), channel_id=1, source_target_pairs={{0,0},{1,16},{2,32},{3,48},{4,64},{5,80},{6,96},{7,112},{8,8},{9,2... | collective-permute-start | bytes 589832 | tf_op jit(solution)/shard_map/ppermute | solution.py:39
  20.5 13.1 %collective-permute-start.4 = (f32[384,256]{1,0:T(8,128)S(1)}, f32[384,256]{1,0:T(8,128)S(1)}, u32[]{:S(2)}, u32[]{:S(2)}) collective-permute-start(f32[384,256]{1,0:T(8,128)S(1)} %collective-permute-done.3.la_ref), channel_id=1, source_target_pairs={{0,4},{1,5},{2,6},{3,7},{4,8},{5,9},{6,10},{7,11},{8,12},{9,13},{1... | collective-permute-start | bytes 1179656 | tf_op jit(solution)/shard_map/ppermute | solution.py:39
  23.4 10.2 %collective-permute-start.6 = (f32[384,256]{1,0:T(8,128)S(1)}, f32[384,256]{1,0:T(8,128)S(1)}, u32[]{:S(2)}, u32[]{:S(2)}) collective-permute-start(f32[384,256]{1,0:T(8,128)S(1)} %collective-permute-done.5.lb_ref), channel_id=1, source_target_pairs={{0,12},{1,13},{2,14},{3,15},{4,0},{5,1},{6,2},{7,3},{8,4},{9,5},{1... | collective-permute-start | bytes 1179656 | tf_op jit(solution)/shard_map/ppermute | solution.py:39
  39.8 9.1 %collective-permute-start.11 = (f32[2,6,2,16,256]{4,3,2,1,0:T(8,128)S(1)}, f32[2,6,2,16,256]{4,3,2,1,0:T(8,128)S(1)}, u32[]{:S(2)}, u32[]{:S(2)}) collective-permute-start(f32[2,6,2,16,256]{4,3,2,1,0:T(8,128)S(1)} %get-tuple-element.46), channel_id=1, source_target_pairs={{0,32},{1,33},{2,34},{3,35},{4,36},{5,37},{6,38},{7,39},{8,40},{9,... | collective-permute-start | bytes 1179656 | tf_op jit(solution)/shard_map/ppermute | solution.py:39
  43.7 5.1 %collective-permute-start.12 = (f32[6,16,256]{2,1,0:T(8,128)S(1)}, f32[6,16,256]{2,1,0:T(8,128)S(1)}, u32[]{:S(2)}, u32[]{:S(2)}) collective-permute-start(f32[6,16,256]{2,1,0:T(8,128)S(1)} %get-tuple-element.49), channel_id=1, source_target_pairs={{0,8},{1,9},{2,10},{3,11},{4,12},{5,13},{6,14},{7,15},{8,0},{9,1},... | collective-permute-start | bytes 294920 | tf_op jit(solution)/shard_map/ppermute | solution.py:39
  48.9 4.9 %collective-permute-start.13 = (f32[6,2,16,256]{3,2,1,0:T(8,128)S(1)}, f32[6,2,16,256]{3,2,1,0:T(8,128)S(1)}, u32[]{:S(2)}, u32[]{:S(2)}) collective-permute-start(f32[6,2,16,256]{3,2,1,0:T(8,128)S(1)} %get-tuple-element.51), channel_id=1, source_target_pairs={{0,96},{1,97},{2,98},{3,99},{4,100},{5,101},{6,102},{7,103},{8,104... | collective-permute-start | bytes 589832 | tf_op jit(solution)/shard_map/ppermute | solution.py:39
  57.0 4.9 %collective-permute-start.16 = (f32[136,128]{1,0:T(8,128)S(1)}, f32[136,128]{1,0:T(8,128)S(1)}, u32[]{:S(2)}, u32[]{:S(2)}) collective-permute-start(f32[136,128]{1,0:T(8,128)S(1)} %get-tuple-element.61), channel_id=1, source_target_pairs={{0,16},{1,17},{2,18},{3,19},{4,20},{5,21},{6,22},{7,23},{8,24},{9,... | collective-permute-start | bytes 208904 | tf_op jit(solution)/shard_map/ppermute | solution.py:39
  59.1 6.1 %collective-permute-start.14 = (f32[6,16,256]{2,1,0:T(8,128)S(1)}, f32[6,16,256]{2,1,0:T(8,128)S(1)}, u32[]{:S(2)}, u32[]{:S(2)}) collective-permute-start(f32[6,16,256]{2,1,0:T(8,128)S(1)} %get-tuple-element.59), channel_id=1, source_target_pairs={{0,8},{1,9},{2,10},{3,11},{4,12},{5,13},{6,14},{7,15},{8,0},{9,1},... | collective-permute-start | bytes 294920 | tf_op jit(solution)/shard_map/ppermute | solution.py:39
  61.9 7.3 %collective-permute-start.17 = (f32[136,128]{1,0:T(8,128)S(1)}, f32[136,128]{1,0:T(8,128)S(1)}, u32[]{:S(2)}, u32[]{:S(2)}) collective-permute-start(f32[136,128]{1,0:T(8,128)S(1)} %add_two.1.part), channel_id=1, source_target_pairs={{0,2},{1,3},{2,0},{3,1},{4,6},{5,7},{6,4},{7,5},{8,10},{9,11},{10,... | collective-permute-start | bytes 208904 | tf_op jit(solution)/shard_map/ppermute | solution.py:39
  62.8 6.4 %collective-permute-start.18 = (f32[136,128]{1,0:T(8,128)S(1)}, f32[136,128]{1,0:T(8,128)S(1)}, u32[]{:S(2)}, u32[]{:S(2)}) collective-permute-start(f32[136,128]{1,0:T(8,128)S(1)} %add_two.1.part), channel_id=1, source_target_pairs={{0,1},{1,0},{2,3},{3,2},{4,5},{5,4},{6,7},{7,6},{8,9},{9,8},{10,11... | collective-permute-start | bytes 208904 | tf_op jit(solution)/shard_map/ppermute | solution.py:39
  63.5 5.7 %collective-permute-start.19 = (f32[136,128]{1,0:T(8,128)S(1)}, f32[136,128]{1,0:T(8,128)S(1)}, u32[]{:S(2)}, u32[]{:S(2)}) collective-permute-start(f32[136,128]{1,0:T(8,128)S(1)} %add_two.1.part), channel_id=1, source_target_pairs={{0,3},{1,2},{2,1},{3,0},{4,7},{5,6},{6,5},{7,4},{8,11},{9,10},{10,... | collective-permute-start | bytes 208904 | tf_op jit(solution)/shard_map/ppermute | solution.py:39
  65.2 23.5 %collective-permute-start.15 = (f32[12,16,256]{2,1,0:T(8,128)S(1)}, f32[12,16,256]{2,1,0:T(8,128)S(1)}, u32[]{:S(2)}, u32[]{:S(2)}) collective-permute-start(f32[12,16,256]{2,1,0:T(8,128)S(1)} %join_rows.1._), channel_id=1, source_target_pairs={{0,0},{1,17},{2,34},{3,51},{4,68},{5,85},{6,102},{7,119},{8,8},{9,... | collective-permute-start | bytes 589832 | tf_op jit(solution)/shard_map/ppermute | solution.py:39
  69.3 10.8 %collective-permute-start.20 = (f32[136,128]{1,0:T(8,128)S(1)}, f32[136,128]{1,0:T(8,128)S(1)}, u32[]{:S(2)}, u32[]{:S(2)}) collective-permute-start(f32[136,128]{1,0:T(8,128)S(1)} %add_four.3.part), channel_id=1, source_target_pairs={{0,8},{1,9},{2,10},{3,11},{4,12},{5,13},{6,14},{7,15},{8,0},{9,1},... | collective-permute-start | bytes 208904 | tf_op jit(solution)/shard_map/ppermute | solution.py:39
  70.8 10.0 %collective-permute-start.21 = (f32[136,128]{1,0:T(8,128)S(1)}, f32[136,128]{1,0:T(8,128)S(1)}, u32[]{:S(2)}, u32[]{:S(2)}) collective-permute-start(f32[136,128]{1,0:T(8,128)S(1)} %add_four.3.part), channel_id=1, source_target_pairs={{0,4},{1,5},{2,6},{3,7},{4,0},{5,1},{6,2},{7,3},{8,12},{9,13},{10,... | collective-permute-start | bytes 208904 | tf_op jit(solution)/shard_map/ppermute | solution.py:39
  70.8 10.1 %collective-permute-start.22 = (f32[136,128]{1,0:T(8,128)S(1)}, f32[136,128]{1,0:T(8,128)S(1)}, u32[]{:S(2)}, u32[]{:S(2)}) collective-permute-start(f32[136,128]{1,0:T(8,128)S(1)} %add_four.3.part), channel_id=1, source_target_pairs={{0,12},{1,13},{2,14},{3,15},{4,8},{5,9},{6,10},{7,11},{8,4},{9,5},... | collective-permute-start | bytes 208904 | tf_op jit(solution)/shard_map/ppermute | solution.py:39
  80.9 4.9 %collective-permute-start.23 = (f32[136,128]{1,0:T(8,128)S(1)}, f32[136,128]{1,0:T(8,128)S(1)}, u32[]{:S(2)}, u32[]{:S(2)}) collective-permute-start(f32[136,128]{1,0:T(8,128)S(1)} %add_four.4.part), channel_id=1, source_target_pairs={{0,64},{1,65},{2,66},{3,67},{4,68},{5,69},{6,70},{7,71},{8,72},{9,... | collective-permute-start | bytes 208904 | tf_op jit(solution)/shard_map/ppermute | solution.py:39
  81.5 5.0 %collective-permute-start.25 = (f32[136,128]{1,0:T(8,128)S(1)}, f32[136,128]{1,0:T(8,128)S(1)}, u32[]{:S(2)}, u32[]{:S(2)}) collective-permute-start(f32[136,128]{1,0:T(8,128)S(1)} %add_four.4.part), channel_id=1, source_target_pairs={{0,96},{1,97},{2,98},{3,99},{4,100},{5,101},{6,102},{7,103},{8,104... | collective-permute-start | bytes 208904 | tf_op jit(solution)/shard_map/ppermute | solution.py:39
  (4 other events, 22.3 us)

commit v5 on v4

--- a/solution.py
+++ b/solution.py
@@ -385,7 +385,7 @@
     mine = jnp.transpose(l_rows[0], (1, 0, 2))
     own = jnp.transpose(lbar_rows[0], (1, 0, 2))
     dma = pltpu.SemaphoreType.DMA
-    lines = kept(4 * SLAB, 128)
+    lines = kept(4 * SLAB + 16, 128)
     square = kept(NB, NB)
 
     far = permute(mine, first_axis(2))

time: 90.7 us -> 90.7 us (level)
  transfers between devices with their start and end apart: 27 -> 27, of which waited for: 10 -> 9; matrix products, arithmetic and copies ran while one was open for 0% -> 0% of each run, Pallas kernels for 17% -> 17%
where the time goes in v5:
time: 90.7 us; the launch traced here: 90.6 us
  starting transfers between devices  48.4 us (53%)
  Pallas kernels  22.5 us (25%)
  waiting for transfers between devices  18.8 us (21%)
    ppermute x27, starting transfers between devices, permute(): return lax.ppermute(value, AXES, pairs(target))  48.4 us
    pallas_call x20, Pallas kernels, call(): pl.pallas_call(kernel, in_specs=specs or [VMEM] * len(inputs), out_specs=...  22.5 us
    ppermute x27, waiting for transfers between devices, permute(): return lax.ppermute(value, AXES, pairs(target))  18.8 us
  transfers between devices with their start and end apart: 27, of which 9 were waited for; matrix products, arithmetic and copies ran while one was open for 0% of the time, Pallas kernels for 17%

profile of v5, /device:TPU:1, one launch (start us, length us, event | category | flops | bytes accessed | tf_op | source)
XLA Modules:
  0.0 90.6 jit_solution(2688012306966299846)
XLA Ops:
  0.6 2.5 %collective-permute-start = (f32[12,16,256]{2,1,0:T(8,128)}, f32[12,16,256]{2,1,0:T(8,128)S(1)}, u32[]{:S(2)}, u32[]{:S(2)}) collective-permute-start(f32[12,16,256]{2,1,0:T(8,128)} %bitcast.14), channel_id=1, source_target_pairs={{0,1},{1,2},{2,3},{3,0},{4,5},{5,6},{6,7},{7,4},{8,9},{9,10},{10,1... | collective-permute-start | bytes 589832 | tf_op jit(solution)/shard_map/ppermute | solution.py:39
  3.2 2.2 %collective-permute-start.1 = (f32[12,16,256]{2,1,0:T(8,128)}, f32[12,16,256]{2,1,0:T(8,128)S(1)}, u32[]{:S(2)}, u32[]{:S(2)}) collective-permute-start(f32[12,16,256]{2,1,0:T(8,128)} %bitcast.15), channel_id=1, source_target_pairs={{0,3},{1,0},{2,1},{3,2},{4,7},{5,4},{6,5},{7,6},{8,11},{9,8},{10,9... | collective-permute-start | bytes 589832 | tf_op jit(solution)/shard_map/ppermute | solution.py:39
  6.6 4.1 %invert_blocks.1 = (f32[9232,128]{1,0:T(8,128)S(1)}, f32[9232,128]{1,0:T(8,128)S(1)}, f32[256,256]{1,0:T(8,128)S(1)}, f32[256,256]{1,0:T(8,128)S(1)}, f32[256,25...) custom-call(f32[36864,128]{1,0:T(8,128)} %bitcast.10, ...), custom_call_target="tpu_custom_call" | custom-call | flops 1207959552 | bytes 10000000 | tf_op jit(solution)/shard_map/invert_blocks/pallas_call | solution.py:121
  15.0 2.7 %collective-permute-start.8 = (f32[384,256]{1,0:T(8,128)S(1)}, f32[384,256]{1,0:T(8,128)S(1)}, u32[]{:S(2)}, u32[]{:S(2)}) collective-permute-start(f32[384,256]{1,0:T(8,128)S(1)} %get-tuple-element.35.la_ref), channel_id=1, source_target_pairs={{0,12},{1,13},{2,14},{3,15},{4,0},{5,1},{6,2},{7,3},{8,4},{9,5},{1... | collective-permute-start | bytes 1179656 | tf_op jit(solution)/shard_map/ppermute | solution.py:39
  17.7 1.9 %collective-permute-start.9 = (f32[12,16,256]{2,1,0:T(8,128)S(1)}, f32[12,16,256]{2,1,0:T(8,128)S(1)}, u32[]{:S(2)}, u32[]{:S(2)}) collective-permute-start(f32[12,16,256]{2,1,0:T(8,128)S(1)} %bitcast.18), channel_id=1, source_target_pairs={{0,0},{1,16},{2,32},{3,48},{4,64},{5,80},{6,96},{7,112},{8,8},{9,2... | collective-permute-start | bytes 589832 | tf_op jit(solution)/shard_map/ppermute | solution.py:39
  20.5 2.9 %collective-permute-start.4 = (f32[384,256]{1,0:T(8,128)S(1)}, f32[384,256]{1,0:T(8,128)S(1)}, u32[]{:S(2)}, u32[]{:S(2)}) collective-permute-start(f32[384,256]{1,0:T(8,128)S(1)} %collective-permute-done.3.la_ref), channel_id=1, source_target_pairs={{0,4},{1,5},{2,6},{3,7},{4,8},{5,9},{6,10},{7,11},{8,12},{9,13},{1... | collective-permute-start | bytes 1179656 | tf_op jit(solution)/shard_map/ppermute | solution.py:39
  23.4 3.3 %collective-permute-start.6 = (f32[384,256]{1,0:T(8,128)S(1)}, f32[384,256]{1,0:T(8,128)S(1)}, u32[]{:S(2)}, u32[]{:S(2)}) collective-permute-start(f32[384,256]{1,0:T(8,128)S(1)} %collective-permute-done.5.lb_ref), channel_id=1, source_target_pairs={{0,12},{1,13},{2,14},{3,15},{4,0},{5,1},{6,2},{7,3},{8,4},{9,5},{1... | collective-permute-start | bytes 1179656 | tf_op jit(solution)/shard_map/ppermute | solution.py:39
  26.6 2.4 %multiply_first.1 = (f32[256,1536]{1,0:T(8,128)S(1)}, f32[9232,128]{1,0:T(8,128)S(1)}) custom-call(f32[384,256]{1,0:T(8,128)S(1)} %get-tuple-element.35.la_ref, f32[384,256]{1,0:T(8,128)S(1)} %get-tuple-element.36.lb_ref, f32[9232,128]{1,0:T(8,128)S(1)} %get-tuple-element.38.s_ref, f32[36864,128]{1,0:T(8,128)} %bitcast.11), custom_call_target="tpu_custom_call" | custom-call | flops 1811939328 | bytes 6000000 | tf_op jit(solution)/shard_map/multiply_first/pallas_call | solution.py:121
  29.0 2.4 %multiply_up.1 = (f32[256,1536]{1,0:T(8,128)S(1)}, f32[9232,128]{1,0:T(8,128)S(1)}) custom-call(f32[384,256]{1,0:T(8,128)S(1)} %collective-permute-done.3.la_ref, f32[384,256]{1,0:T(8,128)S(1)} %collective-permute-done.7.lb_ref, f32[9232,128]{1,0:T(8,128)S(1)} %get-tuple-element.37.s_ref, f32[256,1536]{1,0:T(8,128)S(1)} %get-tuple-element.39.acc_ref._, ...), custom_call_target="tpu_custom_call" | custom-call | flops 1811939328 | bytes 6000000 | tf_op jit(solution)/shard_map/multiply_up/pallas_call | solution.py:121
  31.5 2.1 %multiply_down.1.acc_ref = f32[256,1536]{1,0:T(8,128)S(1)} custom-call(f32[384,256]{1,0:T(8,128)S(1)} %collective-permute-done.8.la_ref, f32[384,256]{1,0:T(8,128)S(1)} %collective-permute-done.5.lb_ref, f32[9232,128]{1,0:T(8,128)S(1)} %get-tuple-element.41.s_ref, f32[256,1536]{1,0:T(8,128)S(1)} %get-tuple-element.42.acc_ref, ...), custom_call_target="tpu_custom_call" | custom-call | flops 1811939328 | bytes 6000000 | tf_op jit(solution)/shard_map/multiply_down/pallas_call | solution.py:121
  33.6 3.1 %multiply_last.1 = (f32[4,6,2,16,256]{4,3,2,1,0:T(8,128)S(1)}, f32[4,6,2,16,256]{4,3,2,1,0:T(8,128)S(1)}) custom-call(f32[384,256]{1,0:T(8,128)S(1)} %collective-permute-done.4.la_ref, f32[384,256]{1,0:T(8,128)S(1)} %collective-permute-done.6.lb_ref, f32[9232,128]{1,0:T(8,128)S(1)} %get-tuple-element.40.s_ref, f32[256,1536]{1,0:T(8,128)S(1)} %multiply_down.1.acc_ref), custom_call_target="tpu_custom_call" | custom-call | flops 1811939328 | bytes 6000000 | tf_op jit(solution)/shard_map/multiply_last/pallas_call | solution.py:121
  37.8 1.9 %collective-permute-done.10.rows_in = f32[4,6,2,16,256]{4,3,2,1,0:T(8,128)S(1)} collective-permute-done((f32[4,6,2,16,256]{4,3,2,1,0:T(8,128)S(1)}, f32[4,6,2,16,256]{4,3,2,1,0:T(8,128)S(1)}, u32[]{:S(2)}, u32[]{:S(2)}) %collective-permute-start.10) | collective-permute-done | bytes 786464 | tf_op jit(solution)/shard_map/ppermute | solution.py:39
  39.8 3.9 %collective-permute-start.11 = (f32[2,6,2,16,256]{4,3,2,1,0:T(8,128)S(1)}, f32[2,6,2,16,256]{4,3,2,1,0:T(8,128)S(1)}, u32[]{:S(2)}, u32[]{:S(2)}) collective-permute-start(f32[2,6,2,16,256]{4,3,2,1,0:T(8,128)S(1)} %get-tuple-element.46), channel_id=1, source_target_pairs={{0,32},{1,33},{2,34},{3,35},{4,36},{5,37},{6,38},{7,39},{8,40},{9,... | collective-permute-start | bytes 1179656 | tf_op jit(solution)/shard_map/ppermute | solution.py:39
  43.8 2.8 %collective-permute-start.12 = (f32[6,16,256]{2,1,0:T(8,128)S(1)}, f32[6,16,256]{2,1,0:T(8,128)S(1)}, u32[]{:S(2)}, u32[]{:S(2)}) collective-permute-start(f32[6,16,256]{2,1,0:T(8,128)S(1)} %get-tuple-element.49), channel_id=1, source_target_pairs={{0,8},{1,9},{2,10},{3,11},{4,12},{5,13},{6,14},{7,15},{8,0},{9,1},... | collective-permute-start | bytes 294920 | tf_op jit(solution)/shard_map/ppermute | solution.py:39
  46.5 2.0 %invert_rest.1._.inv_ref = f32[256,256]{1,0:T(8,128)S(1)} custom-call(f32[256,256]{1,0:T(8,128)S(1)} %get-tuple-element.47.strict_ref, f32[256,256]{1,0:T(8,128)S(1)} %get-tuple-element.34._.blocks_ref, f32[256,256]{1,0:T(8,128)S(1)} %get-tuple-element.48.l_ref, f32[2,6,2,16,256]{4,3,2,1,0:T(8,128)S(1)} %get-tuple-element.45._.rows), custom_call_target="tpu_custom_call" | custom-call | flops 1610612736 | bytes 6000000 | tf_op jit(solution)/shard_map/invert_rest/pallas_call | solution.py:121
  50.2 3.7 %collective-permute-done.13.rows_in = f32[6,2,16,256]{3,2,1,0:T(8,128)S(1)} collective-permute-done((f32[6,2,16,256]{3,2,1,0:T(8,128)S(1)}, f32[6,2,16,256]{3,2,1,0:T(8,128)S(1)}, u32[]{:S(2)}, u32[]{:S(2)}) %collective-permute-start.13) | collective-permute-done | bytes 196640 | tf_op jit(solution)/shard_map/ppermute | solution.py:39
  53.9 3.1 %finish_panel.1 = (f32[136,128]{1,0:T(8,128)S(1)}, f32[136,128]{1,0:T(8,128)S(1)}, f32[6,16,256]{2,1,0:T(8,128)S(1)}) custom-call(f32[6,16,256]{2,1,0:T(8,128)S(1)} %get-tuple-element.52.first_ref.keep_ref, f32[6,16,256]{2,1,0:T(8,128)S(1)} %get-tuple-element.53.second_ref, f32[6,16,256]{2,1,0:T(8,128)S(1)} %get-tuple-element.54.l_first_ref, ...), custom_call_target="tpu_custom_call" | custom-call | flops 1207959552 | bytes 4000000 | tf_op jit(solution)/shard_map/finish_panel/pallas_call | solution.py:121
  57.0 2.2 %collective-permute-start.16 = (f32[136,128]{1,0:T(8,128)S(1)}, f32[136,128]{1,0:T(8,128)S(1)}, u32[]{:S(2)}, u32[]{:S(2)}) collective-permute-start(f32[136,128]{1,0:T(8,128)S(1)} %get-tuple-element.61), channel_id=1, source_target_pairs={{0,16},{1,17},{2,18},{3,19},{4,20},{5,21},{6,22},{7,23},{8,24},{9,... | collective-permute-start | bytes 208904 | tf_op jit(solution)/shard_map/ppermute | solution.py:39
  59.2 2.7 %collective-permute-start.14 = (f32[6,16,256]{2,1,0:T(8,128)S(1)}, f32[6,16,256]{2,1,0:T(8,128)S(1)}, u32[]{:S(2)}, u32[]{:S(2)}) collective-permute-start(f32[6,16,256]{2,1,0:T(8,128)S(1)} %get-tuple-element.59), channel_id=1, source_target_pairs={{0,8},{1,9},{2,10},{3,11},{4,12},{5,13},{6,14},{7,15},{8,0},{9,1},... | collective-permute-start | bytes 294920 | tf_op jit(solution)/shard_map/ppermute | solution.py:39
  65.3 3.9 %collective-permute-start.15 = (f32[12,16,256]{2,1,0:T(8,128)S(1)}, f32[12,16,256]{2,1,0:T(8,128)S(1)}, u32[]{:S(2)}, u32[]{:S(2)}) collective-permute-start(f32[12,16,256]{2,1,0:T(8,128)S(1)} %join_rows.1._), channel_id=1, source_target_pairs={{0,0},{1,17},{2,34},{3,51},{4,68},{5,85},{6,102},{7,119},{8,8},{9,... | collective-permute-start | bytes 589832 | tf_op jit(solution)/shard_map/ppermute | solution.py:39
  70.8 1.8 %collective-permute-start.22 = (f32[136,128]{1,0:T(8,128)S(1)}, f32[136,128]{1,0:T(8,128)S(1)}, u32[]{:S(2)}, u32[]{:S(2)}) collective-permute-start(f32[136,128]{1,0:T(8,128)S(1)} %add_four.3.part), channel_id=1, source_target_pairs={{0,12},{1,13},{2,14},{3,15},{4,8},{5,9},{6,10},{7,11},{8,4},{9,5},... | collective-permute-start | bytes 208904 | tf_op jit(solution)/shard_map/ppermute | solution.py:39
  72.6 7.5 %collective-permute-done.20.beyond = f32[136,128]{1,0:T(8,128)S(1)} collective-permute-done((f32[136,128]{1,0:T(8,128)S(1)}, f32[136,128]{1,0:T(8,128)S(1)}, u32[]{:S(2)}, u32[]{:S(2)}) %collective-permute-start.20) | collective-permute-done | bytes 69664 | tf_op jit(solution)/shard_map/ppermute | solution.py:39
  81.5 2.7 %collective-permute-start.25 = (f32[136,128]{1,0:T(8,128)S(1)}, f32[136,128]{1,0:T(8,128)S(1)}, u32[]{:S(2)}, u32[]{:S(2)}) collective-permute-start(f32[136,128]{1,0:T(8,128)S(1)} %add_four.4.part), channel_id=1, source_target_pairs={{0,96},{1,97},{2,98},{3,99},{4,100},{5,101},{6,102},{7,103},{8,104... | collective-permute-start | bytes 208904 | tf_op jit(solution)/shard_map/ppermute | solution.py:39
  86.5 2.2 %collective-permute-start.26 = (f32[136,128]{1,0:T(8,128)S(1)}, f32[136,128]{1,0:T(8,128)S(1)}, u32[]{:S(2)}, u32[]{:S(2)}) collective-permute-start(f32[136,128]{1,0:T(8,128)S(1)} %add_four.5.part), channel_id=1, source_target_pairs={{0,16},{1,17},{2,18},{3,19},{4,20},{5,21},{6,22},{7,23},{8,24},{9,... | collective-permute-start | bytes 208904 | tf_op jit(solution)/shard_map/ppermute | solution.py:39
  (52 shorter events, 19.7 us)
Async XLA Ops:
  0.6 10.1 %collective-permute-start = (f32[12,16,256]{2,1,0:T(8,128)}, f32[12,16,256]{2,1,0:T(8,128)S(1)}, u32[]{:S(2)}, u32[]{:S(2)}) collective-permute-start(f32[12,16,256]{2,1,0:T(8,128)} %bitcast.14), channel_id=1, source_target_pairs={{0,1},{1,2},{2,3},{3,0},{4,5},{5,6},{6,7},{7,4},{8,9},{9,10},{10,1... | collective-permute-start | bytes 589832 | tf_op jit(solution)/shard_map/ppermute | solution.py:39
  3.2 7.6 %collective-permute-start.1 = (f32[12,16,256]{2,1,0:T(8,128)}, f32[12,16,256]{2,1,0:T(8,128)S(1)}, u32[]{:S(2)}, u32[]{:S(2)}) collective-permute-start(f32[12,16,256]{2,1,0:T(8,128)} %bitcast.15), channel_id=1, source_target_pairs={{0,3},{1,0},{2,1},{3,2},{4,7},{5,4},{6,5},{7,6},{8,11},{9,8},{10,9... | collective-permute-start | bytes 589832 | tf_op jit(solution)/shard_map/ppermute | solution.py:39
  5.4 6.8 %collective-permute-start.2 = (f32[12,16,256]{2,1,0:T(8,128)}, f32[12,16,256]{2,1,0:T(8,128)S(1)}, u32[]{:S(2)}, u32[]{:S(2)}) collective-permute-start(f32[12,16,256]{2,1,0:T(8,128)} %bitcast.16), channel_id=1, source_target_pairs={{0,2},{1,3},{2,0},{3,1},{4,6},{5,7},{6,4},{7,5},{8,10},{9,11},{10,... | collective-permute-start | bytes 589832 | tf_op jit(solution)/shard_map/ppermute | solution.py:39
  12.3 8.2 %collective-permute-start.3 = (f32[384,256]{1,0:T(8,128)S(1)}, f32[384,256]{1,0:T(8,128)S(1)}, u32[]{:S(2)}, u32[]{:S(2)}) collective-permute-start(f32[384,256]{1,0:T(8,128)S(1)} %get-tuple-element.35.la_ref), channel_id=1, source_target_pairs={{0,4},{1,5},{2,6},{3,7},{4,8},{5,9},{6,10},{7,11},{8,12},{9,13},{1... | collective-permute-start | bytes 1179656 | tf_op jit(solution)/shard_map/ppermute | solution.py:39
  13.4 10.0 %collective-permute-start.5 = (f32[384,256]{1,0:T(8,128)S(1)}, f32[384,256]{1,0:T(8,128)S(1)}, u32[]{:S(2)}, u32[]{:S(2)}) collective-permute-start(f32[384,256]{1,0:T(8,128)S(1)} %get-tuple-element.36.lb_ref), channel_id=1, source_target_pairs={{0,12},{1,13},{2,14},{3,15},{4,0},{5,1},{6,2},{7,3},{8,4},{9,5},{1... | collective-permute-start | bytes 1179656 | tf_op jit(solution)/shard_map/ppermute | solution.py:39
  15.0 14.0 %collective-permute-start.7 = (f32[384,256]{1,0:T(8,128)S(1)}, f32[384,256]{1,0:T(8,128)S(1)}, u32[]{:S(2)}, u32[]{:S(2)}) collective-permute-start(f32[384,256]{1,0:T(8,128)S(1)} %get-tuple-element.36.lb_ref), channel_id=1, source_target_pairs={{0,4},{1,5},{2,6},{3,7},{4,8},{5,9},{6,10},{7,11},{8,12},{9,13},{1... | collective-permute-start | bytes 1179656 | tf_op jit(solution)/shard_map/ppermute | solution.py:39
  15.0 16.4 %collective-permute-start.8 = (f32[384,256]{1,0:T(8,128)S(1)}, f32[384,256]{1,0:T(8,128)S(1)}, u32[]{:S(2)}, u32[]{:S(2)}) collective-permute-start(f32[384,256]{1,0:T(8,128)S(1)} %get-tuple-element.35.la_ref), channel_id=1, source_target_pairs={{0,12},{1,13},{2,14},{3,15},{4,0},{5,1},{6,2},{7,3},{8,4},{9,5},{1... | collective-permute-start | bytes 1179656 | tf_op jit(solution)/shard_map/ppermute | solution.py:39
  17.7 13.7 %collective-permute-start.9 = (f32[12,16,256]{2,1,0:T(8,128)S(1)}, f32[12,16,256]{2,1,0:T(8,128)S(1)}, u32[]{:S(2)}, u32[]{:S(2)}) collective-permute-start(f32[12,16,256]{2,1,0:T(8,128)S(1)} %bitcast.18), channel_id=1, source_target_pairs={{0,0},{1,16},{2,32},{3,48},{4,64},{5,80},{6,96},{7,112},{8,8},{9,2... | collective-permute-start | bytes 589832 | tf_op jit(solution)/shard_map/ppermute | solution.py:39
  20.5 13.1 %collective-permute-start.4 = (f32[384,256]{1,0:T(8,128)S(1)}, f32[384,256]{1,0:T(8,128)S(1)}, u32[]{:S(2)}, u32[]{:S(2)}) collective-permute-start(f32[384,256]{1,0:T(8,128)S(1)} %collective-permute-done.3.la_ref), channel_id=1, source_target_pairs={{0,4},{1,5},{2,6},{3,7},{4,8},{5,9},{6,10},{7,11},{8,12},{9,13},{1... | collective-permute-start | bytes 1179656 | tf_op jit(solution)/shard_map/ppermute | solution.py:39
  23.4 10.2 %collective-permute-start.6 = (f32[384,256]{1,0:T(8,128)S(1)}, f32[384,256]{1,0:T(8,128)S(1)}, u32[]{:S(2)}, u32[]{:S(2)}) collective-permute-start(f32[384,256]{1,0:T(8,128)S(1)} %collective-permute-done.5.lb_ref), channel_id=1, source_target_pairs={{0,12},{1,13},{2,14},{3,15},{4,0},{5,1},{6,2},{7,3},{8,4},{9,5},{1... | collective-permute-start | bytes 1179656 | tf_op jit(solution)/shard_map/ppermute | solution.py:39
  39.8 9.1 %collective-permute-start.11 = (f32[2,6,2,16,256]{4,3,2,1,0:T(8,128)S(1)}, f32[2,6,2,16,256]{4,3,2,1,0:T(8,128)S(1)}, u32[]{:S(2)}, u32[]{:S(2)}) collective-permute-start(f32[2,6,2,16,256]{4,3,2,1,0:T(8,128)S(1)} %get-tuple-element.46), channel_id=1, source_target_pairs={{0,32},{1,33},{2,34},{3,35},{4,36},{5,37},{6,38},{7,39},{8,40},{9,... | collective-permute-start | bytes 1179656 | tf_op jit(solution)/shard_map/ppermute | solution.py:39
  43.8 5.1 %collective-permute-start.12 = (f32[6,16,256]{2,1,0:T(8,128)S(1)}, f32[6,16,256]{2,1,0:T(8,128)S(1)}, u32[]{:S(2)}, u32[]{:S(2)}) collective-permute-start(f32[6,16,256]{2,1,0:T(8,128)S(1)} %get-tuple-element.49), channel_id=1, source_target_pairs={{0,8},{1,9},{2,10},{3,11},{4,12},{5,13},{6,14},{7,15},{8,0},{9,1},... | collective-permute-start | bytes 294920 | tf_op jit(solution)/shard_map/ppermute | solution.py:39
  49.0 4.9 %collective-permute-start.13 = (f32[6,2,16,256]{3,2,1,0:T(8,128)S(1)}, f32[6,2,16,256]{3,2,1,0:T(8,128)S(1)}, u32[]{:S(2)}, u32[]{:S(2)}) collective-permute-start(f32[6,2,16,256]{3,2,1,0:T(8,128)S(1)} %get-tuple-element.51), channel_id=1, source_target_pairs={{0,96},{1,97},{2,98},{3,99},{4,100},{5,101},{6,102},{7,103},{8,104... | collective-permute-start | bytes 589832 | tf_op jit(solution)/shard_map/ppermute | solution.py:39
  57.0 4.9 %collective-permute-start.16 = (f32[136,128]{1,0:T(8,128)S(1)}, f32[136,128]{1,0:T(8,128)S(1)}, u32[]{:S(2)}, u32[]{:S(2)}) collective-permute-start(f32[136,128]{1,0:T(8,128)S(1)} %get-tuple-element.61), channel_id=1, source_target_pairs={{0,16},{1,17},{2,18},{3,19},{4,20},{5,21},{6,22},{7,23},{8,24},{9,... | collective-permute-start | bytes 208904 | tf_op jit(solution)/shard_map/ppermute | solution.py:39
  59.2 6.1 %collective-permute-start.14 = (f32[6,16,256]{2,1,0:T(8,128)S(1)}, f32[6,16,256]{2,1,0:T(8,128)S(1)}, u32[]{:S(2)}, u32[]{:S(2)}) collective-permute-start(f32[6,16,256]{2,1,0:T(8,128)S(1)} %get-tuple-element.59), channel_id=1, source_target_pairs={{0,8},{1,9},{2,10},{3,11},{4,12},{5,13},{6,14},{7,15},{8,0},{9,1},... | collective-permute-start | bytes 294920 | tf_op jit(solution)/shard_map/ppermute | solution.py:39
  61.9 7.3 %collective-permute-start.17 = (f32[136,128]{1,0:T(8,128)S(1)}, f32[136,128]{1,0:T(8,128)S(1)}, u32[]{:S(2)}, u32[]{:S(2)}) collective-permute-start(f32[136,128]{1,0:T(8,128)S(1)} %add_two.1.part), channel_id=1, source_target_pairs={{0,2},{1,3},{2,0},{3,1},{4,6},{5,7},{6,4},{7,5},{8,10},{9,11},{10,... | collective-permute-start | bytes 208904 | tf_op jit(solution)/shard_map/ppermute | solution.py:39
  62.9 6.4 %collective-permute-start.18 = (f32[136,128]{1,0:T(8,128)S(1)}, f32[136,128]{1,0:T(8,128)S(1)}, u32[]{:S(2)}, u32[]{:S(2)}) collective-permute-start(f32[136,128]{1,0:T(8,128)S(1)} %add_two.1.part), channel_id=1, source_target_pairs={{0,1},{1,0},{2,3},{3,2},{4,5},{5,4},{6,7},{7,6},{8,9},{9,8},{10,11... | collective-permute-start | bytes 208904 | tf_op jit(solution)/shard_map/ppermute | solution.py:39
  63.5 5.7 %collective-permute-start.19 = (f32[136,128]{1,0:T(8,128)S(1)}, f32[136,128]{1,0:T(8,128)S(1)}, u32[]{:S(2)}, u32[]{:S(2)}) collective-permute-start(f32[136,128]{1,0:T(8,128)S(1)} %add_two.1.part), channel_id=1, source_target_pairs={{0,3},{1,2},{2,1},{3,0},{4,7},{5,6},{6,5},{7,4},{8,11},{9,10},{10,... | collective-permute-start | bytes 208904 | tf_op jit(solution)/shard_map/ppermute | solution.py:39
  65.3 23.5 %collective-permute-start.15 = (f32[12,16,256]{2,1,0:T(8,128)S(1)}, f32[12,16,256]{2,1,0:T(8,128)S(1)}, u32[]{:S(2)}, u32[]{:S(2)}) collective-permute-start(f32[12,16,256]{2,1,0:T(8,128)S(1)} %join_rows.1._), channel_id=1, source_target_pairs={{0,0},{1,17},{2,34},{3,51},{4,68},{5,85},{6,102},{7,119},{8,8},{9,... | collective-permute-start | bytes 589832 | tf_op jit(solution)/shard_map/ppermute | solution.py:39
  69.3 10.8 %collective-permute-start.20 = (f32[136,128]{1,0:T(8,128)S(1)}, f32[136,128]{1,0:T(8,128)S(1)}, u32[]{:S(2)}, u32[]{:S(2)}) collective-permute-start(f32[136,128]{1,0:T(8,128)S(1)} %add_four.3.part), channel_id=1, source_target_pairs={{0,8},{1,9},{2,10},{3,11},{4,12},{5,13},{6,14},{7,15},{8,0},{9,1},... | collective-permute-start | bytes 208904 | tf_op jit(solution)/shard_map/ppermute | solution.py:39
  70.8 10.1 %collective-permute-start.21 = (f32[136,128]{1,0:T(8,128)S(1)}, f32[136,128]{1,0:T(8,128)S(1)}, u32[]{:S(2)}, u32[]{:S(2)}) collective-permute-start(f32[136,128]{1,0:T(8,128)S(1)} %add_four.3.part), channel_id=1, source_target_pairs={{0,4},{1,5},{2,6},{3,7},{4,0},{5,1},{6,2},{7,3},{8,12},{9,13},{10,... | collective-permute-start | bytes 208904 | tf_op jit(solution)/shard_map/ppermute | solution.py:39
  70.8 10.1 %collective-permute-start.22 = (f32[136,128]{1,0:T(8,128)S(1)}, f32[136,128]{1,0:T(8,128)S(1)}, u32[]{:S(2)}, u32[]{:S(2)}) collective-permute-start(f32[136,128]{1,0:T(8,128)S(1)} %add_four.3.part), channel_id=1, source_target_pairs={{0,12},{1,13},{2,14},{3,15},{4,8},{5,9},{6,10},{7,11},{8,4},{9,5},... | collective-permute-start | bytes 208904 | tf_op jit(solution)/shard_map/ppermute | solution.py:39
  80.9 4.9 %collective-permute-start.23 = (f32[136,128]{1,0:T(8,128)S(1)}, f32[136,128]{1,0:T(8,128)S(1)}, u32[]{:S(2)}, u32[]{:S(2)}) collective-permute-start(f32[136,128]{1,0:T(8,128)S(1)} %add_four.4.part), channel_id=1, source_target_pairs={{0,64},{1,65},{2,66},{3,67},{4,68},{5,69},{6,70},{7,71},{8,72},{9,... | collective-permute-start | bytes 208904 | tf_op jit(solution)/shard_map/ppermute | solution.py:39
  81.5 5.0 %collective-permute-start.25 = (f32[136,128]{1,0:T(8,128)S(1)}, f32[136,128]{1,0:T(8,128)S(1)}, u32[]{:S(2)}, u32[]{:S(2)}) collective-permute-start(f32[136,128]{1,0:T(8,128)S(1)} %add_four.4.part), channel_id=1, source_target_pairs={{0,96},{1,97},{2,98},{3,99},{4,100},{5,101},{6,102},{7,103},{8,104... | collective-permute-start | bytes 208904 | tf_op jit(solution)/shard_map/ppermute | solution.py:39
  (4 other events, 22.2 us)
